TPU v7x, 32 devices: a whole 2x2x4 slice. The times are simulated.
32 devices in a mesh: dp: 8 (over y, x, core), tensor: 4 (over z).
Axes of the slice: x: 2, y: 2, z: 4, core: 2. Of those that a mesh axis runs over, the one named last changes fastest.
Arguments:
- hidden: bfloat16 [16384, 1024], P(('dp', 'tensor')), may hold values from -6 to 6
- segments: int32 [8, 2048], P('dp'), may hold values from 0 to 15, never falling along the last dimension, each value on 1 to 1024 neighbouring positions
- cotangent: bfloat16 [16384, 1024], P(('dp', 'tensor')), may hold values from -6 to 6
- norm_gain: float32 [1024], replicated, may hold values from 0.5 to 1.5
- ffn_gain: float32 [1024], replicated, may hold values from 0.5 to 1.5
- query_proj: bfloat16 [1024, 512], P('dp', 'tensor'), may hold values from -0.1875 to 0.1875
- key_proj: bfloat16 [1024, 128], P('dp'), may hold values from -0.1875 to 0.1875
- value_proj: bfloat16 [1024, 128], P('dp'), may hold values from -0.1875 to 0.1875
- attn_out_proj: bfloat16 [512, 1024], P('tensor', 'dp'), may hold values from -1 to 1
- gate_inner: bfloat16 [1024, 1536], P('dp', 'tensor'), may hold values from -0.1875 to 0.1875
- input_inner: bfloat16 [1024, 1536], P('dp', 'tensor'), may hold values from -0.1875 to 0.1875
- state_proj: bfloat16 [1024, 256], P('dp'), may hold values from -0.1875 to 0.1875
- step_proj: bfloat16 [1024, 24], P('dp', 'tensor'), may hold values from -0.1875 to 0.1875
- mamba_out: bfloat16 [1536, 1024], P('tensor', 'dp'), may hold values from -0.15625 to 0.15625
- conv_weight: float32 [4, 1792], replicated, may hold values from -4 to 4
- conv_bias: float32 [1792], replicated, may hold values from -4 to 4
- decay_log: float32 [24], replicated, may hold values from -4 to 2.5
- skip_gain: float32 [24], replicated, may hold values from 0.5 to 1.5
- step_bias: float32 [24], replicated, may hold values from -5 to -1
- ffn_gate: bfloat16 [1024, 2048], P('dp', 'tensor'), may hold values from -0.1875 to 0.1875
- ffn_up: bfloat16 [1024, 2048], P('dp', 'tensor'), may hold values from -0.1875 to 0.1875
- ffn_down: bfloat16 [2048, 1024], P('tensor', 'dp'), may hold values from -0.125 to 0.125
Outputs:
- output: bfloat16 [16384, 1024], P(('dp', 'tensor'))
- hidden_grad: float32 [16384, 1024], P(('dp', 'tensor'))
- norm_gain_grad: float32 [1024], replicated
- ffn_gain_grad: float32 [1024], replicated
- query_proj_grad: float32 [1024, 512], P('dp', 'tensor')
- key_proj_grad: float32 [1024, 128], P(('dp', 'tensor'))
- value_proj_grad: float32 [1024, 128], P(('dp', 'tensor'))
- attn_out_proj_grad: float32 [512, 1024], P('tensor', 'dp')
- gate_inner_grad: float32 [1024, 1536], P('dp', 'tensor')
- input_inner_grad: float32 [1024, 1536], P('dp', 'tensor')
- state_proj_grad: float32 [1024, 256], P(('dp', 'tensor'))
- step_proj_grad: float32 [1024, 24], P('dp', 'tensor')
- mamba_out_grad: float32 [1536, 1024], P('tensor', 'dp')
- conv_weight_grad: float32 [4, 1792], replicated
- conv_bias_grad: float32 [1792], replicated
- decay_log_grad: float32 [24], replicated
- skip_gain_grad: float32 [24], replicated
- step_bias_grad: float32 [24], replicated
- ffn_gate_grad: float32 [1024, 2048], P('dp', 'tensor')
- ffn_up_grad: float32 [1024, 2048], P('dp', 'tensor')
- ffn_down_grad: float32 [2048, 1024], P('tensor', 'dp')
Inputs may be any that keep to these rules, and one draw needn't show every extreme that they name: `segments`: in each row the numbers never fall; a document holds 1 to half of 2048 positions, and one holds exactly that many.
All inputs are finite; a program needn't handle non-finite values.
Results may differ from a plain program's by a relative error of at most 0.012.
Values may be sent and summed in bfloat16 or wider, within the bound.
No kernel may reach another device: no remote copies, remote signals or barrier semaphores. Data moves between devices by JAX's collectives and lax.ppermute only.
A program may use at most 256 MiB of HBM per device.

v0:
```python
import jax
import jax.numpy as jnp
from jax import lax
from jax.sharding import PartitionSpec as P

QH = 8
KVH = 2
HD = 64
MH = 24
MP = 64
NS = 128
SPAN = 128
BLOCK = 512


epsilon = 1e-05
rope_base = 100000000000.0


def as_sent(value):
    return jax.tree.map(lambda a: a.astype(jnp.bfloat16) if a.dtype == jnp.float32 else a, value)


def to_bfloat(values):
    return lax.optimization_barrier(values.astype(jnp.bfloat16)).astype(jnp.float32)


def rounders():

    def value_round(values):
        return to_bfloat(values)

    def value_keep(values):
        return (to_bfloat(values), None)

    def value_pass(kept, grad):
        return (grad,)

    def grad_plain(values):
        return values

    def grad_keep(values):
        return (values, None)

    def grad_round(kept, grad):
        return (to_bfloat(grad),)

    rounding = jax.custom_vjp(value_round)
    rounding.defvjp(value_keep, value_pass)
    back_rounding = jax.custom_vjp(grad_plain)
    back_rounding.defvjp(grad_keep, grad_round)
    return (rounding, back_rounding)


def low(values):
    return rounders()[0](values)


def low_back(values):
    return rounders()[1](values)


def matmul(left, right):
    return jnp.dot(left, right)


def rms_scale(values, gain_vec):
    return (
        values * lax.rsqrt(jnp.mean(values * values, axis=-1, keepdims=True) + epsilon) * gain_vec
    )


def norm_rounded(values, gain_vec):
    return low(rms_scale(values, gain_vec))


def rotary(values):
    length, head_count, head_size = values.shape
    half_size = head_size // 2
    frequency = rope_base ** (-2.0 * jnp.arange(half_size, dtype=jnp.float32) / head_size)
    angles = jnp.arange(length, dtype=jnp.float32)[:, None] * frequency[None, :]
    cosine = jnp.cos(angles)[:, None, :]
    sine_part = jnp.sin(angles)[:, None, :]
    first_half = values[..., :half_size]
    second_half = values[..., half_size:]
    return jnp.concatenate(
        [
            first_half * cosine - second_half * sine_part,
            second_half * cosine + first_half * sine_part,
        ],
        axis=-1,
    )


def attend(query, key_heads, values, segment):
    length, head_count, head_size = query.shape
    group_size = head_count // key_heads.shape[1]
    keys_all = jnp.repeat(key_heads, group_size, axis=1)
    values_all = jnp.repeat(values, group_size, axis=1)
    block_rows = min(BLOCK, length)
    block_count = length // block_rows
    begin_rows = (jnp.arange(block_count) * block_rows).astype(jnp.int32)
    columns = jnp.arange(length)

    def one_block(element):
        rows_query, begin_at = element
        row_segment = lax.dynamic_slice_in_dim(segment, begin_at, block_rows)
        row_position = begin_at + jnp.arange(block_rows)
        allowed = (row_segment[:, None] == segment[None, :]) & (
            row_position[:, None] >= columns[None, :]
        )
        scores = jnp.einsum("qhd,khd->hqk", rows_query, keys_all) * head_size ** (-0.5)
        scores = low_back(scores)
        scores = jnp.where(allowed[None], scores, -1e30)
        attn_probs = low(jax.nn.softmax(scores, axis=-1))
        return jnp.einsum("hqk,khd->qhd", attn_probs, values_all)

    result = lax.map(
        jax.checkpoint(one_block),
        (query.reshape(block_count, block_rows, head_count, head_size), begin_rows),
    )
    return result.reshape(length, head_count, head_size)


def causal_conv(raw_input, kernel, conv_shift, segment):
    length = raw_input.shape[0]
    kernel_taps = kernel.shape[0]
    summed = conv_shift[None, :] + kernel[kernel_taps - 1][None, :] * raw_input
    for offset in range(1, kernel_taps):
        shifted = jnp.pad(raw_input, ((offset, 0), (0, 0)))[:length]
        seg_shift = jnp.pad(segment, (offset, 0), constant_values=-1)[:length]
        keep_mask = (seg_shift == segment).astype(jnp.float32)[:, None]
        summed = summed + kernel[kernel_taps - 1 - offset][None, :] * shifted * keep_mask
    return summed


def state_scan(x_heads, input_mat, output_mat, dt_step, log_decay, segment):
    length, head_count, head_size = x_heads.shape
    state_size = input_mat.shape[1]
    block_rows = min(SPAN, length)
    block_count = length // block_rows
    previous = jnp.concatenate([jnp.full((1,), -1, jnp.int32), segment[:-1]])
    elements = (
        x_heads.reshape(block_count, block_rows, head_count, head_size),
        input_mat.reshape(block_count, block_rows, state_size),
        output_mat.reshape(block_count, block_rows, state_size),
        dt_step.reshape(block_count, block_rows, head_count),
        log_decay.reshape(block_count, block_rows, head_count),
        segment.reshape(block_count, block_rows),
        previous.reshape(block_count, block_rows)[:, 0],
    )
    positions = jnp.arange(block_rows)
    causal = positions[:, None] >= positions[None, :]

    def advance(carried, element):
        x_block, b_block, c_block, dt_block, decay_block, seg_block, before = element
        cumulative = jnp.cumsum(decay_block, axis=0)
        allowed = causal & (seg_block[:, None] == seg_block[None, :])
        log_gap = cumulative[:, None, :] - cumulative[None, :, :]
        decays = jnp.exp(jnp.where(allowed[:, :, None], log_gap, 0.0)) * allowed[:, :, None]
        affinity = jnp.dot(c_block, b_block.T, precision=lax.Precision.HIGHEST)
        mixing = affinity[:, :, None] * decays * dt_block[None, :, :]
        within = jnp.einsum("tsh,shp->thp", mixing, x_block, precision=lax.Precision.HIGHEST)
        carry_in = (seg_block == before).astype(jnp.float32)
        reached = jnp.einsum("tn,hnp->thp", c_block, carried, precision=lax.Precision.HIGHEST)
        carried_part = reached * (carry_in[:, None] * jnp.exp(cumulative))[:, :, None]
        last_seg = (seg_block == seg_block[-1]).astype(jnp.float32)
        final_weight = last_seg[:, None] * jnp.exp(cumulative[-1][None, :] - cumulative) * dt_block
        next_state = carried * (carry_in[-1] * jnp.exp(cumulative[-1]))[:, None, None] + jnp.einsum(
            "sh,sn,shp->hnp", final_weight, b_block, x_block, precision=lax.Precision.HIGHEST
        )
        return (next_state, within + carried_part)

    initial = jnp.zeros((head_count, state_size, head_size), jnp.float32)
    final_state, outputs = lax.scan(jax.checkpoint(advance), initial, elements)
    return outputs.reshape(length, head_count, head_size)


def mixer_core(
    normed,
    query_proj,
    key_proj,
    value_proj,
    attn_out_proj,
    gate_inner,
    input_inner,
    state_proj,
    step_proj,
    mamba_out,
    conv_weight,
    conv_bias,
    decay_log,
    skip_gain,
    step_bias,
    segment,
):
    length = normed.shape[0]
    query = low_back(low(rotary(matmul(normed, query_proj).reshape(length, -1, HD))))
    key_heads = low(rotary(matmul(normed, key_proj).reshape(length, -1, HD)))
    values = low(matmul(normed, value_proj).reshape(length, -1, HD))
    attended = attend(query, key_heads, values, segment)
    attended = low_back(low(attended.reshape(length, -1)))
    head_count = decay_log.shape[0]
    inner_width = head_count * MP
    z_gate = low_back(matmul(normed, gate_inner))
    x_raw = low_back(matmul(normed, input_inner))
    bc_raw = matmul(normed, state_proj)
    dt_raw = low_back(matmul(normed, step_proj))
    mixed = jax.nn.silu(
        causal_conv(jnp.concatenate([x_raw, bc_raw], axis=1), conv_weight, conv_bias, segment)
    )
    x_heads = low(mixed[:, :inner_width]).reshape(length, head_count, MP)
    input_mat = low(mixed[:, inner_width : inner_width + NS])
    output_mat = low(mixed[:, inner_width + NS :])
    dt_step = jax.nn.softplus(dt_raw + step_bias[None, :])
    log_decay = dt_step * (-jnp.exp(decay_log))[None, :]
    scanned = state_scan(x_heads, input_mat, output_mat, dt_step, log_decay, segment)
    full_y = scanned + skip_gain[None, :, None] * x_heads
    gated = low_back(low(full_y.reshape(length, inner_width) * jax.nn.silu(z_gate)))
    return matmul(attended, attn_out_proj) + matmul(gated, mamba_out)


def ffn_core(normed2, ffn_gate, ffn_up, ffn_down):
    gate_lin = low_back(matmul(normed2, ffn_gate))
    up_lin = low_back(matmul(normed2, ffn_up))
    activation = low_back(low(jax.nn.silu(gate_lin) * up_lin))
    return matmul(activation, ffn_down)


def as_float(elements):
    return tuple((element.astype(jnp.float32) for element in elements))


def per_device(
    hidden,
    segments,
    cotangent,
    norm_gain,
    ffn_gain,
    query_proj,
    key_proj,
    value_proj,
    attn_out_proj,
    gate_inner,
    input_inner,
    state_proj,
    step_proj,
    mamba_out,
    conv_weight,
    conv_bias,
    decay_log,
    skip_gain,
    step_bias,
    ffn_gate,
    ffn_up,
    ffn_down,
):
    tensor_index = lax.axis_index("tensor")
    segment = segments[0]

    def mixer_local(
        normed_in,
        query_w,
        key_w,
        value_w,
        attn_out_w,
        gate_w,
        input_w,
        state_w,
        step_w,
        mamba_w,
        conv_w,
        conv_shift,
        decay_all,
        skip_all,
        bias_all,
    ):
        query_heads = query_w.shape[1] // HD
        shared_head = tensor_index * query_heads // (QH // KVH)
        key_local = lax.dynamic_slice_in_dim(key_w, shared_head * HD, HD, 1)
        value_local = lax.dynamic_slice_in_dim(value_w, shared_head * HD, HD, 1)
        head_count = step_w.shape[1]
        inner_width = head_count * MP
        channel_start = tensor_index * inner_width
        conv_local = jnp.concatenate(
            [lax.dynamic_slice_in_dim(conv_w, channel_start, inner_width, 1), conv_w[:, MH * MP :]],
            axis=1,
        )
        shift_local = jnp.concatenate(
            [
                lax.dynamic_slice_in_dim(conv_shift, channel_start, inner_width, 0),
                conv_shift[MH * MP :],
            ]
        )
        decay_local = lax.dynamic_slice_in_dim(decay_all, tensor_index * head_count, head_count, 0)
        skip_local = lax.dynamic_slice_in_dim(skip_all, tensor_index * head_count, head_count, 0)
        bias_local = lax.dynamic_slice_in_dim(bias_all, tensor_index * head_count, head_count, 0)
        return mixer_core(
            normed_in,
            query_w,
            key_local,
            value_local,
            attn_out_w,
            gate_w,
            input_w,
            state_w,
            step_w,
            mamba_w,
            conv_local,
            shift_local,
            decay_local,
            skip_local,
            bias_local,
            segment,
        )

    small_params = (conv_weight, conv_bias, decay_log, skip_gain, step_bias)
    hidden_f = hidden.astype(jnp.float32)
    normed, norm_pullback = jax.vjp(norm_rounded, hidden_f, norm_gain)
    normed_rows = lax.all_gather(normed.astype(jnp.bfloat16), "tensor", axis=0, tiled=True)
    normed_all = normed_rows.astype(jnp.float32)
    mixer_w = (
        lax.all_gather(query_proj, "dp", axis=0, tiled=True),
        lax.all_gather(key_proj, "dp", axis=0, tiled=True),
        lax.all_gather(value_proj, "dp", axis=0, tiled=True),
        lax.all_gather(attn_out_proj, "dp", axis=1, tiled=True),
        lax.all_gather(gate_inner, "dp", axis=0, tiled=True),
        lax.all_gather(input_inner, "dp", axis=0, tiled=True),
        lax.all_gather(state_proj, "dp", axis=0, tiled=True),
        lax.all_gather(step_proj, "dp", axis=0, tiled=True),
        lax.all_gather(mamba_out, "dp", axis=1, tiled=True),
    )
    mixer_part = mixer_local(normed_all, *as_float(mixer_w), *small_params)
    mixer = lax.psum_scatter(mixer_part, "tensor", scatter_dimension=0, tiled=True)
    residual = hidden_f + mixer
    normed2, norm2_pullback = jax.vjp(norm_rounded, residual, ffn_gain)
    ffn_w = (
        lax.all_gather(ffn_gate, "dp", axis=0, tiled=True),
        lax.all_gather(ffn_up, "dp", axis=0, tiled=True),
        lax.all_gather(ffn_down, "dp", axis=1, tiled=True),
    )
    ffn_whole = (
        lax.all_gather(ffn_w[0], "tensor", axis=1, tiled=True),
        lax.all_gather(ffn_w[1], "tensor", axis=1, tiled=True),
        lax.all_gather(ffn_w[2], "tensor", axis=0, tiled=True),
    )
    ffn_result, ffn_pullback = jax.vjp(ffn_core, normed2, *as_float(ffn_whole))
    output = (residual + ffn_result).astype(jnp.bfloat16)
    local_grads = ffn_pullback(cotangent.astype(jnp.float32))
    normed2_grad = local_grads[0]
    ffn_weight_grads = (
        lax.psum_scatter(
            local_grads[1].astype(jnp.bfloat16), "tensor", scatter_dimension=1, tiled=True
        ).astype(jnp.float32),
        lax.psum_scatter(
            local_grads[2].astype(jnp.bfloat16), "tensor", scatter_dimension=1, tiled=True
        ).astype(jnp.float32),
        lax.psum_scatter(
            local_grads[3].astype(jnp.bfloat16), "tensor", scatter_dimension=0, tiled=True
        ).astype(jnp.float32),
    )
    residual_norm_grad, ffn_gain_grad = norm2_pullback(normed2_grad)
    residual_grad = cotangent.astype(jnp.float32) + residual_norm_grad
    mixer_cot = lax.all_gather(
        residual_grad.astype(jnp.bfloat16), "tensor", axis=0, tiled=True
    ).astype(jnp.float32)
    mixer_again = (
        lax.all_gather(query_proj, "dp", axis=0, tiled=True),
        lax.all_gather(key_proj, "dp", axis=0, tiled=True),
        lax.all_gather(value_proj, "dp", axis=0, tiled=True),
        lax.all_gather(attn_out_proj, "dp", axis=1, tiled=True),
        lax.all_gather(gate_inner, "dp", axis=0, tiled=True),
        lax.all_gather(input_inner, "dp", axis=0, tiled=True),
        lax.all_gather(state_proj, "dp", axis=0, tiled=True),
        lax.all_gather(step_proj, "dp", axis=0, tiled=True),
        lax.all_gather(mamba_out, "dp", axis=1, tiled=True),
    )
    spare_mixer, mixer_pullback_again = jax.vjp(
        mixer_local, normed_all, *as_float(mixer_again), *small_params
    )
    mixer_grads = mixer_pullback_again(mixer_cot)
    normed_grad = jax.tree.map(
        lambda part: part.astype(jnp.float32),
        lax.psum_scatter(as_sent(mixer_grads[0]), "tensor", scatter_dimension=0, tiled=True),
    )
    hidden_norm_grad, norm_gain_grad = norm_pullback(normed_grad)
    hidden_grad = residual_grad + hidden_norm_grad
    split_sum = (
        lax.psum_scatter(mixer_grads[1], "dp", scatter_dimension=0, tiled=True),
        lax.psum_scatter(mixer_grads[4], "dp", scatter_dimension=1, tiled=True),
        lax.psum_scatter(mixer_grads[5], "dp", scatter_dimension=0, tiled=True),
        lax.psum_scatter(mixer_grads[6], "dp", scatter_dimension=0, tiled=True),
        lax.psum_scatter(mixer_grads[8], "dp", scatter_dimension=0, tiled=True),
        lax.psum_scatter(mixer_grads[9], "dp", scatter_dimension=1, tiled=True),
        lax.psum_scatter(ffn_weight_grads[0], "dp", scatter_dimension=0, tiled=True),
        lax.psum_scatter(ffn_weight_grads[1], "dp", scatter_dimension=0, tiled=True),
        lax.psum_scatter(ffn_weight_grads[2], "dp", scatter_dimension=1, tiled=True),
    )
    shared_sum = (
        lax.psum_scatter(mixer_grads[2], ("dp", "tensor"), scatter_dimension=0, tiled=True),
        lax.psum_scatter(mixer_grads[3], ("dp", "tensor"), scatter_dimension=0, tiled=True),
        lax.psum_scatter(mixer_grads[7], ("dp", "tensor"), scatter_dimension=0, tiled=True),
    )
    small_sum = lax.psum(
        (
            norm_gain_grad,
            ffn_gain_grad,
            mixer_grads[10],
            mixer_grads[11],
            mixer_grads[12],
            mixer_grads[13],
            mixer_grads[14],
        ),
        ("dp", "tensor"),
    )
    return (
        output,
        hidden_grad,
        small_sum[0],
        small_sum[1],
        split_sum[0],
        shared_sum[0],
        shared_sum[1],
        split_sum[1],
        split_sum[2],
        split_sum[3],
        shared_sum[2],
        split_sum[4],
        split_sum[5],
        small_sum[2],
        small_sum[3],
        small_sum[4],
        small_sum[5],
        small_sum[6],
        split_sum[6],
        split_sum[7],
        split_sum[8],
    )


def solution(mesh):
    in_specs = (
        P(("dp", "tensor"), None),
        P("dp", None),
        P(("dp", "tensor"), None),
        P(),
        P(),
        P("dp", "tensor"),
        P("dp", None),
        P("dp", None),
        P("tensor", "dp"),
        P("dp", "tensor"),
        P("dp", "tensor"),
        P("dp", None),
        P("dp", "tensor"),
        P("tensor", "dp"),
        P(),
        P(),
        P(),
        P(),
        P(),
        P("dp", "tensor"),
        P("dp", "tensor"),
        P("tensor", "dp"),
    )
    out_specs = (
        P(("dp", "tensor"), None),
        P(("dp", "tensor"), None),
        P(),
        P(),
        P("dp", "tensor"),
        P(("dp", "tensor"), None),
        P(("dp", "tensor"), None),
        P("tensor", "dp"),
        P("dp", "tensor"),
        P("dp", "tensor"),
        P(("dp", "tensor"), None),
        P("dp", "tensor"),
        P("tensor", "dp"),
        P(),
        P(),
        P(),
        P(),
        P(),
        P("dp", "tensor"),
        P("dp", "tensor"),
        P("tensor", "dp"),
    )
    return jax.shard_map(
        per_device, mesh=mesh, in_specs=in_specs, out_specs=out_specs, check_vma=False
    )
```

profile of v0, /device:TPU:0, one launch (start us, length us, event | category | flops | bytes accessed | tf_op | source)
XLA Modules:
  0.0 2679.0 jit_solution(15896046576478058346)
XLA Ops:
  14.1 11.9 all_gather.62
  26.0 10.9 all_gather.63
  36.9 9.4 all_gather.61
  48.5 8.9 all_gather.65
  57.5 9.5 all_gather.64
  68.3 9.7 all_gather.67
  78.1 9.5 all_gather.66
  87.6 11.3 all_gather.68
  98.8 11.0 all_gather.69
  111.9 8.6 all-gather.9.cloned.1.call-done
  127.8 6.8 multiply_convert_fusion
  148.8 270.3 %while.97 = (s32[]{:T(128)}, f32[6,128,64]{1,2,0:T(8,128)S(1)}, f32[16,128,6,64]{1,0,3,2:T(8,128)}, s32[16,128]{1,0:T(8,128)S(1)}, s32[16]{0:T(128)S(1)}, /*inde...) while((s32[]{:T(128)}, f32[6,128,64]{1,2,0:T(8,128)S(1)}, ...), condition=%wide.region_7.8_spmd.clone, body=%wide.region_5.7_spmd.clone.sunk | while | flops 252611328 | bytes 2995539 | solution.py:175
  419.1 8.9 fusion.200
  434.3 62.4 %while.96 = (s32[]{:T(128)}, bf16[4,512,2,64]{1,3,2,0:T(8,128)(2,1)S(1)}, s32[4]{0:T(128)S(1)}, s32[2048]{0:T(1024)S(1)}, s32[1,2048]{1,0:T(1,128)S(1)}, /*index...) while((s32[]{:T(128)}, ...), condition=%wide.region_4.5_spmd.clone, body=%wide.region_1.4_spmd.clone.sunk | while | flops 552602112 | bytes 28076204 | solution.py:118
  513.3 135.5 %reduce-scatter.18.cloned.1.call-done = f32[512,1024]{1,0:T(8,128)} async-done(((f32[2048,1024]{1,0:T(8,128)}), f32[512,1024]{1,0:T(8,128)}) %reduce-scatter.18.cloned.1.call-update) | async-done | bytes 2097168 | tf_op jit(solution)/shard_map/reduce_scatter | solution.py:334
  652.6 79.4 %all-gather.17.cloned.1.call-done = bf16[1024,2048]{1,0:T(8,128)(2,1)} async-done(((bf16[1024,512]{1,0:T(8,128)(2,1)}), bf16[1024,2048]{1,0:T(8,128)(2,1)}) %all-gather.17.cloned.1.call-update) | async-done | bytes 4194320 | tf_op jit(solution)/shard_map/all_gather | solution.py:344
  731.9 6.8 fusion.284
  738.7 74.1 %all-gather.13.cloned.1.call-done = bf16[1024,2048]{1,0:T(8,128)(2,1)} async-done(((bf16[1024,512]{1,0:T(8,128)(2,1)}), bf16[1024,2048]{1,0:T(8,128)(2,1)}) %all-gather.13.cloned.1.call-update) | async-done | bytes 4194320 | tf_op jit(solution)/shard_map/all_gather | solution.py:343
  812.8 10.1 fusion.195
  833.3 6.4 convolution_convert_fusion.2
  839.8 6.4 convolution_convert_fusion.1
  848.2 294.8 %while.98 = (s32[]{:T(128)}, f32[6,128,64]{1,2,0:T(8,128)S(1)}, f32[16,128,6,64]{1,0,3,2:T(8,128)}, f32[16,6,128,64]{2,3,1,0:T(8,128)}, s32[16,128]{1,0:T(8,128)...) while((s32[]{:T(128)}, f32[6,128,64]{1,2,0:T(8,128)S(1)}, ...), condition=%wide.region_13.14_spmd.clone, body=%wide.region_11.13_spmd.clone.sunk | while | flops 252611328 | bytes 3192667 | solution.py:175
  1023.6 6.2 dynamic_update_slice.145
  1042.1 6.2 dynamic_update_slice.145
  1143.0 6.2 convolution_convert_fusion
  1164.1 423.1 %while.99 = (s32[]{:T(128)}, f32[6,128,64]{1,2,0:T(8,128)S(1)}, f32[16,128,6,64]{1,0,3,2:T(8,128)}, f32[16,128,128]{2,1,0:T(8,128)}, f32[16,128,128]{2,1,0:T(8,1...) while((s32[]{:T(128)}, f32[6,128,64]{1,2,0:T(8,128)S(1)}, ...), condition=%wide.region_24.25_spmd.clone, body=%wide.region_14.24_spmd.clone.sunk | while | flops 606926848 | bytes 8193151 | solution.py:175
  1600.7 125.6 %while.100 = (s32[]{:T(128)}, f32[2048,2,64]{0,2,1:T(8,128)}, f32[2048,2,64]{0,2,1:T(8,128)S(1)}, bf16[4,512,2,64]{1,3,2,0:T(8,128)(2,1)}, bf16[4,512,2,64]{1,3,...) while((s32[]{:T(128)}, f32[2048,2,64]{0,2,1:T(8,128)}, ...), condition=%wide.region_29.30_spmd.clone, body=%wide.region_25.29_spmd.clone.sunk | while | flops 1384124928 | bytes 131799728 | solution.py:118
  1606.9 7.2 fusion.515
  1638.3 7.2 fusion.515
  1669.6 7.2 fusion.515
  1701.0 7.2 fusion.515
  1726.3 10.3 multiply_convert_fusion.2
  1736.7 14.7 multiply_reduce_fusion.9
  1801.9 19.1 add_convert_fusion
  1880.2 6.2 add_convert_fusion.1
  1887.6 9.1 reduce-scatter.20.cloned.1.call-done
  1898.9 42.0 %all-reduce.24 = (f32[1024]{0:T(1024)}, f32[1024]{0:T(1024)}, f32[4,1792]{1,0:T(4,128)}, f32[1792]{0:T(1024)}, f32[24]{0:T(128)}, /*index=5*/f32[24]{0:T(128)}, f32[24]{0:T(128)}) all-reduce(f32[1024]{0:T(1024)S(1)} %get-tuple-element.1441, f32[1024]{0:T(1024)S(1)} %copy-done.100, ...), channel_id=1, replica_groups=mesh['dp'=8,'tensor'=4] {'dp','tensor'}, use_global_device_ids=true, to_apply=%region_35.36 | all-reduce | flops 11080 | bytes 88640 | tf_op jit(solution)/shard_map/psum | solution.py:404
  1945.6 24.3 reduce-scatter.22.cloned.1.call-done
  1969.9 37.6 %reduce-scatter.28.cloned.1.call-done = f32[128,128]{1,0:T(8,128)} async-done(((f32[128,1024]{1,0:T(8,128)}), f32[128,128]{1,0:T(8,128)}) %reduce-scatter.28.cloned.1.call-update) | async-done | bytes 65552 | tf_op jit(solution)/shard_map/reduce_scatter | solution.py:390
  2007.5 136.9 %reduce-scatter.24.cloned.1.call-done = f32[32,128]{1,0:T(8,128)} async-done(((f32[1024,128]{1,0:T(8,128)}), f32[32,128]{1,0:T(8,128)}) %reduce-scatter.24.cloned.1.call-update) | async-done | bytes 16400 | tf_op jit(solution)/shard_map/reduce_scatter | solution.py:400
  2144.4 133.4 %reduce-scatter.26.cloned.1.call-done = f32[32,128]{1,0:T(8,128)} async-done(((f32[1024,128]{1,0:T(8,128)}), f32[32,128]{1,0:T(8,128)}) %reduce-scatter.26.cloned.1.call-update) | async-done | bytes 16400 | tf_op jit(solution)/shard_map/reduce_scatter | solution.py:401
  2277.8 135.1 %reduce-scatter.34.cloned.1.call-done = f32[32,256]{1,0:T(8,128)} async-done(((f32[1024,256]{1,0:T(8,128)}), f32[32,256]{1,0:T(8,128)}) %reduce-scatter.34.cloned.1.call-update) | async-done | bytes 32784 | tf_op jit(solution)/shard_map/reduce_scatter | solution.py:402
  2412.9 38.8 %reduce-scatter.38.cloned.1.call-done = f32[384,128]{1,0:T(8,128)} async-done(((f32[384,1024]{1,0:T(8,128)}), f32[384,128]{1,0:T(8,128)}) %reduce-scatter.38.cloned.1.call-update) | async-done | bytes 196624 | tf_op jit(solution)/shard_map/reduce_scatter | solution.py:394
  2451.7 42.4 %reduce-scatter.32.cloned.1.call-done = f32[128,384]{1,0:T(8,128)} async-done(((f32[1024,384]{1,0:T(8,128)}), f32[128,384]{1,0:T(8,128)}) %reduce-scatter.32.cloned.1.call-update) | async-done | bytes 196624 | tf_op jit(solution)/shard_map/reduce_scatter | solution.py:392
  2494.1 42.4 %reduce-scatter.30.cloned.1.call-done = f32[128,384]{1,0:T(8,128)} async-done(((f32[1024,384]{1,0:T(8,128)}), f32[128,384]{1,0:T(8,128)}) %reduce-scatter.30.cloned.1.call-update) | async-done | bytes 196624 | tf_op jit(solution)/shard_map/reduce_scatter | solution.py:391
  2536.5 45.1 %reduce-scatter.42.cloned.1.call-done = f32[128,512]{1,0:T(8,128)} async-done(((f32[1024,512]{1,0:T(8,128)}), f32[128,512]{1,0:T(8,128)}) %reduce-scatter.42.cloned.1.call-update) | async-done | bytes 262160 | tf_op jit(solution)/shard_map/reduce_scatter | solution.py:395
  2581.6 45.3 %reduce-scatter.46.cloned.1.call-done = f32[128,512]{1,0:T(8,128)} async-done(((f32[1024,512]{1,0:T(8,128)}), f32[128,512]{1,0:T(8,128)}) %reduce-scatter.46.cloned.1.call-update) | async-done | bytes 262160 | tf_op jit(solution)/shard_map/reduce_scatter | solution.py:396
  2626.9 45.1 %reduce-scatter.50.cloned.1.call-done = f32[512,128]{1,0:T(8,128)} async-done(((f32[512,1024]{1,0:T(8,128)}), f32[512,128]{1,0:T(8,128)}) %reduce-scatter.50.cloned.1.call-update) | async-done | bytes 262160 | tf_op jit(solution)/shard_map/reduce_scatter | solution.py:397
  (1986 shorter events, 1330.9 us)
Async XLA Ops:
  7.2 50.2 %slice-start.4 = ((f32[4,1792]{1,0:T(4,128)}), f32[4,256]{1,0:T(4,128)S(1)}, s32[]{:S(2)}) async-start(f32[4,1792]{1,0:T(4,128)} %param.48), calls=%async_computation.46 | async-start | bytes 8192 | tf_op jit(solution)/shard_map/slice | solution.py:286
  7.3 59.7 %copy-start.104 = (f32[24]{0:T(128)S(1)}, f32[24]{0:T(128)}, u32[]{:S(2)}) copy-start(f32[24]{0:T(128)} %param.50) | copy-start | bytes 292
  7.3 60.3 %copy-start.53 = (s32[1,2048]{1,0:T(1,128)S(1)}, s32[1,2048]{1,0:T(1,128)}, u32[]{:S(2)}) copy-start(s32[1,2048]{1,0:T(1,128)} %param.35) | copy-start | bytes 24580
  7.3 61.0 %copy-start.70 = (bf16[128,256]{1,0:T(8,128)(2,1)S(1)}, bf16[128,256]{1,0:T(8,128)(2,1)}, u32[]{:S(2)}) copy-start(bf16[128,256]{1,0:T(8,128)(2,1)} %param.45) | copy-start | bytes 196612
  7.3 70.7 %copy-start.67 = (bf16[128,384]{1,0:T(8,128)(2,1)S(1)}, bf16[128,384]{1,0:T(8,128)(2,1)}, u32[]{:S(2)}) copy-start(bf16[128,384]{1,0:T(8,128)(2,1)} %param.44) | copy-start | bytes 294916
  7.3 80.2 %copy-start.68 = (bf16[128,384]{1,0:T(8,128)(2,1)S(1)}, bf16[128,384]{1,0:T(8,128)(2,1)}, u32[]{:S(2)}) copy-start(bf16[128,384]{1,0:T(8,128)(2,1)} %param.43) | copy-start | bytes 294916
  7.3 91.5 %copy-start.69 = (bf16[384,128]{1,0:T(8,128)(2,1)S(1)}, bf16[384,128]{1,0:T(8,128)(2,1)}, u32[]{:S(2)}) copy-start(bf16[384,128]{1,0:T(8,128)(2,1)} %param.47) | copy-start | bytes 294916
  7.3 104.4 %all-gather.19.cloned.1.call-start = ((), (), s32[]{:S(2)}) async-start(), calls=%async_computation.23 | async-start | bytes 1179648 | tf_op jit(solution)/shard_map/all_gather | solution.py:340
  8.1 112.4 %all-gather.9.cloned.1.call-start = ((), (), s32[]{:S(2)}) async-start(), calls=%async_computation.17 | async-start | bytes 5242880 | tf_op jit(solution)/shard_map/all_gather | solution.py:320
  12.2 493.5 %all-gather.15.cloned.1.call-start = ((), (), s32[]{:S(2)}) async-start(), calls=%async_computation.21 | async-start | bytes 1179648 | tf_op jit(solution)/shard_map/all_gather | solution.py:339
  12.9 493.5 %all-gather.11.cloned.1.call-start = ((), (), s32[]{:S(2)}) async-start(), calls=%async_computation.19 | async-start | bytes 1179648 | tf_op jit(solution)/shard_map/all_gather | solution.py:338
  13.5 493.9 %all-gather.21.cloned.1.call-start = ((), (), s32[]{:S(2)}) async-start(), calls=%async_computation.24 | async-start | bytes 5242880 | tf_op jit(solution)/shard_map/all_gather | solution.py:345
  13.6 415.9 %copy-start.96 = (f32[32]{0:T(128)}, f32[32]{0:T(128)S(1)}, u32[]{:S(2)}) copy-start(f32[32]{0:T(128)S(1)} %multiply_power_fusion) | copy-start | bytes 388
  48.5 370.5 %copy-start.95 = (f32[384]{0:T(512)}, f32[384]{0:T(512)S(1)}, u32[]{:S(2)}) copy-start(f32[384]{0:T(512)S(1)} %mul.1326) | copy-start | bytes 4612
  57.4 83.7 %copy-start.59 = (bf16[1024,6]{0,1:T(8,128)(2,1)}, bf16[1024,6]{0,1:T(8,128)(2,1)S(1)}, u32[]{:S(2)}) copy-start(bf16[1024,6]{0,1:T(8,128)(2,1)S(1)} %all_gather.65) | copy-start | bytes 36868
  57.4 70.3 %copy-start.74 = (f32[640]{0:T(1024)}, f32[640]{0:T(1024)S(1)}, u32[]{:S(2)}) copy-start(f32[640]{0:T(1024)S(1)} %get-tuple-element.1443) | copy-start | bytes 7684
  57.5 70.3 %copy-start.76 = (f32[640]{0:T(1024)}, f32[640]{0:T(1024)S(1)}, u32[]{:S(2)}) copy-start(f32[640]{0:T(1024)S(1)} %get-tuple-element.1444) | copy-start | bytes 7684
  57.5 70.3 %copy-start.78 = (f32[640]{0:T(1024)}, f32[640]{0:T(1024)S(1)}, u32[]{:S(2)}) copy-start(f32[640]{0:T(1024)S(1)} %get-tuple-element.1445) | copy-start | bytes 7684
  57.5 70.3 %copy-start.80 = (f32[640]{0:T(1024)}, f32[640]{0:T(1024)S(1)}, u32[]{:S(2)}) copy-start(f32[640]{0:T(1024)S(1)} %get-tuple-element.1446) | copy-start | bytes 7684
  111.8 537.0 %reduce-scatter.18.cloned.1.call-start = ((), (), s32[]{:S(2)}) async-start(), calls=%async_computation.18 | async-start | bytes 10485760 | tf_op jit(solution)/shard_map/reduce_scatter | solution.py:334
  134.8 284.3 %copy-start.7 = (bf16[2048,384]{0,1:T(8,128)(2,1)}, bf16[2048,384]{0,1:T(8,128)(2,1)S(1)}, u32[]{:S(2)}) copy-start(bf16[2048,384]{0,1:T(8,128)(2,1)S(1)} %slice.196) | copy-start | bytes 4718596
  434.3 63.8 %copy-start.54 = (bf16[128,1024]{1,0:T(8,128)(2,1)S(1)}, bf16[128,1024]{1,0:T(8,128)(2,1)}, u32[]{:S(2)}) copy-start(bf16[128,1024]{1,0:T(8,128)(2,1)} %all_gather.64) | copy-start | bytes 786436
  505.6 226.3 %all-gather.17.cloned.1.call-start = ((), (), s32[]{:S(2)}) async-start(), calls=%async_computation.22 | async-start | bytes 5242880 | tf_op jit(solution)/shard_map/all_gather | solution.py:344
  506.4 306.4 %all-gather.13.cloned.1.call-start = ((), (), s32[]{:S(2)}) async-start(), calls=%async_computation.20 | async-start | bytes 5242880 | tf_op jit(solution)/shard_map/all_gather | solution.py:343
  507.1 642.4 %all-gather.23.cloned.1.call-start = ((), (), s32[]{:S(2)}) async-start(), calls=%async_computation.25 | async-start | bytes 5242880 | tf_op jit(solution)/shard_map/all_gather | solution.py:364
  513.3 137.8 %copy-start.72 = (f32[1024]{0:T(1024)S(1)}, f32[1024]{0:T(1024)}, u32[]{:S(2)}) copy-start(f32[1024]{0:T(1024)} %param.38) | copy-start | bytes 12292
  651.0 179.3 %copy-start.4 = (f32[512,1024]{1,0:T(8,128)}, f32[512,1024]{1,0:T(8,128)S(1)}, u32[]{:S(2)}) copy-start(f32[512,1024]{1,0:T(8,128)S(1)} %get-tuple-element.1580) | copy-start | bytes 6291460
  651.0 179.3 %copy-start.88 = (f32[512]{0:T(512)}, f32[512]{0:T(512)S(1)}, u32[]{:S(2)}) copy-start(f32[512]{0:T(512)S(1)} %fusion.254) | copy-start | bytes 6148
  833.2 1038.0 %reduce-scatter.40.cloned.1.call-start = ((), (), s32[]{:S(2)}) async-start(), calls=%async_computation.36 | async-start | bytes 5242880 | tf_op jit(solution)/shard_map/reduce_scatter | solution.py:352
  839.7 1034.5 %reduce-scatter.44.cloned.1.call-start = ((), (), s32[]{:S(2)}) async-start(), calls=%async_computation.38 | async-start | bytes 5242880 | tf_op jit(solution)/shard_map/reduce_scatter | solution.py:355
  846.2 1031.0 %reduce-scatter.48.cloned.1.call-start = ((), (), s32[]{:S(2)}) async-start(), calls=%async_computation.40 | async-start | bytes 5242880 | tf_op jit(solution)/shard_map/reduce_scatter | solution.py:358
  1149.3 747.4 %reduce-scatter.20.cloned.1.call-start = ((), (), s32[]{:S(2)}) async-start(), calls=%async_computation.26 | async-start | bytes 5242880 | tf_op jit(solution)/shard_map/reduce_scatter | solution.py:384
  1821.0 124.5 %reduce-scatter.36.cloned.1.call-start = ((), (), s32[]{:S(2)}) async-start(), calls=%async_computation.34 | async-start | bytes 36864 | tf_op jit(solution)/shard_map/reduce_scatter | solution.py:393
  1824.5 145.4 %reduce-scatter.22.cloned.1.call-start = ((), (), s32[]{:S(2)}) async-start(), calls=%async_computation.27 | async-start | bytes 589824 | tf_op jit(solution)/shard_map/reduce_scatter | solution.py:389
  1830.0 177.5 %reduce-scatter.28.cloned.1.call-start = ((), (), s32[]{:S(2)}) async-start(), calls=%async_computation.30 | async-start | bytes 589824 | tf_op jit(solution)/shard_map/reduce_scatter | solution.py:390
  1833.8 310.5 %reduce-scatter.24.cloned.1.call-start = ((), (), s32[]{:S(2)}) async-start(), calls=%async_computation.28 | async-start | bytes 540672 | tf_op jit(solution)/shard_map/reduce_scatter | solution.py:400
  1841.2 436.6 %reduce-scatter.26.cloned.1.call-start = ((), (), s32[]{:S(2)}) async-start(), calls=%async_computation.29 | async-start | bytes 540672 | tf_op jit(solution)/shard_map/reduce_scatter | solution.py:401
  1848.5 564.4 %reduce-scatter.34.cloned.1.call-start = ((), (), s32[]{:S(2)}) async-start(), calls=%async_computation.33 | async-start | bytes 1081344 | tf_op jit(solution)/shard_map/reduce_scatter | solution.py:402
  1853.0 598.7 %reduce-scatter.38.cloned.1.call-start = ((), (), s32[]{:S(2)}) async-start(), calls=%async_computation.35 | async-start | bytes 1769472 | tf_op jit(solution)/shard_map/reduce_scatter | solution.py:394
  1859.0 635.1 %reduce-scatter.32.cloned.1.call-start = ((), (), s32[]{:S(2)}) async-start(), calls=%async_computation.32 | async-start | bytes 1769472 | tf_op jit(solution)/shard_map/reduce_scatter | solution.py:392
  1865.0 671.5 %reduce-scatter.30.cloned.1.call-start = ((), (), s32[]{:S(2)}) async-start(), calls=%async_computation.31 | async-start | bytes 1769472 | tf_op jit(solution)/shard_map/reduce_scatter | solution.py:391
  1871.2 710.4 %reduce-scatter.42.cloned.1.call-start = ((), (), s32[]{:S(2)}) async-start(), calls=%async_computation.37 | async-start | bytes 2359296 | tf_op jit(solution)/shard_map/reduce_scatter | solution.py:395
  1874.1 752.8 %reduce-scatter.46.cloned.1.call-start = ((), (), s32[]{:S(2)}) async-start(), calls=%async_computation.39 | async-start | bytes 2359296 | tf_op jit(solution)/shard_map/reduce_scatter | solution.py:396
  1877.1 794.9 %reduce-scatter.50.cloned.1.call-start = ((), (), s32[]{:S(2)}) async-start(), calls=%async_computation.41 | async-start | bytes 2359296 | tf_op jit(solution)/shard_map/reduce_scatter | solution.py:397
  1880.2 60.7 %copy-start.93 = (f32[512]{0:T(512)S(1)}, f32[512]{0:T(512)}, u32[]{:S(2)}) copy-start(f32[512]{0:T(512)} %copy-done.92) | copy-start | bytes 6148
  1880.2 60.7 %copy-start.73 = (f32[1024]{0:T(1024)S(1)}, f32[1024]{0:T(1024)}, u32[]{:S(2)}) copy-start(f32[1024]{0:T(1024)} %param.38) | copy-start | bytes 12292
  1880.2 60.7 %copy-start.89 = (f32[512]{0:T(512)S(1)}, f32[512]{0:T(512)}, u32[]{:S(2)}) copy-start(f32[512]{0:T(512)} %copy-done.88) | copy-start | bytes 6148
  1880.2 60.7 %copy-start.91 = (f32[512]{0:T(512)S(1)}, f32[512]{0:T(512)}, u32[]{:S(2)}) copy-start(f32[512]{0:T(512)} %copy-done.90) | copy-start | bytes 6148
  (133 other events, 1035.2 us)
Sparse Core Ops, SparseCore 0:
  10.1 27.3 all-gather.18
  39.6 80.7 all-gather.8
  122.3 22.0 all-gather.14
  146.1 23.5 all-gather.10
  171.1 80.7 all-gather.20
  505.7 143.0 reduce-scatter.17
  650.4 81.4 all-gather.16
  733.5 79.2 all-gather.12
  833.4 79.2 all-gather.22
  914.8 75.2 reduce-scatter.39
  992.5 77.2 reduce-scatter.43
  1149.4 75.4 reduce-scatter.47
  1821.1 75.5 reduce-scatter.19
  1900.2 31.7 reduce-scatter.35
  1935.7 34.1 reduce-scatter.21
  1973.4 34.0 reduce-scatter.27
  2010.3 134.0 reduce-scatter.23
  2147.0 130.7 reduce-scatter.25
  2280.7 132.1 reduce-scatter.33
  2416.6 35.0 reduce-scatter.37
  2455.6 38.4 reduce-scatter.31
  2498.0 38.4 reduce-scatter.29
  2540.3 41.1 reduce-scatter.41
  2585.6 41.2 reduce-scatter.45
  2630.8 41.2 reduce-scatter.49
where the time goes:
time: 2710 us; the launch traced here: 2680 us
  waiting for transfers between devices  1040 us (38%)
  local copies, waits for them, and re-layouts  599 us (22%)
  matrix products  549 us (20%)
  other arithmetic  321 us (12%)
  blocking collectives  134 us (5%)
    dynamic_update_slice x48, local copies, waits for them, and re-layouts, state_scan(): final_state, outputs = lax.scan(jax.checkpoint(advance), initial, elements)  294 us
    dot_general x36, matrix products, matmul(): return jnp.dot(left, right)  183 us
    reduce_scatter x1, waiting for transfers between devices, per_device(): lax.psum_scatter(mixer_grads[2], ('dp', 'tensor'), scatter_dimension=0, t...  137 us
    reduce_scatter x1, waiting for transfers between devices, per_device(): lax.psum_scatter(mixer_part, 'tensor', scatter_dimension=0, tiled=True)  136 us
    reduce_scatter x1, waiting for transfers between devices, per_device(): lax.psum_scatter(mixer_grads[7], ('dp', 'tensor'), scatter_dimension=0, t...  135 us
    reduce_scatter x1, waiting for transfers between devices, per_device(): lax.psum_scatter(mixer_grads[3], ('dp', 'tensor'), scatter_dimension=0, t...  133 us
    squeeze x176, local copies, waits for them, and re-layouts, state_scan(): final_state, outputs = lax.scan(jax.checkpoint(advance), initial, elements)  100 us
    dot_general x64, matrix products, advance(): jnp.einsum('tsh,shp->thp', mixing, x_block, precision=lax.Precision.HIGHEST)  86.6 us
  transfers between devices with their start and end apart: 25, of which 16 were waited for; matrix products, arithmetic and copies ran while one was open for 54% of the time, Pallas kernels for 0%

commit v1 on v0

v1 whole, which is shorter than its diff:
```python
import functools

import jax
import jax.numpy as jnp
from jax import lax
from jax.experimental import pallas as pl
from jax.experimental.pallas import tpu as pltpu
from jax.sharding import PartitionSpec as P

QH = 8
KVH = 2
HD = 64
MH = 24
MP = 64
NS = 128
KCONV = 4
GROUP = QH // KVH
INNER = MH * MP
SPAN = 128
HALO = 16
QB = 128
KB = 256
NEG = -1e30

epsilon = 1e-05
rope_base = 100000000000.0
f32 = jnp.float32
bf16 = jnp.bfloat16

NN = (((1,), (0,)), ((), ()))
NT = (((1,), (1,)), ((), ()))
TN = (((0,), (0,)), ((), ()))


def dot(a, b, dims=NN):
    return lax.dot_general(a, b, dims, preferred_element_type=f32)


def split2(v, axis=1):
    hi = v.astype(bf16)
    lo = (v - hi.astype(f32)).astype(bf16)
    return jnp.concatenate([hi, lo], axis=axis)


def params(mb):
    return pltpu.CompilerParams(vmem_limit_bytes=mb * 1024 * 1024)


def sds(shape, dtype):
    return jax.ShapeDtypeStruct(shape, dtype)


def whole(shape):
    return pl.BlockSpec(shape, lambda *_: (0,) * len(shape))


def attn_keep(segk_ref, segq_ref, off, i, back):
    pos_k = lax.broadcasted_iota(jnp.int32, (KB, QB), 0) + off
    pos_q = lax.broadcasted_iota(jnp.int32, (KB, QB), 1) + (back + i * QB)
    same = segk_ref[pl.ds(off, KB), :] == segq_ref[:, i * QB : (i + 1) * QB]
    return same & (pos_k <= pos_q)


def head_columns(place_ref, base, pair):
    return pl.ds(pl.multiple_of(place_ref[base + pair] * (2 * HD), 2 * HD), 2 * HD)


def stack_heads(ref, i, columns):
    rows = slice(i * QB, (i + 1) * QB)
    heads = []
    for at in columns:
        pair = ref[rows, at]
        heads += [pair[:, :HD], pair[:, HD:]]
    return jnp.concatenate(heads, axis=0)


def attn_fwd_kernel(first_ref, q_ref, k_ref, vt_ref, segq_ref, segk_ref, o_ref, lse_ref):
    rows = q_ref.shape[0]
    back = k_ref.shape[1] - rows
    wide = GROUP * QB
    for i in range(rows // QB):
        last = (back + (i + 1) * QB + KB - 1) // KB
        for g in range(KVH):
            columns = [head_columns(first_ref, rows // QB, g * GROUP // 2 + n) for n in range(GROUP // 2)]
            queries = stack_heads(q_ref, i, columns)

            def body(j, carry):
                top, total, acc = carry
                off = pl.multiple_of(j * KB, KB)
                scores = dot(k_ref[g, pl.ds(off, KB), :], queries, NT)
                keep = attn_keep(segk_ref, segq_ref, off, i, back)
                keep = jnp.concatenate([keep] * GROUP, axis=1)
                scores = jnp.where(keep, scores, NEG)
                new_top = jnp.maximum(top, jnp.max(scores, axis=0, keepdims=True))
                scale = jnp.exp(top - new_top)
                probs = jnp.exp(scores - new_top)
                total = total * scale + jnp.sum(probs, axis=0, keepdims=True)
                vt = vt_ref[g * HD : (g + 1) * HD, pl.ds(off, KB)]
                acc = acc * scale + dot(vt, probs.astype(bf16))
                return new_top, total, acc

            start = (jnp.full((1, wide), NEG, f32), jnp.zeros((1, wide), f32), jnp.zeros((HD, wide), f32))
            top, total, acc = lax.fori_loop(first_ref[i], last, body, start)
            lse_ref[i * KVH + g : i * KVH + g + 1, :] = top + jnp.log(total)
            acc = acc / total
            for h in range(0, GROUP, 2):
                pair = jnp.concatenate(
                    [acc[:, h * QB : (h + 1) * QB], acc[:, (h + 1) * QB : (h + 2) * QB]], axis=0
                ).T
                o_ref[i * QB : (i + 1) * QB, columns[h // 2]] = pair.astype(bf16)


def attn_bwd_kernel(first_ref, q_ref, k_ref, v_ref, do_ref, o_ref, lse_ref, segq_ref, segk_ref,
                    dq_ref, dk_ref, dv_ref):
    rows = q_ref.shape[0]
    back = k_ref.shape[1] - rows
    wide = GROUP * QB
    dk_ref[...] = jnp.zeros_like(dk_ref)
    dv_ref[...] = jnp.zeros_like(dv_ref)
    for i in range(rows // QB):
        last = (back + (i + 1) * QB + KB - 1) // KB
        for g in range(KVH):
            columns = [head_columns(first_ref, rows // QB, g * GROUP // 2 + n) for n in range(GROUP // 2)]
            queries = stack_heads(q_ref, i, columns)
            grads = stack_heads(do_ref, i, columns)
            outs = stack_heads(o_ref, i, columns)
            prod = grads.astype(f32) * outs.astype(f32)
            ones = jnp.ones((8, 2 * HD), bf16)
            delta = dot(ones, split2(prod), NT)[0:1, :]
            lse = lse_ref[i * KVH + g : i * KVH + g + 1, :]

            def body(j, acc):
                off = pl.multiple_of(j * KB, KB)
                keys = k_ref[g, pl.ds(off, KB), :]
                vals = v_ref[g, pl.ds(off, KB), :]
                keep = attn_keep(segk_ref, segq_ref, off, i, back)
                keep = jnp.concatenate([keep] * GROUP, axis=1)
                scores = jnp.where(keep, dot(keys, queries, NT), NEG)
                probs = jnp.exp(scores - lse)
                dprobs = dot(vals, grads, NT)
                dscores = (probs * (dprobs - delta)).astype(bf16)
                dv_ref[g, pl.ds(off, KB), :] += dot(probs.astype(bf16), grads)
                dk_ref[g, pl.ds(off, KB), :] += dot(dscores, queries)
                return acc + dot(keys, dscores, TN)

            acc = lax.fori_loop(first_ref[i], last, body, jnp.zeros((HD, wide), f32))
            acc = acc * (HD ** -0.5)
            for h in range(0, GROUP, 2):
                pair = jnp.concatenate(
                    [acc[:, h * QB : (h + 1) * QB], acc[:, (h + 1) * QB : (h + 2) * QB]], axis=0
                ).T
                dq_ref[i * QB : (i + 1) * QB, columns[h // 2]] = pair.astype(bf16)


SMEM = pl.BlockSpec(memory_space=pltpu.SMEM)


def vmem_specs(n):
    return [pl.BlockSpec(memory_space=pltpu.VMEM)] * n


def attn_fwd(first, q, k, vt, segq, segk):
    rows = q.shape[0]
    return pl.pallas_call(
        attn_fwd_kernel,
        out_shape=(sds(q.shape, bf16), sds((rows // QB * KVH, GROUP * QB), f32)),
        in_specs=[SMEM] + vmem_specs(5),
        out_specs=tuple(vmem_specs(2)),
        compiler_params=params(40),
        cost_estimate=pl.CostEstimate(flops=4_000_000_000, bytes_accessed=4_000_000, transcendentals=4_000_000),
        name="attn_fwd",
    )(first, q, k, vt, segq, segk)


def attn_bwd(first, q, k, v, do, o, lse, segq, segk):
    return pl.pallas_call(
        attn_bwd_kernel,
        out_shape=(sds(q.shape, bf16), sds(k.shape, f32), sds(k.shape, f32)),
        in_specs=[SMEM] + vmem_specs(8),
        out_specs=tuple(vmem_specs(3)),
        compiler_params=params(40),
        cost_estimate=pl.CostEstimate(flops=10_000_000_000, bytes_accessed=8_000_000, transcendentals=4_000_000),
        name="attn_bwd",
    )(first, q, k, v, do, o, lse, segq, segk)


LANE = 128
COLS = (INNER + 2 * NS) // LANE


def expander():
    head = jnp.arange(LANE)[:, None]
    channel = jnp.arange(INNER)[None, :] // MP
    return (head == channel).astype(bf16)


def tri_masks():
    t = lax.broadcasted_iota(jnp.int32, (SPAN, SPAN), 0)
    s = lax.broadcasted_iota(jnp.int32, (SPAN, SPAN), 1)
    return t, s


def widen(v, spread2):
    return dot(split2(v), spread2)


def conv_block(u_ref, tap_ref, meta, base, col):
    lanes = slice(col * LANE, (col + 1) * LANE)
    window = u_ref[pl.ds(base + HALO - 8, SPAN + 8), lanes]
    taps = [window[8:, :]]
    for j in range(1, KCONV):
        taps.append(window[8 - j : 8 - j + SPAN, :] * meta[:, j : j + 1])
    total = tap_ref[KCONV : KCONV + 1, lanes] + tap_ref[KCONV - 1 : KCONV, lanes] * taps[0]
    for j in range(1, KCONV):
        total = total + tap_ref[KCONV - 1 - j : KCONV - j, lanes] * taps[j]
    return taps, total


def mamba_pre_kernel(u_ref, tap_ref, meta_ref, dtr_ref, head_ref, spread_ref,
                     mix_ref, dt_ref, cum_ref, cumt_ref, ec_ref, fw_ref, g_ref, fin_ref):
    c = pl.program_id(0)
    base = pl.multiple_of(c * SPAN, SPAN)

    @pl.when(c == 0)
    def _():
        fin_ref[...] = jnp.zeros_like(fin_ref)

    meta = meta_ref[...]
    for col in range(COLS):
        total = conv_block(u_ref, tap_ref, meta, base, col)[1]
        mix_ref[:, col * LANE : (col + 1) * LANE] = (total * jax.nn.sigmoid(total)).astype(bf16)
    raw = dtr_ref[...] + head_ref[0:1, :]
    dt = jnp.maximum(raw, 0.0) + jnp.log1p(jnp.exp(-jnp.abs(raw)))
    decay = dt * head_ref[1:2, :]
    t, s = tri_masks()
    lower = (t >= s).astype(f32)
    cum = lax.dot_general(lower, decay, NN, precision=lax.Precision.HIGHEST, preferred_element_type=f32)
    end = cum[SPAN - 1 : SPAN, :]
    ec = meta[:, 4:5] * jnp.exp(cum)
    fw = meta[:, 5:6] * jnp.exp(end - cum)
    gain = ec[SPAN - 1 : SPAN, :]
    dt_ref[...] = dt
    cum_ref[...] = cum
    cumt_ref[...] = cum.T[: cumt_ref.shape[0], :]
    ec_ref[...] = ec
    fw_ref[...] = fw
    gain8 = jnp.broadcast_to(gain, (8, LANE))
    g_ref[...] = gain8
    spread2 = spread_ref[...]
    weight = widen(fw * dt, spread2)
    x = mix_ref[:, :INNER].astype(f32)
    b = mix_ref[:, INNER : INNER + NS]
    state = fin_ref[...] * widen(gain8, spread2)[0:1, :]
    fin_ref[...] = state + dot(b, (x * weight).astype(bf16), TN)


def chunk_spec(width):
    return pl.BlockSpec((SPAN, width), lambda c: (c, 0))


def mamba_pre(u, taps, meta, dt_raw, heads, spread2):
    rows = meta.shape[0]
    n = rows // SPAN
    width = INNER + 2 * NS
    hl = 32
    return pl.pallas_call(
        mamba_pre_kernel,
        grid=(n,),
        in_specs=[whole(u.shape), whole(taps.shape), chunk_spec(8), chunk_spec(LANE), whole(heads.shape),
                  whole(spread2.shape)],
        out_specs=(chunk_spec(width), chunk_spec(LANE), chunk_spec(LANE), pl.BlockSpec((hl, SPAN), lambda c: (0, c)),
                   chunk_spec(LANE), chunk_spec(LANE), pl.BlockSpec((8, LANE), lambda c: (c, 0)), whole((NS, INNER))),
        out_shape=(sds((rows, width), bf16), sds((rows, LANE), f32), sds((rows, LANE), f32), sds((hl, rows), f32),
                   sds((rows, LANE), f32), sds((rows, LANE), f32), sds((8 * n, LANE), f32), sds((NS, INNER), f32)),
        compiler_params=params(40),
        cost_estimate=pl.CostEstimate(flops=1_000_000_000, bytes_accessed=9_000_000, transcendentals=2_000_000),
        name="mamba_pre",
    )(u, taps, meta, dt_raw, heads, spread2)


def pair_halves(v):
    lane = lax.broadcasted_iota(jnp.int32, v.shape, 1)
    zero = jnp.zeros_like(v)
    return jnp.concatenate([jnp.where(lane < MP, v, zero), jnp.where(lane < MP, zero, v)], axis=0)


def mamba_fwd_kernel(init_ref, mix_ref, dt_ref, cum_ref, cumt_ref, ec_ref, fw_ref, g_ref, segc_ref, segr_ref,
                     z_ref, skip_ref, spread_ref, gated_ref, full_ref, states_ref, state_ref):
    c = pl.program_id(0)

    @pl.when(c == 0)
    def _():
        state_ref[...] = init_ref[...]

    state = state_ref[...].astype(bf16)
    states_ref[0] = state
    spread2 = spread_ref[...]
    b = mix_ref[:, INNER : INNER + NS]
    cm = mix_ref[:, INNER + NS :]
    t, s = tri_masks()
    allowed = (segc_ref[...] == segr_ref[...]) & (t >= s)
    off = jnp.where(allowed, 0.0, NEG)
    affinity = dot(cm, b, NT)
    cum = cum_ref[...]
    dt = dt_ref[...]
    dt_wide = widen(dt, spread2)
    ec_wide = widen(ec_ref[...], spread2)
    carried = dot(cm, state) * ec_wide
    for p in range(MH // 2):
        lanes = slice(p * LANE, (p + 1) * LANE)
        x = mix_ref[:, lanes].astype(f32)
        pieces = []
        for h in (2 * p, 2 * p + 1):
            gap = cum[:, h : h + 1] - cumt_ref[h : h + 1, :] + off
            pieces.append((affinity * jnp.exp(gap)).astype(bf16))
        scaled = (x * dt_wide[:, lanes]).astype(bf16)
        y = dot(jnp.concatenate(pieces, axis=1), pair_halves(scaled)) + carried[:, lanes]
        y = y + skip_ref[0:1, lanes] * x
        z = z_ref[:, lanes]
        full_ref[:, lanes] = y.astype(bf16)
        gated_ref[:, lanes] = (y * (z * jax.nn.sigmoid(z))).astype(bf16)
    weight = widen(fw_ref[...] * dt, spread2)
    x = mix_ref[:, :INNER].astype(f32)
    gain = widen(g_ref[...], spread2)[0:1, :]
    state_ref[...] = state_ref[...] * gain + dot(b, (x * weight).astype(bf16), TN)


def mamba_fwd(init, mix, dt, cum, cumt, ec, fw, g, segc, segr, z, skip, spread2):
    rows = mix.shape[0]
    n = rows // SPAN
    return pl.pallas_call(
        mamba_fwd_kernel,
        grid=(n,),
        in_specs=[whole(init.shape), chunk_spec(mix.shape[1]), chunk_spec(LANE), chunk_spec(LANE),
                  pl.BlockSpec((cumt.shape[0], SPAN), lambda c: (0, c)), chunk_spec(LANE), chunk_spec(LANE),
                  pl.BlockSpec((8, LANE), lambda c: (c, 0)), chunk_spec(1), pl.BlockSpec((1, SPAN), lambda c: (0, c)),
                  chunk_spec(INNER), whole(skip.shape), whole(spread2.shape)],
        out_specs=(chunk_spec(INNER), chunk_spec(INNER), pl.BlockSpec((1, NS, INNER), lambda c: (c, 0, 0))),
        out_shape=(sds((rows, INNER), bf16), sds((rows, INNER), bf16), sds((n, NS, INNER), bf16)),
        scratch_shapes=[pltpu.VMEM((NS, INNER), f32)],
        compiler_params=params(40),
        cost_estimate=pl.CostEstimate(flops=3_000_000_000, bytes_accessed=12_000_000, transcendentals=3_000_000),
        name="mamba_fwd",
    )(init, mix, dt, cum, cumt, ec, fw, g, segc, segr, z, skip, spread2)


def mamba_bpre_kernel(dg_ref, z_ref, full_ref, cm_ref, ec_ref, g_ref, spread_ref, dy_ref, dz_ref, back_ref):
    c = pl.program_id(0)

    @pl.when(c == 0)
    def _():
        back_ref[...] = jnp.zeros_like(back_ref)

    spread2 = spread_ref[...]
    z = z_ref[...]
    sig = jax.nn.sigmoid(z)
    dg = dg_ref[...].astype(f32)
    dy = dg * (z * sig)
    dy_ref[...] = dy.astype(bf16)
    dz_ref[...] = (dg * full_ref[...].astype(f32) * (sig * (1.0 + z * (1.0 - sig)))).astype(bf16)
    weighted = (dy * widen(ec_ref[...], spread2)).astype(bf16)
    gain = widen(g_ref[...], spread2)[0:1, :]
    back_ref[...] = back_ref[...] * gain + dot(cm_ref[...], weighted, TN)


def mamba_bpre(dg, z, full, mix, ec, g, spread2):
    rows = dg.shape[0]
    n = rows // SPAN
    rev = lambda width, col=0: pl.BlockSpec((SPAN, width), lambda c: (n - 1 - c, col))
    return pl.pallas_call(
        mamba_bpre_kernel,
        grid=(n,),
        in_specs=[rev(INNER), rev(INNER), rev(INNER), rev(NS, (INNER + NS) // NS), rev(LANE),
                  pl.BlockSpec((8, LANE), lambda c: (n - 1 - c, 0)), whole(spread2.shape)],
        out_specs=(rev(INNER), rev(INNER), whole((NS, INNER))),
        out_shape=(sds((rows, INNER), bf16), sds((rows, INNER), bf16), sds((NS, INNER), f32)),
        compiler_params=params(40),
        cost_estimate=pl.CostEstimate(flops=500_000_000, bytes_accessed=11_000_000, transcendentals=1_000_000),
        name="mamba_bpre",
    )(dg, z, full, mix, ec, g, spread2)


def mamba_bwd_kernel(init_ref, mix_ref, dt_ref, cum_ref, cumt_ref, ec_ref, fw_ref, g_ref, segc_ref, segr_ref,
                     dy_ref, states_ref, u_ref, tap_ref, meta_ref, skip_ref, head_ref, spread_ref, gather_ref,
                     dpre_ref, ddt_ref, conv_ref, small_ref, dstate_ref, acc_ref, rows_ref, dx_ref, dbc_ref):
    step = pl.program_id(0)
    c = pl.num_programs(0) - 1 - step
    base = pl.multiple_of(c * SPAN, SPAN)

    @pl.when(step == 0)
    def _():
        dstate_ref[...] = init_ref[...]
        conv_ref[...] = jnp.zeros_like(conv_ref)
        small_ref[...] = jnp.zeros_like(small_ref)
        rows_ref[...] = jnp.zeros_like(rows_ref)

    spread2 = spread_ref[...]
    gather2 = gather_ref[...]
    b = mix_ref[:, INNER : INNER + NS]
    cm = mix_ref[:, INNER + NS :]
    cum = cum_ref[...]
    dt = dt_ref[...]
    dt_wide = widen(dt, spread2)
    s, t = tri_masks()
    allowed = (segc_ref[...] == segr_ref[...]) & (t >= s)
    off = jnp.where(allowed, 0.0, NEG)
    affinity = dot(b, cm, NT)
    acc_ref[...] = jnp.zeros_like(acc_ref)
    for p in range(MH // 2):
        lanes = slice(p * LANE, (p + 1) * LANE)
        x = mix_ref[:, lanes].astype(f32)
        scaled = (x * dt_wide[:, lanes]).astype(bf16)
        dy = dy_ref[:, lanes]
        dmix = dot(pair_halves(scaled), dy, NT)
        pieces = []
        total = None
        for q, h in enumerate((2 * p, 2 * p + 1)):
            gap = cumt_ref[h : h + 1, :] - cum[:, h : h + 1] + off
            decays = jnp.exp(gap)
            mixing = (affinity * decays).astype(bf16)
            pieces.append(mixing)
            dm = dmix[q * SPAN : (q + 1) * SPAN, :]
            rows_ref[h : h + 1, :] = jnp.sum(dm * mixing.astype(f32), axis=0, keepdims=True)
            part = dm * decays
            total = part if total is None else total + part
        acc_ref[...] += total
        dx_ref[:, lanes] = dot(jnp.concatenate(pieces, axis=1), pair_halves(dy))
    dscaled = dx_ref[...]
    x = mix_ref[:, :INNER].astype(f32)
    scaled = (x * dt_wide).astype(bf16).astype(f32)
    dy = dy_ref[...].astype(f32)
    dstate = dstate_ref[...]
    dstate_low = dstate.astype(bf16)
    state = states_ref[0]
    ec_wide = widen(ec_ref[...], spread2)
    fw_wide = widen(fw_ref[...], spread2)
    from_state = fw_wide * dot(b, dstate_low)
    carried = ec_wide * dot(cm, state)
    weighted_dy = (dy * ec_wide).astype(bf16)
    cols_sum = dot(split2(scaled * dscaled), gather2)
    carr_sum = dot(split2(dy * carried), gather2)
    fdf_sum = dot(split2(scaled * from_state), gather2)
    dxd = dscaled + from_state
    ddt_direct = dot(split2(x * dxd), gather2)
    skip_part = dot(split2(dy * x), gather2)
    gain = widen(g_ref[...], spread2)[0:1, :]
    state_dot = jnp.sum(dstate * state.astype(f32), axis=0, keepdims=True) * gain
    state_dot = dot(split2(jnp.broadcast_to(state_dot, (8, INNER))), gather2)[0:1, :]
    tt, ss = tri_masks()
    suffix = (ss >= tt).astype(bf16)
    prefix = (ss < tt).astype(bf16)
    suffix2 = jnp.concatenate([suffix, suffix], axis=1)
    dlog = dot(suffix2, split2(carr_sum - cols_sum, axis=0))
    dlog = dlog + dot(suffix2, split2(rows_ref[...]), NT)
    dlog = dlog + dot(jnp.concatenate([prefix, prefix], axis=1), split2(fdf_sum, axis=0)) + state_dot
    decay_rate = head_ref[1:2, :]
    ddt = (ddt_direct + dlog * decay_rate) * (1.0 - jnp.exp(-dt))
    ddt_ref[...] = ddt.astype(bf16)
    small_ref[0:1, :] += jnp.sum(dlog * dt, axis=0, keepdims=True) * decay_rate
    small_ref[1:2, :] += jnp.sum(skip_part, axis=0, keepdims=True)
    small_ref[2:3, :] += jnp.sum(ddt, axis=0, keepdims=True)
    dx_ref[...] = dxd * dt_wide + skip_ref[0:1, :] * dy
    daff = acc_ref[...]
    daff_low = daff.astype(bf16)
    fx = (scaled * fw_wide).astype(bf16)
    dbc_ref[:, :NS] = dot(daff_low, cm) + dot(fx, dstate_low, NT)
    dbc_ref[:, NS:] = dot(daff_low, b, TN) + dot(weighted_dy, state, NT)
    dstate_ref[...] = dstate * gain + dot(cm, weighted_dy, TN)
    meta = meta_ref[...]
    for col in range(COLS):
        lanes = slice(col * LANE, (col + 1) * LANE)
        taps, total = conv_block(u_ref, tap_ref, meta, base, col)
        sig = jax.nn.sigmoid(total)
        if col * LANE < INNER:
            dmixed = dx_ref[:, lanes]
        else:
            dmixed = dbc_ref[:, col * LANE - INNER : (col + 1) * LANE - INNER]
        dpre = dmixed * (sig * (1.0 + total * (1.0 - sig)))
        dpre_ref[:, lanes] = dpre
        for j in range(KCONV):
            conv_ref[KCONV - 1 - j : KCONV - j, lanes] += jnp.sum(dpre * taps[j], axis=0, keepdims=True)
        conv_ref[KCONV : KCONV + 1, lanes] += jnp.sum(dpre, axis=0, keepdims=True)


def mamba_bwd(init, mix, dt, cum, cumt, ec, fw, g, segc, segr, dy, states, u, taps, meta, skip, heads, spread2, gather2):
    rows = mix.shape[0]
    n = rows // SPAN
    width = mix.shape[1]
    rev = lambda w: pl.BlockSpec((SPAN, w), lambda c: (n - 1 - c, 0))
    return pl.pallas_call(
        mamba_bwd_kernel,
        grid=(n,),
        in_specs=[whole(init.shape), rev(width), rev(LANE), rev(LANE),
                  pl.BlockSpec((cumt.shape[0], SPAN), lambda c: (0, n - 1 - c)), rev(LANE), rev(LANE),
                  pl.BlockSpec((8, LANE), lambda c: (n - 1 - c, 0)), rev(1),
                  pl.BlockSpec((1, SPAN), lambda c: (0, n - 1 - c)), rev(INNER),
                  pl.BlockSpec((1, NS, INNER), lambda c: (n - 1 - c, 0, 0)), whole(u.shape), whole(taps.shape),
                  rev(8), whole(skip.shape), whole(heads.shape), whole(spread2.shape), whole(gather2.shape)],
        out_specs=(rev(width), rev(LANE), whole((8, width)), whole((8, LANE))),
        out_shape=(sds((rows, width), f32), sds((rows, LANE), bf16), sds((8, width), f32), sds((8, LANE), f32)),
        scratch_shapes=[pltpu.VMEM((NS, INNER), f32), pltpu.VMEM((SPAN, SPAN), f32), pltpu.VMEM((LANE, SPAN), f32),
                        pltpu.VMEM((SPAN, INNER), f32), pltpu.VMEM((SPAN, 2 * NS), f32)],
        compiler_params=params(56),
        cost_estimate=pl.CostEstimate(flops=6_000_000_000, bytes_accessed=16_000_000, transcendentals=4_000_000),
        name="mamba_bwd",
    )(init, mix, dt, cum, cumt, ec, fw, g, segc, segr, dy, states, u, taps, meta, skip, heads, spread2, gather2)


class Ring:
    def __init__(self, mesh):
        self.nd = mesh.shape["dp"]
        self.nt = mesh.shape["tensor"]
        k = self.nd.bit_length() - 1
        self.bits = [1 << i for i in range(k)]
        self.masks = [0]
        for bit in self.bits[:0:-1] if k else []:
            pass
        order = [1] + [1 << i for i in range(k - 1, 0, -1)] if k else []
        self.order = order
        masks = [0]
        for bit in reversed(order):
            masks = masks + [m ^ bit for m in masks]
        self.masks = masks

    def dp(self, value, bit):
        return lax.ppermute(value, "dp", [(i, i ^ bit) for i in range(self.nd)])

    def shift(self, value, s):
        n = self.nt
        return lax.ppermute(value, "tensor", [(i, (i + s) % n) for i in range(n)])

    def line(self, value, s):
        n = self.nt
        return lax.ppermute(value, "tensor", [(i, i + s) for i in range(n) if 0 <= i + s < n])

    def gather_dp(self, value):
        rows, cols = value.shape
        if self.nd == 1:
            return value
        near, last = self.order[1:], self.order[0]
        half = cols // 2
        sides = []
        for piece, order in ((value[:, :half], near[::-1]), (value[:, half:], near)):
            held, masks = piece, [0]
            for bit in order:
                held = jnp.concatenate([held, self.dp(held, bit)], axis=0)
                masks = masks + [m ^ bit for m in masks]
            sides.append([held[masks.index(m) * rows : (masks.index(m) + 1) * rows] for m in self.masks[: self.nd // 2]])
        low = jnp.concatenate([jnp.concatenate(side, axis=0) for side in sides], axis=1)
        return jnp.concatenate([low, self.dp(low, last)], axis=0)

    def gather_tensor(self, value):
        return [value] + [self.shift(value, s) for s in range(1, self.nt)]

    def scatter_dp(self, make, cols):
        total = self.nd
        last, near = self.order[0], self.order[1:]
        upper = make(1, 2)
        got = self.dp(upper, last)
        kept = (make(0, 2).astype(f32) + got.astype(f32)).astype(bf16)
        rows = kept.shape[0] // (total // 2)
        half = cols // 2
        blocks = total // 2
        outs = []
        for piece, order in ((kept[:, :half], near), (kept[:, half:], near[::-1])):
            held = [piece[i * rows : (i + 1) * rows] for i in range(blocks)]
            masks = list(self.masks[:blocks])
            for bit in order:
                mine = [i for i, m in enumerate(masks) if not m & bit]
                theirs = [i for i, m in enumerate(masks) if m & bit]
                sent = jnp.concatenate([held[i] for i in theirs], axis=0)
                came = self.dp(sent, bit)
                held = [
                    (held[i].astype(f32) + came[n * rows : (n + 1) * rows].astype(f32)).astype(bf16)
                    for n, i in enumerate(mine)
                ]
                masks = [masks[i] for i in mine]
            outs.append(held[0])
        return jnp.concatenate(outs, axis=1)

    def scatter_tensor(self, parts):
        total = parts[0].astype(f32)
        for s in range(1, self.nt):
            total = total + self.shift(parts[s], self.nt - s).astype(f32)
        return total

    def line_heads(self, value, s):
        return jnp.roll(self.line(value, s), s * (value.shape[1] // self.nt), axis=1)

    def all_sum(self, value):
        for bit in self.bits:
            value = value + self.dp(value, bit)
        return value + sum(self.shift(value, s) for s in range(1, self.nt))


def rms_back(d_normed, values, scale, gain):
    weighted = d_normed * gain
    inner = jnp.mean(weighted * values, axis=-1, keepdims=True)
    gain_grad = jnp.sum(d_normed * values * scale, axis=0)
    return scale * weighted - values * (scale * scale * scale * inner), gain_grad


def rope_tables(rows, start):
    half = HD // 2
    frequency = rope_base ** (-2.0 * jnp.arange(half, dtype=f32) / HD)
    angles = (start + jnp.arange(rows)).astype(f32)[:, None] * frequency[None, :]
    return jnp.cos(angles)[:, None, :], jnp.sin(angles)[:, None, :]


def rotate(values, cosine, sine):
    heads = values.reshape(values.shape[0], -1, HD)
    a, b = heads[..., : HD // 2], heads[..., HD // 2 :]
    return jnp.concatenate([a * cosine - b * sine, b * cosine + a * sine], axis=-1).reshape(values.shape)


def per_device(
    mesh,
    hidden,
    segments,
    cotangent,
    norm_gain,
    ffn_gain,
    query_proj,
    key_proj,
    value_proj,
    attn_out_proj,
    gate_inner,
    input_inner,
    state_proj,
    step_proj,
    mamba_out,
    conv_weight,
    conv_bias,
    decay_log,
    skip_gain,
    step_bias,
    ffn_gate,
    ffn_up,
    ffn_down,
):
    ring = Ring(mesh)
    nd, nt = ring.nd, ring.nt
    di, ti = lax.axis_index("dp"), lax.axis_index("tensor")
    rows, width = hidden.shape
    block = width // nd
    seq = segments.shape[1]
    hops = -(-(seq // 2 - 1) // rows)
    back = hops * rows
    segment = segments[0]

    def permute_width(values, forward=True):
        axis = values.ndim - 1
        pieces = []
        for r in range(nd):
            if forward:
                at = di ^ ring.masks[r]
            else:
                index = jnp.asarray([ring.masks.index(m) for m in range(nd)])
                at = index[di ^ r]
            pieces.append(lax.dynamic_slice_in_dim(values, at * block, block, axis))
        return jnp.concatenate(pieces, axis=axis)

    def relative(values, axis):
        step = values.shape[axis] // nt
        pieces = [
            lax.dynamic_slice_in_dim(values, lax.rem(ti + nt - s, nt) * step, step, axis) for s in range(nt)
        ]
        return jnp.concatenate(pieces, axis=axis)

    step_cols = step_proj.shape[1]
    step_pad = jnp.pad(step_proj, ((0, 0), (0, LANE - step_cols)))

    def gather(packs, widths):
        parts = ring.gather_tensor(packs)
        pieces = []
        at = 0
        for w in widths:
            pieces += [part[:, at : at + w] for part in parts]
            at += w
        full = ring.gather_dp(jnp.concatenate(pieces, axis=1))
        outs, at = [], 0
        for w in widths:
            outs.append(full[:, at : at + w * nt])
            at += w * nt
        return outs

    w_shared = ring.gather_dp(jnp.concatenate([key_proj, value_proj, state_proj], axis=1))
    w_q, w_step4, w_x = gather(
        jnp.concatenate([query_proj, step_pad, input_inner], axis=1),
        (query_proj.shape[1], LANE, input_inner.shape[1]),
    )
    w_z, w_ao, w_mo = gather(
        jnp.concatenate([gate_inner, attn_out_proj.T, mamba_out.T], axis=1),
        (gate_inner.shape[1], attn_out_proj.shape[0], mamba_out.shape[0]),
    )
    w_fg, w_fu = gather(jnp.concatenate([ffn_gate, ffn_up], axis=1), (ffn_gate.shape[1], ffn_up.shape[1]))
    (w_fd,) = gather(ffn_down.T, (ffn_down.shape[0],))
    w_step = jnp.concatenate([w_step4[:, s * LANE : s * LANE + step_cols] for s in range(nt)], axis=1)
    w_step = jnp.pad(w_step, ((0, 0), (0, LANE - MH)))
    w_kv, w_bc = w_shared[:, : 2 * KVH * HD], w_shared[:, 2 * KVH * HD :]

    hid = permute_width(hidden).astype(f32)
    cot = permute_width(cotangent)
    gain1 = permute_width(norm_gain)[None, :]
    gain2 = permute_width(ffn_gain)[None, :]
    scale1 = lax.rsqrt(jnp.mean(hid * hid, axis=-1, keepdims=True) + epsilon)
    normed = (hid * scale1 * gain1).astype(bf16)

    halo = ring.line(normed[rows - HALO :], 1)
    normed_ext = jnp.concatenate([halo, normed], axis=0)

    start = ti * rows
    cosine, sine = rope_tables(rows, start)
    padded = jnp.concatenate([jnp.full((back,), -1, jnp.int32), segment])
    seg_keys = lax.dynamic_slice_in_dim(padded, start, back + rows)
    seg_own = seg_keys[back:]
    seg_col, seg_row = seg_own[:, None], seg_own[None, :]
    chunks = rows // SPAN
    grouped = seg_own.reshape(chunks, SPAN)
    before = jnp.concatenate([seg_keys[back - 1 : back], grouped[:-1, -1]])
    carry_in = (grouped == before[:, None]).astype(f32).reshape(rows)
    in_last = (grouped == grouped[:, -1:]).astype(f32).reshape(rows)
    keeps = [(seg_keys[back - j : back - j + rows] == seg_own).astype(f32) for j in range(KCONV)]
    zero = jnp.zeros((rows,), f32)
    meta = jnp.stack(keeps + [carry_in, in_last, zero, zero], axis=1)
    first_tokens = seg_own.reshape(rows // QB, QB)[:, 0]
    doc_start = jnp.sum((segment[None, :] < first_tokens[:, None]).astype(jnp.int32), axis=1)
    first_block = jnp.maximum(doc_start - (start - back), 0) // KB
    per_place = QH // nt // 2
    place = jnp.stack(
        [lax.rem(ti + nt - a // per_place, nt) * per_place + a % per_place for a in range(QH // 2)]
    ).astype(jnp.int32)
    first_block = jnp.concatenate([first_block.astype(jnp.int32), place])

    kv = dot(normed, w_kv)
    key = rotate(kv[:, : KVH * HD], cosine, sine).astype(bf16)
    value = kv[:, KVH * HD :].astype(bf16)
    kv_own = jnp.concatenate([key, value], axis=1)
    kv_all = jnp.concatenate([ring.line(kv_own, s) for s in range(hops, 0, -1)] + [kv_own], axis=0)
    keys3 = kv_all[:, : KVH * HD].reshape(-1, KVH, HD).transpose(1, 0, 2)
    vals3 = kv_all[:, KVH * HD :].reshape(-1, KVH, HD).transpose(1, 0, 2)
    vals_t = kv_all[:, KVH * HD :].T
    query = rotate(dot(normed, w_q), cosine, sine).astype(bf16)
    query8 = query * jnp.asarray(HD ** -0.5, bf16)

    bc_raw = dot(normed_ext, w_bc)
    x_raw = dot(normed_ext, w_x)
    u = jnp.concatenate([x_raw, bc_raw], axis=1)
    dt_raw = dot(normed, w_step)
    conv_rel = jnp.concatenate([relative(conv_weight[:, :INNER], 1), conv_weight[:, INNER:]], axis=1)
    bias_rel = jnp.concatenate([relative(conv_bias[:INNER], 0), conv_bias[INNER:]], axis=0)
    taps = jnp.concatenate([conv_rel, bias_rel[None, :], jnp.zeros((3, INNER + 2 * NS), f32)], axis=0)
    rate = -jnp.exp(relative(decay_log, 0))
    heads = jnp.zeros((8, LANE), f32)
    heads = heads.at[0, :MH].set(relative(step_bias, 0)).at[1, :MH].set(rate)
    skip = jnp.broadcast_to(jnp.repeat(relative(skip_gain, 0), MP)[None, :], (8, INNER))
    spread = expander()
    spread2 = jnp.concatenate([spread, spread], axis=0)
    gather2 = jnp.concatenate([spread.T, spread.T], axis=0)

    mix, dt, cum, cumt, ec, fw, g, final = mamba_pre(u, taps, meta, dt_raw, heads, spread2)
    decay_all = jnp.prod(g.reshape(chunks, 8, LANE)[:, 0, :], axis=0)[:MH]
    decay_wide = jnp.repeat(decay_all, MP)[None, :]
    final_low = final.astype(bf16)
    state_in = None
    for s in range(hops, 0, -1):
        came = ring.line_heads(final_low, s)
        if s > 1:
            decays_came = ring.line_heads(decay_wide, 1)
            state_in = came.astype(f32) * decays_came
        else:
            state_in = came.astype(f32) if state_in is None else state_in + came.astype(f32)

    attended, lse = attn_fwd(first_block, query8, keys3, vals_t, seg_row, seg_keys[:, None])
    z_gate = dot(normed, w_z)
    gated, full, states = mamba_fwd(
        state_in, mix, dt, cum, cumt, ec, fw, g, seg_col, seg_row, z_gate, skip, spread2
    )
    mixer = dot(attended, w_ao, NT) + dot(gated, w_mo, NT)
    residual = hid + mixer
    scale2 = lax.rsqrt(jnp.mean(residual * residual, axis=-1, keepdims=True) + epsilon)
    normed2 = (residual * scale2 * gain2).astype(bf16)

    gate_lin = dot(normed2, w_fg)
    up_lin = dot(normed2, w_fu)
    sig = jax.nn.sigmoid(gate_lin)
    silu = gate_lin * sig
    activation = (silu * up_lin).astype(bf16)
    output = (residual + dot(activation, w_fd, NT)).astype(bf16)

    d_act = dot(cot, w_fd).astype(bf16).astype(f32)
    d_gate = (d_act * up_lin * (sig * (1.0 + gate_lin * (1.0 - sig)))).astype(bf16)
    d_up = (d_act * silu).astype(bf16)
    d_normed2 = dot(d_gate, w_fg, NT) + dot(d_up, w_fu, NT)
    d_res_norm, ffn_gain_grad = rms_back(d_normed2, residual, scale2, gain2)
    d_residual = cot.astype(f32) + d_res_norm
    d_mixer = d_residual.astype(bf16)

    def scatter(pairs):
        cols = sum(right.shape[1] for _, right in pairs)

        def make(lo, hi):
            half = width // 2
            if hi - lo == 2:
                return jnp.concatenate([dot(l[:, :half], r, TN) for l, r in pairs], axis=1)
            return jnp.concatenate([dot(l[:, half:], r, TN).astype(bf16) for l, r in pairs], axis=1)

        return ring.scatter_dp(make, cols)

    def scatter_both(pairs, widths=None):
        summed = scatter(pairs)
        parts = []
        for s in range(nt):
            at, pieces = 0, []
            for _, right in pairs:
                w = right.shape[1] // nt
                pieces.append(summed[:, at + s * w : at + (s + 1) * w])
                at += right.shape[1]
            parts.append(jnp.concatenate(pieces, axis=1))
        own = ring.scatter_tensor(parts)
        outs, at = [], 0
        for _, right in pairs:
            w = right.shape[1] // nt
            outs.append(own[:, at : at + w])
            at += w
        return outs

    (g_fd,) = scatter_both([(cot, activation)])
    g_fg, g_fu = scatter_both([(normed2, d_gate), (normed2, d_up)])

    d_gated = dot(d_mixer, w_mo).astype(bf16)
    d_attended = dot(d_mixer, w_ao).astype(bf16)
    dy, d_z, back_state = mamba_bpre(d_gated, z_gate, full, mix, ec, g, spread2)
    back_low = back_state.astype(bf16)
    d_state = None
    for s in range(hops, 0, -1):
        came = ring.line_heads(back_low, -s)
        if s > 1:
            decays_came = ring.line_heads(decay_wide, -1)
            d_state = came.astype(f32) * decays_came
        else:
            d_state = came.astype(f32) if d_state is None else d_state + came.astype(f32)
    g_ao, g_mo = scatter_both([(d_mixer, attended), (d_mixer, gated)])

    d_query, dk3, dv3 = attn_bwd(
        first_block, query8, keys3, vals3, d_attended, attended, lse, seg_row, seg_keys[:, None]
    )
    dkv = jnp.concatenate([dk3.transpose(1, 0, 2).reshape(-1, KVH * HD), dv3.transpose(1, 0, 2).reshape(-1, KVH * HD)], axis=1)
    dkv_own = dkv[back:]
    for s in range(1, hops + 1):
        at = back - s * rows
        dkv_own = dkv_own + ring.line(dkv[at : at + rows].astype(bf16), -s).astype(f32)
    d_k = rotate(dkv_own[:, : KVH * HD], cosine, -sine).astype(bf16)
    d_v = dkv_own[:, KVH * HD :].astype(bf16)
    d_q = rotate(d_query.astype(f32), cosine, -sine).astype(bf16)

    d_pre, d_step, conv_grads, small = mamba_bwd(
        d_state, mix, dt, cum, cumt, ec, fw, g, seg_col, seg_row, dy, states, u, taps, meta, skip, heads, spread2, gather2
    )
    after = jnp.concatenate([ring.line_heads(d_pre[:8, :INNER], -1), ring.line(d_pre[:8, INNER:], -1)], axis=1)
    d_ext = jnp.concatenate([d_pre, after], axis=0)
    seg_pad = jnp.concatenate([segment, jnp.full((KCONV,), -2, jnp.int32)])
    d_u = taps[KCONV - 1 : KCONV] * d_pre
    for j in range(1, KCONV):
        same = (lax.dynamic_slice_in_dim(seg_pad, start + j, rows) == seg_own).astype(f32)[:, None]
        d_u = d_u + taps[KCONV - 1 - j : KCONV - j] * d_ext[j : j + rows] * same
    d_u = d_u.astype(bf16)
    d_x, d_bc = d_u[:, :INNER], d_u[:, INNER:]

    d_shared = jnp.concatenate([d_k, d_v, d_bc], axis=1)
    w_shared_in = w_shared
    d_normed = (
        dot(d_q, w_q, NT) + dot(d_z, w_z, NT) + dot(d_x, w_x, NT) + dot(d_shared, w_shared_in, NT) + dot(d_step, w_step, NT)
    )
    d_hid_norm, norm_gain_grad = rms_back(d_normed, hid, scale1, gain1)
    hidden_grad = permute_width(d_residual + d_hid_norm, False)

    d_step4 = jnp.concatenate(
        [jnp.pad(d_step[:, s * step_cols : (s + 1) * step_cols], ((0, 0), (0, LANE - step_cols))) for s in range(nt)], axis=1
    )
    g_q, g_z = scatter_both([(normed, d_q), (normed, d_z)])
    g_x, g_step = scatter_both([(normed, d_x), (normed, d_step4)])
    shared = scatter([(normed, d_shared)])
    piece = block // nt
    shared_parts = [
        lax.dynamic_slice_in_dim(shared, lax.rem(ti + nt - s, nt) * piece, piece, 0) for s in range(nt)
    ]
    g_shared = ring.scatter_tensor(shared_parts)

    conv_flat = jnp.concatenate([relative(conv_grads[: KCONV + 1, :INNER], 1), conv_grads[: KCONV + 1, INNER:]], axis=1)
    small_flat = relative(small[:3, :MH], 1)
    vector = jnp.concatenate(
        [permute_width(norm_gain_grad, False), permute_width(ffn_gain_grad, False), conv_flat.reshape(-1), small_flat.reshape(-1)]
    )
    size = vector.shape[0]
    padded_size = -(-size // 1024) * 1024
    vector = ring.all_sum(jnp.pad(vector, (0, padded_size - size)).reshape(-1, LANE)).reshape(-1)
    at = 2 * width
    conv_sum = vector[at : at + conv_flat.size].reshape(conv_flat.shape)
    at += conv_flat.size
    small_sum = vector[at : at + 3 * MH].reshape(3, MH)
    return (
        output_back(permute_width, output),
        hidden_grad,
        vector[:width],
        vector[width : 2 * width],
        g_q,
        g_shared[:, : KVH * HD],
        g_shared[:, KVH * HD : 2 * KVH * HD],
        g_ao.T,
        g_z,
        g_x,
        g_shared[:, 2 * KVH * HD :],
        g_step[:, :step_cols],
        g_mo.T,
        conv_sum[:KCONV],
        conv_sum[KCONV],
        small_sum[0],
        small_sum[1],
        small_sum[2],
        g_fg,
        g_fu,
        g_fd.T,
    )


def output_back(permute, output):
    return permute(output, False)


def solution(mesh):
    in_specs = (
        P(("dp", "tensor"), None),
        P("dp", None),
        P(("dp", "tensor"), None),
        P(),
        P(),
        P("dp", "tensor"),
        P("dp", None),
        P("dp", None),
        P("tensor", "dp"),
        P("dp", "tensor"),
        P("dp", "tensor"),
        P("dp", None),
        P("dp", "tensor"),
        P("tensor", "dp"),
        P(),
        P(),
        P(),
        P(),
        P(),
        P("dp", "tensor"),
        P("dp", "tensor"),
        P("tensor", "dp"),
    )
    out_specs = (
        P(("dp", "tensor"), None),
        P(("dp", "tensor"), None),
        P(),
        P(),
        P("dp", "tensor"),
        P(("dp", "tensor"), None),
        P(("dp", "tensor"), None),
        P("tensor", "dp"),
        P("dp", "tensor"),
        P("dp", "tensor"),
        P(("dp", "tensor"), None),
        P("dp", "tensor"),
        P("tensor", "dp"),
        P(),
        P(),
        P(),
        P(),
        P(),
        P("dp", "tensor"),
        P("dp", "tensor"),
        P("tensor", "dp"),
    )
    return jax.shard_map(
        functools.partial(per_device, mesh), mesh=mesh, in_specs=in_specs, out_specs=out_specs, check_vma=False
    )
```

time: 2710 us -> 818 us (0.30)
  waiting for transfers between devices: 1040 us -> 243 us
  local copies, waits for them, and re-layouts: 599 us -> 128 us
  matrix products: 549 us -> 88 us
  other arithmetic: 321 us -> 170 us
  blocking collectives: 134 us -> 0 us
  starting transfers between devices: 1.87 us -> 111 us
  Pallas kernels: 0 us -> 54.4 us
    reduce_scatter x17 -> x0, waiting for transfers between devices: 871 us -> none  [the longest x1 137 us: per_device(): lax.psum_scatter(mixer_grads[2], ('dp', 'tensor'), scatter_dimension=0, t...]
    dot_general x296 -> x41, matrix products: 457 us -> 88 us  [dot(): return lax.dot_general(a, b, dims, preferred_element_type=f32)]
    dynamic_update_slice x52 -> x0, local copies, waits for them, and re-layouts: 300 us -> none  [the longest x48 294 us: state_scan(): final_state, outputs = lax.scan(jax.checkpoint(advance), initial, elements)]
    ppermute x0 -> x104, waiting for transfers between devices: none -> 243 us  [the longest x58 164 us: dp(): return lax.ppermute(value, 'dp', [(i, i ^ bit) for i in range(self.nd)])]
    all_gather x8 -> x0, waiting for transfers between devices: 162 us -> none  [the longest x1 79.4 us: per_device(): lax.all_gather(ffn_w[1], 'tensor', axis=1, tiled=True)]
    concatenate x4 -> x65, other arithmetic: 0.65 us -> 138 us  [the longest x5 58.1 us: gather_dp(): return jnp.concatenate([low, self.dp(low, last)], axis=0)]
    ppermute x0 -> x104, starting transfers between devices: none -> 111 us  [the longest x33 48.8 us: shift(): return lax.ppermute(value, 'tensor', [(i, (i + s) % n) for i in range(n)])]
    squeeze x212 -> x1, local copies, waits for them, and re-layouts: 107 us -> 0.6 us  [per_device(): conv_sum[KCONV]]
  transfers between devices with their start and end apart: 25 -> 104, of which waited for: 16 -> 41; matrix products, arithmetic and copies ran while one was open for 54% -> 40% of each run, Pallas kernels for 0% -> 6%
where the time goes in v1:
time: 818 us; the launch traced here: 805 us
  waiting for transfers between devices  243 us (30%)
  other arithmetic  170 us (21%)
  local copies, waits for them, and re-layouts  128 us (16%)
  starting transfers between devices  111 us (14%)
  matrix products  88 us (11%)
  Pallas kernels  54.4 us (7%)
  between operations  10.7 us (1%)
    ppermute x58, waiting for transfers between devices, dp(): return lax.ppermute(value, 'dp', [(i, i ^ bit) for i in range(self.nd)])  164 us
    dot_general x41, matrix products, dot(): return lax.dot_general(a, b, dims, preferred_element_type=f32)  88 us
    unnamed x564, local copies, waits for them, and re-layouts  67.8 us
    concatenate x5, other arithmetic, gather_dp(): return jnp.concatenate([low, self.dp(low, last)], axis=0)  58.1 us
    ppermute x33, waiting for transfers between devices, shift(): return lax.ppermute(value, 'tensor', [(i, (i + s) % n) for i in range(n)])  53.3 us
    concatenate x5, other arithmetic, gather_dp(): jnp.concatenate([jnp.concatenate(side, axis=0) for side in sides], axis=1)  52.3 us
    ppermute x33, starting transfers between devices, shift(): return lax.ppermute(value, 'tensor', [(i, (i + s) % n) for i in range(n)])  48.8 us
    ppermute x58, starting transfers between devices, dp(): return lax.ppermute(value, 'dp', [(i, i ^ bit) for i in range(self.nd)])  37.9 us
  transfers between devices with their start and end apart: 104, of which 41 were waited for; matrix products, arithmetic and copies ran while one was open for 40% of the time, Pallas kernels for 6%

profile of v1, /device:TPU:0, one launch (start us, length us, event | category | flops | bytes accessed | tf_op | source)
XLA Modules:
  0.0 805.1 jit_solution(7147449173954180259)
XLA Ops:
  4.0 5.0 collective-permute-start.2
  87.0 3.7 collective-permute-done.38
  92.7 6.8 collective-permute-done.35
  119.1 4.4 collective-permute-done.9
  126.3 3.8 collective-permute-start.23
  133.4 6.3 collective-permute-done.28
  142.9 7.4 collective-permute-done.5
  153.2 6.9 collective-permute-done.20
  176.6 9.6 %collective-permute-done.41 = bf16[256,1024]{0,1:T(8,128)(2,1)S(1)} collective-permute-done((bf16[256,1024]{0,1:T(8,128)(2,1)S(1)}, bf16[256,1024]{0,1:T(8,128)(2,1)S(1)}, u32[]{:S(2)}, u32[]{:S(2)}) %collective-permute-start.41) | collective-permute-done | bytes 524320 | tf_op jit(solution)/shard_map/ppermute | solution.py:526
  190.0 8.2 %maximum_maximum_fusion.4 = bf16[512,2048]{0,1:T(8,128)(2,1)} fusion(bf16[128,1024]{0,1:T(8,128)(2,1)S(1)} %get-tuple-element.279, bf16[128,1024]{0,1:T(8,128)(2,1)S(1)} %collective-permute-done.40, bf16[128,1024]{0,1:T(8,128)(2,1)S(1)} %get-tuple-element.278, bf16[128,1024]{0,1:T(8,128)(2,1)S(1)} %constant_dynamic-update-slice_fusion.41, ...), kind=kLoop, calls=%fused_computation.78 | loop fusion | flops 16777216 | bytes 4194304 | tf_op jit(solution)/shard_map/concatenate | solution.py:549
  207.5 6.6 maximum_maximum_fusion.3
  214.1 5.9 collective-permute-done.21
  221.9 11.1 %maximum_maximum_fusion.2 = bf16[512,3584]{0,1:T(8,128)(2,1)} fusion(bf16[128,1792]{0,1:T(8,128)(2,1)S(1)} %get-tuple-element.256, bf16[128,1792]{0,1:T(8,128)(2,1)S(1)} %copy-done.66, bf16[128,1792]{0,1:T(8,128)(2,1)S(1)} %get-tuple-element.255, bf16[128,1792]{0,1:T(8,128)(2,1)S(1)} %copy-done.62, bf16[256,1792]{0,1:T(8,128)(2,1)S(1)} %collective-permute-done.19, ...), kind=kLoop, calls=%fused_computation.48 | loop fusion | flops 25690112 | bytes 7340032 | tf_op jit(solution)/shard_map/concatenate | solution.py:549
  233.1 6.6 collective-permute-done.33
  241.2 25.5 %maximum_maximum_fusion = bf16[512,4096]{1,0:T(8,128)(2,1)} fusion(bf16[128,2048]{1,0:T(8,128)(2,1)S(1)} %get-tuple-element.254, bf16[128,2048]{1,0:T(8,128)(2,1)S(1)} %copy-done.82, bf16[128,2048]{1,0:T(8,128)(2,1)S(1)} %get-tuple-element.253, bf16[128,512]{1,0:T(8,128)(2,1)S(1)} %copy-done.116, bf16[128,512]{1,0:T(8,128)(2,1)S(1)} %copy-done.122, ...), kind=kLoop, calls=%fused_computation.15 | loop fusion | flops 54525952 | bytes 8388608 | tf_op jit(solution)/shard_map/concatenate | solution.py:549
  266.9 11.8 %pad_maximum_fusion.2 = bf16[1024,2048]{0,1:T(8,128)(2,1)S(1)} fusion(bf16[512,2048]{0,1:T(8,128)(2,1)S(1)} %collective-permute-done.42, bf16[128,1024]{0,1:T(8,128)(2,1)S(1)} %copy-done.144, bf16[128,1024]{0,1:T(8,128)(2,1)S(1)} %copy-done.138, bf16[128,1024]{0,1:T(8,128)(2,1)S(1)} %copy-done.142, bf16[128,1024]{0,1:T(8,128)(2,1)S(1)} %copy-done.132, ...), kind=kLoop, calls=%fused_computation.16 | loop fusion | flops 37748736 | bytes 8388608 | tf_op jit(solution)/shard_map/concatenate | solution.py:550
  278.7 5.9 convolution_convert_fusion.3
  286.5 10.0 %pad_maximum_fusion.1 = bf16[1024,2560]{0,1:T(8,128)(2,1)S(1)} fusion(bf16[512,2560]{0,1:T(8,128)(2,1)S(1)} %collective-permute-done.7, bf16[128,1280]{0,1:T(8,128)(2,1)S(1)} %get-tuple-element.263, bf16[128,1280]{0,1:T(8,128)(2,1)S(1)} %copy-done.78, bf16[128,1280]{0,1:T(8,128)(2,1)S(1)} %get-tuple-element.262, bf16[128,1280]{0,1:T(8,128)(2,1)S(1)} %copy-done.57, ...), kind=kLoop, calls=%fused_computation.5 | loop fusion | flops 41943040 | bytes 10485760 | tf_op jit(solution)/shard_map/concatenate | solution.py:550
  299.2 5.8 mamba_pre.1
  325.5 6.3 attn_fwd.1
  339.7 14.2 %pad_maximum_fusion.5 = (bf16[1024,1536]{0,1:T(8,128)(2,1)}, bf16[1024,1536]{0,1:T(8,128)(2,1)S(1)}) fusion(bf16[512,3584]{0,1:T(8,128)(2,1)} %collective-permute-done.22, bf16[128,1792]{0,1:T(8,128)(2,1)S(1)} %copy-done.74, bf16[256,1792]{0,1:T(8,128)(2,1)S(1)} %copy-done.55, bf16[128,1792]{0,1:T(8,128)(2,1)S(1)} %copy-done.67, ...), kind=kLoop, calls=%fused_computation.49 | loop fusion | flops 50331648 | bytes 13631488 | tf_op jit(solution)/shard_map/concatenate | solution.py:550
  356.3 6.2 mamba_fwd.1
  368.6 21.1 %pad_maximum_fusion = bf16[1024,4096]{1,0:T(8,128)(2,1)S(1)} fusion(bf16[512,4096]{1,0:T(8,128)(2,1)} %collective-permute-done.34, bf16[128,2048]{1,0:T(8,128)(2,1)S(1)} %copy-done.90, bf16[128,2048]{1,0:T(8,128)(2,1)S(1)} %copy-done.83, bf16[128,2048]{1,0:T(8,128)(2,1)S(1)} %copy-done.88, bf16[128,512]{1,0:T(8,128)(2,1)S(1)} %copy-done.117, ...), kind=kLoop, calls=%fused_computation | loop fusion | flops 117440512 | bytes 16777216 | tf_op jit(solution)/shard_map/concatenate | solution.py:550
  389.8 4.3 fusion.14
  394.1 6.9 fusion.2
  425.2 8.4 %attn_bwd.1 = (bf16[512,512]{1,0:T(8,128)(2,1)S(1)}, f32[2,1536,64]{2,1,0:T(8,128)S(1)}, f32[2,1536,64]{2,1,0:T(8,128)S(1)}) custom-call(s32[8]{0:T(128)S(1)} %concatenate.420.first_ref, bf16[512,512]{1,0:T(8,128)(2,1)S(1)} %copy-done.15, bf16[2,1536,64]{2,1,0:T(8,128)(2,1)S(1)} %bitcast.121, bf16[2,1536,64]{2,1,0:T(8,128)(2,1)S(1)} %bitcast.122, ...), custom_call_target="tpu_custom_call" | custom-call | flops 10000000000 | bytes 8000000 | tf_op jit(solution)/shard_map/attn_bwd/pallas_call | solution.py:176
  437.5 3.4 fusion.49
  490.6 16.6 %collective-permute-done.49 = bf16[512,256]{1,0:T(8,128)(2,1)S(1)} collective-permute-done((bf16[512,256]{1,0:T(8,128)(2,1)S(1)}, bf16[512,256]{1,0:T(8,128)(2,1)S(1)}, u32[]{:S(2)}, u32[]{:S(2)}) %collective-permute-start.49) | collective-permute-done | bytes 262176 | tf_op jit(solution)/shard_map/ppermute | solution.py:534
  511.6 24.5 %mamba_bwd.1 = (f32[512,1792]{1,0:T(8,128)}, bf16[512,128]{1,0:T(8,128)(2,1)}, f32[8,1792]{1,0:T(8,128)}, f32[8,128]{1,0:T(8,128)}) custom-call(f32[128,1536]{1,0:T(8,128)} %convert_add_fusion.1.init_ref, bf16[512,1792]{1,0:T(8,128)(2,1)} %copy-done.2, f32[512,128]{1,0:T(8,128)} %copy-done.27, f32[512,128]{1,0:T(8,128)} %copy-done.29, f32[32,512]{1,0:T(8,128)} %copy-done.33, ...), custom_call_target="tpu_custom_call" | custom-call | flops 6000000000 | bytes 16000000 | tf_op jit(solution)/shard_map/mamba_bwd/pallas_call | solution.py:490
  544.0 8.8 %collective-permute-done.46 = f32[8,1536]{1,0:T(8,128)S(1)} collective-permute-done((f32[8,1536]{1,0:T(8,128)S(1)}, f32[8,1536]{1,0:T(8,128)S(1)}, u32[]{:S(2)}, u32[]{:S(2)}) %collective-permute-start.46) | collective-permute-done | bytes 49184 | tf_op jit(solution)/shard_map/ppermute | solution.py:534
  598.9 3.7 collective-permute-done.66
  628.4 3.6 collective-permute-done.57
  632.0 11.2 %collective-permute-done.73 = bf16[256,1024]{1,0:T(8,128)(2,1)S(1)} collective-permute-done((bf16[256,1024]{1,0:T(8,128)(2,1)S(1)}, bf16[256,1024]{1,0:T(8,128)(2,1)S(1)}, u32[]{:S(2)}, u32[]{:S(2)}) %collective-permute-start.73) | collective-permute-done | bytes 524320 | tf_op jit(solution)/shard_map/ppermute | solution.py:526
  643.3 10.8 %collective-permute-done.97 = bf16[256,1024]{1,0:T(8,128)(2,1)S(1)} collective-permute-done((bf16[256,1024]{1,0:T(8,128)(2,1)S(1)}, bf16[256,1024]{1,0:T(8,128)(2,1)S(1)}, u32[]{:S(2)}, u32[]{:S(2)}) %collective-permute-start.97) | collective-permute-done | bytes 524320 | tf_op jit(solution)/shard_map/ppermute | solution.py:526
  657.6 16.9 %collective-permute-done.74 = bf16[128,1024]{1,0:T(8,128)(2,1)S(1)} collective-permute-done((bf16[128,1024]{1,0:T(8,128)(2,1)S(1)}, bf16[128,1024]{1,0:T(8,128)(2,1)S(1)}, u32[]{:S(2)}, u32[]{:S(2)}) %collective-permute-start.74) | collective-permute-done | bytes 262176 | tf_op jit(solution)/shard_map/ppermute | solution.py:526
  675.9 14.1 %collective-permute-done.98 = bf16[128,1024]{1,0:T(8,128)(2,1)S(1)} collective-permute-done((bf16[128,1024]{1,0:T(8,128)(2,1)S(1)}, bf16[128,1024]{1,0:T(8,128)(2,1)S(1)}, u32[]{:S(2)}, u32[]{:S(2)}) %collective-permute-start.98) | collective-permute-done | bytes 262176 | tf_op jit(solution)/shard_map/ppermute | solution.py:526
  692.8 6.5 collective-permute-done.76
  706.4 5.1 collective-permute-done.61
  714.2 3.5 collective-permute-done.78
  717.6 4.7 collective-permute-start.103
  725.9 3.4 collective-permute-done.103
  729.3 4.1 collective-permute-done.102
  737.5 23.4 %collective-permute-done.89 = bf16[256,2048]{1,0:T(8,128)(2,1)S(1)} collective-permute-done((bf16[256,2048]{1,0:T(8,128)(2,1)S(1)}, bf16[256,2048]{1,0:T(8,128)(2,1)S(1)}, u32[]{:S(2)}, u32[]{:S(2)}) %collective-permute-start.89) | collective-permute-done | bytes 1048608 | tf_op jit(solution)/shard_map/ppermute | solution.py:526
  764.6 7.5 collective-permute-done.90
  773.9 3.9 collective-permute-start.85
  777.8 4.9 collective-permute-done.92
  783.2 3.9 collective-permute-start.93
  794.0 9.7 %collective-permute-done.94 = bf16[128,1024]{1,0:T(8,128)(2,1)S(1)} collective-permute-done((bf16[128,1024]{1,0:T(8,128)(2,1)S(1)}, bf16[128,1024]{1,0:T(8,128)(2,1)S(1)}, u32[]{:S(2)}, u32[]{:S(2)}) %collective-permute-start.94) | collective-permute-done | bytes 262176 | tf_op jit(solution)/shard_map/ppermute | solution.py:530
  (1042 shorter events, 381.5 us)
Async XLA Ops:
  4.0 102.7 %collective-permute-start.2 = (bf16[128,640]{0,1:T(8,128)(2,1)}, bf16[128,640]{0,1:T(8,128)(2,1)}, u32[]{:S(2)}, u32[]{:S(2)}) collective-permute-start(bf16[128,640]{0,1:T(8,128)(2,1)} %pad_maximum_fusion.47), channel_id=1, source_target_pairs={{0,3},{1,0},{2,1},{3,2},{4,7},{5,4},{6,5},{7,6},{8,11},{9,8},{10,9... | collective-permute-start | bytes 491528 | tf_op jit(solution)/shard_map/ppermute | solution.py:530
  9.0 93.9 %collective-permute-start.1 = (bf16[128,640]{0,1:T(8,128)(2,1)}, bf16[128,640]{0,1:T(8,128)(2,1)}, u32[]{:S(2)}, u32[]{:S(2)}) collective-permute-start(bf16[128,640]{0,1:T(8,128)(2,1)} %pad_maximum_fusion.47), channel_id=1, source_target_pairs={{0,2},{1,3},{2,0},{3,1},{4,6},{5,7},{6,4},{7,5},{8,10},{9,11},{10,... | collective-permute-start | bytes 491528 | tf_op jit(solution)/shard_map/ppermute | solution.py:530
  9.0 90.5 %collective-permute-start = (bf16[128,640]{0,1:T(8,128)(2,1)}, bf16[128,640]{0,1:T(8,128)(2,1)}, u32[]{:S(2)}, u32[]{:S(2)}) collective-permute-start(bf16[128,640]{0,1:T(8,128)(2,1)} %pad_maximum_fusion.47), channel_id=1, source_target_pairs={{0,1},{1,2},{2,3},{3,0},{4,5},{5,6},{6,7},{7,4},{8,9},{9,10},{10,1... | collective-permute-start | bytes 491528 | tf_op jit(solution)/shard_map/ppermute | solution.py:530
  10.0 71.1 %collective-permute-start.10 = (bf16[128,256]{1,0:T(8,128)(2,1)}, bf16[128,256]{1,0:T(8,128)(2,1)S(1)}, u32[]{:S(2)}, u32[]{:S(2)}) collective-permute-start(bf16[128,256]{1,0:T(8,128)(2,1)} %param.69), channel_id=1, source_target_pairs={{0,16},{4,20},{8,24},{12,28},{16,0},{20,4},{24,8},{28,12},{1,17},{... | collective-permute-start | bytes 196616 | tf_op jit(solution)/shard_map/ppermute | solution.py:526
  13.1 70.1 %collective-permute-start.8 = (bf16[128,256]{1,0:T(8,128)(2,1)S(1)}, bf16[128,256]{1,0:T(8,128)(2,1)}, u32[]{:S(2)}, u32[]{:S(2)}) collective-permute-start(bf16[128,256]{1,0:T(8,128)(2,1)S(1)} %constant_dynamic-update-slice_fusion.18), channel_id=1, source_target_pairs={{0,8},{4,12},{8,0},{12,4},{16,24},{20,28},{24,16},{28,20},{1,9},{5... | collective-permute-start | bytes 196616 | tf_op jit(solution)/shard_map/ppermute | solution.py:526
  92.2 38.9 %collective-permute-start.15 = (bf16[128,896]{0,1:T(8,128)(2,1)}, bf16[128,896]{0,1:T(8,128)(2,1)S(1)}, u32[]{:S(2)}, u32[]{:S(2)}) collective-permute-start(bf16[128,896]{0,1:T(8,128)(2,1)} %pad_maximum_fusion.46), channel_id=1, source_target_pairs={{0,1},{1,2},{2,3},{3,0},{4,5},{5,6},{6,7},{7,4},{8,9},{9,10},{10,1... | collective-permute-start | bytes 688136 | tf_op jit(solution)/shard_map/ppermute | solution.py:530
  99.4 25.1 %collective-permute-start.16 = (bf16[128,896]{0,1:T(8,128)(2,1)}, bf16[128,896]{0,1:T(8,128)(2,1)S(1)}, u32[]{:S(2)}, u32[]{:S(2)}) collective-permute-start(bf16[128,896]{0,1:T(8,128)(2,1)} %pad_maximum_fusion.46), channel_id=1, source_target_pairs={{0,2},{1,3},{2,0},{3,1},{4,6},{5,7},{6,4},{7,5},{8,10},{9,11},{10,... | collective-permute-start | bytes 688136 | tf_op jit(solution)/shard_map/ppermute | solution.py:530
  99.5 26.7 %collective-permute-start.17 = (bf16[128,896]{0,1:T(8,128)(2,1)}, bf16[128,896]{0,1:T(8,128)(2,1)S(1)}, u32[]{:S(2)}, u32[]{:S(2)}) collective-permute-start(bf16[128,896]{0,1:T(8,128)(2,1)} %pad_maximum_fusion.46), channel_id=1, source_target_pairs={{0,3},{1,0},{2,1},{3,2},{4,7},{5,4},{6,5},{7,6},{8,11},{9,8},{10,9... | collective-permute-start | bytes 688136 | tf_op jit(solution)/shard_map/ppermute | solution.py:530
  102.9 28.9 %collective-permute-start.29 = (bf16[128,1024]{1,0:T(8,128)(2,1)}, bf16[128,1024]{1,0:T(8,128)(2,1)S(1)}, u32[]{:S(2)}, u32[]{:S(2)}) collective-permute-start(bf16[128,1024]{1,0:T(8,128)(2,1)} %constant_dynamic-update-slice_fusion.39), channel_id=1, source_target_pairs={{0,3},{1,0},{2,1},{3,2},{4,7},{5,4},{6,5},{7,6},{8,11},{9,8},{10,9... | collective-permute-start | bytes 786440 | tf_op jit(solution)/shard_map/ppermute | solution.py:530
  126.3 40.0 %collective-permute-start.23 = (bf16[16,1024]{1,0:T(8,128)(2,1)}, bf16[16,1024]{1,0:T(8,128)(2,1)S(1)}, u32[]{:S(2)}, u32[]{:S(2)}) collective-permute-start(bf16[16,1024]{1,0:T(8,128)(2,1)} %slice.1185), channel_id=1, source_target_pairs={{0,1},{1,2},{2,3},{4,5},{5,6},{6,7},{8,9},{9,10},{10,11},{12,13},{... | collective-permute-start | bytes 98312 | tf_op jit(solution)/shard_map/ppermute | solution.py:534
  141.0 23.2 %collective-permute-start.12 = (bf16[512,512]{1,0:T(8,128)(2,1)S(1)}, bf16[512,512]{1,0:T(8,128)(2,1)S(1)}, u32[]{:S(2)}, u32[]{:S(2)}) collective-permute-start(bf16[512,512]{1,0:T(8,128)(2,1)S(1)} %maximum_maximum_fusion.6), channel_id=1, source_target_pairs={{0,4},{4,0},{8,12},{12,8},{16,20},{20,16},{24,28},{28,24},{1,5},{5... | collective-permute-start | bytes 1572872 | tf_op jit(solution)/shard_map/ppermute | solution.py:526
  141.2 18.9 %collective-permute-start.20 = (bf16[128,1792]{0,1:T(8,128)(2,1)S(1)}, bf16[128,1792]{0,1:T(8,128)(2,1)S(1)}, u32[]{:S(2)}, u32[]{:S(2)}) collective-permute-start(bf16[128,1792]{0,1:T(8,128)(2,1)S(1)} %get-tuple-element.315), channel_id=1, source_target_pairs={{0,16},{4,20},{8,24},{12,28},{16,0},{20,4},{24,8},{28,12},{1,17},{... | collective-permute-start | bytes 1376264 | tf_op jit(solution)/shard_map/ppermute | solution.py:526
  151.7 19.6 %collective-permute-start.32 = (bf16[128,2048]{1,0:T(8,128)(2,1)S(1)}, bf16[128,2048]{1,0:T(8,128)(2,1)S(1)}, u32[]{:S(2)}, u32[]{:S(2)}) collective-permute-start(bf16[128,2048]{1,0:T(8,128)(2,1)S(1)} %pad_maximum_fusion.29), channel_id=1, source_target_pairs={{0,16},{4,20},{8,24},{12,28},{16,0},{20,4},{24,8},{28,12},{1,17},{... | collective-permute-start | bytes 1572872 | tf_op jit(solution)/shard_map/ppermute | solution.py:526
  161.7 24.5 %collective-permute-start.41 = (bf16[256,1024]{0,1:T(8,128)(2,1)S(1)}, bf16[256,1024]{0,1:T(8,128)(2,1)S(1)}, u32[]{:S(2)}, u32[]{:S(2)}) collective-permute-start(bf16[256,1024]{0,1:T(8,128)(2,1)S(1)} %pad_maximum_fusion.31), channel_id=1, source_target_pairs={{0,8},{4,12},{8,0},{12,4},{16,24},{20,28},{24,16},{28,20},{1,9},{5... | collective-permute-start | bytes 1572872 | tf_op jit(solution)/shard_map/ppermute | solution.py:526
  164.3 23.3 %collective-permute-start.37 = (bf16[256,1024]{0,1:T(8,128)(2,1)S(1)}, bf16[256,1024]{0,1:T(8,128)(2,1)S(1)}, u32[]{:S(2)}, u32[]{:S(2)}) collective-permute-start(bf16[256,1024]{0,1:T(8,128)(2,1)S(1)} %pad_maximum_fusion.30), channel_id=1, source_target_pairs={{0,16},{4,20},{8,24},{12,28},{16,0},{20,4},{24,8},{28,12},{1,17},{... | collective-permute-start | bytes 1572872 | tf_op jit(solution)/shard_map/ppermute | solution.py:526
  166.3 38.5 %collective-permute-start.6 = (bf16[256,1280]{0,1:T(8,128)(2,1)}, bf16[256,1280]{0,1:T(8,128)(2,1)}, u32[]{:S(2)}, u32[]{:S(2)}) collective-permute-start(bf16[256,1280]{0,1:T(8,128)(2,1)} %pad_maximum_fusion.27), channel_id=1, source_target_pairs={{0,8},{4,12},{8,0},{12,4},{16,24},{20,28},{24,16},{28,20},{1,9},{5... | collective-permute-start | bytes 1966088 | tf_op jit(solution)/shard_map/ppermute | solution.py:526
  171.3 36.1 %collective-permute-start.4 = (bf16[256,1280]{0,1:T(8,128)(2,1)}, bf16[256,1280]{0,1:T(8,128)(2,1)}, u32[]{:S(2)}, u32[]{:S(2)}) collective-permute-start(bf16[256,1280]{0,1:T(8,128)(2,1)} %pad_maximum_fusion.26), channel_id=1, source_target_pairs={{0,16},{4,20},{8,24},{12,28},{16,0},{20,4},{24,8},{28,12},{1,17},{... | collective-permute-start | bytes 1966088 | tf_op jit(solution)/shard_map/ppermute | solution.py:526
  175.0 45.0 %collective-permute-start.21 = (bf16[256,1792]{0,1:T(8,128)(2,1)}, bf16[256,1792]{0,1:T(8,128)(2,1)}, u32[]{:S(2)}, u32[]{:S(2)}) collective-permute-start(bf16[256,1792]{0,1:T(8,128)(2,1)} %pad_maximum_fusion.23), channel_id=1, source_target_pairs={{0,8},{4,12},{8,0},{12,4},{16,24},{20,28},{24,16},{28,20},{1,9},{5... | collective-permute-start | bytes 2752520 | tf_op jit(solution)/shard_map/ppermute | solution.py:526
  198.2 23.6 %collective-permute-start.19 = (bf16[256,1792]{0,1:T(8,128)(2,1)}, bf16[256,1792]{0,1:T(8,128)(2,1)S(1)}, u32[]{:S(2)}, u32[]{:S(2)}) collective-permute-start(bf16[256,1792]{0,1:T(8,128)(2,1)} %pad_maximum_fusion.22), channel_id=1, source_target_pairs={{0,16},{4,20},{8,24},{12,28},{16,0},{20,4},{24,8},{28,12},{1,17},{... | collective-permute-start | bytes 2752520 | tf_op jit(solution)/shard_map/ppermute | solution.py:526
  198.8 41.0 %collective-permute-start.33 = (bf16[256,2048]{1,0:T(8,128)(2,1)}, bf16[256,2048]{1,0:T(8,128)(2,1)}, u32[]{:S(2)}, u32[]{:S(2)}) collective-permute-start(bf16[256,2048]{1,0:T(8,128)(2,1)} %pad_maximum_fusion.20), channel_id=1, source_target_pairs={{0,8},{4,12},{8,0},{12,4},{16,24},{20,28},{24,16},{28,20},{1,9},{5... | collective-permute-start | bytes 3145736 | tf_op jit(solution)/shard_map/ppermute | solution.py:526
  204.8 36.3 %collective-permute-start.31 = (bf16[256,2048]{1,0:T(8,128)(2,1)}, bf16[256,2048]{1,0:T(8,128)(2,1)S(1)}, u32[]{:S(2)}, u32[]{:S(2)}) collective-permute-start(bf16[256,2048]{1,0:T(8,128)(2,1)} %pad_maximum_fusion.19), channel_id=1, source_target_pairs={{0,16},{4,20},{8,24},{12,28},{16,0},{20,4},{24,8},{28,12},{1,17},{... | collective-permute-start | bytes 3145736 | tf_op jit(solution)/shard_map/ppermute | solution.py:526
  207.4 59.4 %collective-permute-start.42 = (bf16[512,2048]{0,1:T(8,128)(2,1)}, bf16[512,2048]{0,1:T(8,128)(2,1)S(1)}, u32[]{:S(2)}, u32[]{:S(2)}) collective-permute-start(bf16[512,2048]{0,1:T(8,128)(2,1)} %maximum_maximum_fusion.4), channel_id=1, source_target_pairs={{0,4},{4,0},{8,12},{12,8},{16,20},{20,16},{24,28},{28,24},{1,5},{5... | collective-permute-start | bytes 6291464 | tf_op jit(solution)/shard_map/ppermute | solution.py:526
  220.1 64.5 %collective-permute-start.7 = (bf16[512,2560]{0,1:T(8,128)(2,1)S(1)}, bf16[512,2560]{0,1:T(8,128)(2,1)S(1)}, u32[]{:S(2)}, u32[]{:S(2)}) collective-permute-start(bf16[512,2560]{0,1:T(8,128)(2,1)S(1)} %maximum_maximum_fusion.3), channel_id=1, source_target_pairs={{0,4},{4,0},{8,12},{12,8},{16,20},{20,16},{24,28},{28,24},{1,5},{5... | collective-permute-start | bytes 7864328 | tf_op jit(solution)/shard_map/ppermute | solution.py:526
  233.0 105.5 %collective-permute-start.22 = (bf16[512,3584]{0,1:T(8,128)(2,1)}, bf16[512,3584]{0,1:T(8,128)(2,1)}, u32[]{:S(2)}, u32[]{:S(2)}) collective-permute-start(bf16[512,3584]{0,1:T(8,128)(2,1)} %maximum_maximum_fusion.2), channel_id=1, source_target_pairs={{0,4},{4,0},{8,12},{12,8},{16,20},{20,16},{24,28},{28,24},{1,5},{5... | collective-permute-start | bytes 11010056 | tf_op jit(solution)/shard_map/ppermute | solution.py:526
  309.3 28.0 %collective-permute-start.24 = (bf16[128,1536]{1,0:T(8,128)(2,1)}, bf16[128,1536]{1,0:T(8,128)(2,1)}, u32[]{:S(2)}, u32[]{:S(2)}) collective-permute-start(bf16[128,1536]{1,0:T(8,128)(2,1)} %convert_element_type.592), channel_id=1, source_target_pairs={{0,2},{1,3},{4,6},{5,7},{8,10},{9,11},{12,14},{13,15},{16,18},{17,... | collective-permute-start | bytes 1179656 | tf_op jit(solution)/shard_map/ppermute | solution.py:534
  311.5 23.9 %collective-permute-start.26 = (bf16[128,1536]{1,0:T(8,128)(2,1)}, bf16[128,1536]{1,0:T(8,128)(2,1)}, u32[]{:S(2)}, u32[]{:S(2)}) collective-permute-start(bf16[128,1536]{1,0:T(8,128)(2,1)} %convert_element_type.592), channel_id=1, source_target_pairs={{0,1},{1,2},{2,3},{4,5},{5,6},{6,7},{8,9},{9,10},{10,11},{12,13},{... | collective-permute-start | bytes 1179656 | tf_op jit(solution)/shard_map/ppermute | solution.py:534
  331.9 34.1 %collective-permute-start.34 = (bf16[512,4096]{1,0:T(8,128)(2,1)S(1)}, bf16[512,4096]{1,0:T(8,128)(2,1)}, u32[]{:S(2)}, u32[]{:S(2)}) collective-permute-start(bf16[512,4096]{1,0:T(8,128)(2,1)S(1)} %copy-done.93), channel_id=1, source_target_pairs={{0,4},{4,0},{8,12},{12,8},{16,20},{20,16},{24,28},{28,24},{1,5},{5... | collective-permute-start | bytes 12582920 | tf_op jit(solution)/shard_map/ppermute | solution.py:526
  415.6 94.0 %collective-permute-start.43 = (bf16[128,1536]{1,0:T(8,128)(2,1)}, bf16[128,1536]{1,0:T(8,128)(2,1)}, u32[]{:S(2)}, u32[]{:S(2)}) collective-permute-start(bf16[128,1536]{1,0:T(8,128)(2,1)} %convert_element_type.607), channel_id=1, source_target_pairs={{2,0},{3,1},{6,4},{7,5},{10,8},{11,9},{14,12},{15,13},{18,16},{19,... | collective-permute-start | bytes 1179656 | tf_op jit(solution)/shard_map/ppermute | solution.py:534
  417.1 90.5 %collective-permute-start.45 = (bf16[128,1536]{1,0:T(8,128)(2,1)}, bf16[128,1536]{1,0:T(8,128)(2,1)}, u32[]{:S(2)}, u32[]{:S(2)}) collective-permute-start(bf16[128,1536]{1,0:T(8,128)(2,1)} %convert_element_type.607), channel_id=1, source_target_pairs={{1,0},{2,1},{3,2},{5,4},{6,5},{7,6},{9,8},{10,9},{11,10},{13,12},{... | collective-permute-start | bytes 1179656 | tf_op jit(solution)/shard_map/ppermute | solution.py:534
  476.0 31.2 %collective-permute-start.49 = (bf16[512,256]{1,0:T(8,128)(2,1)S(1)}, bf16[512,256]{1,0:T(8,128)(2,1)S(1)}, u32[]{:S(2)}, u32[]{:S(2)}) collective-permute-start(bf16[512,256]{1,0:T(8,128)(2,1)S(1)} %get-tuple-element.258), channel_id=1, source_target_pairs={{2,0},{3,1},{6,4},{7,5},{10,8},{11,9},{14,12},{15,13},{18,16},{19,... | collective-permute-start | bytes 786440 | tf_op jit(solution)/shard_map/ppermute | solution.py:534
  477.6 29.6 %collective-permute-start.48 = (bf16[512,256]{1,0:T(8,128)(2,1)S(1)}, bf16[512,256]{1,0:T(8,128)(2,1)S(1)}, u32[]{:S(2)}, u32[]{:S(2)}) collective-permute-start(bf16[512,256]{1,0:T(8,128)(2,1)S(1)} %get-tuple-element.257), channel_id=1, source_target_pairs={{1,0},{2,1},{3,2},{5,4},{6,5},{7,6},{9,8},{10,9},{11,10},{13,12},{... | collective-permute-start | bytes 786440 | tf_op jit(solution)/shard_map/ppermute | solution.py:534
  480.8 133.0 %collective-permute-start.56 = (bf16[512,2048]{1,0:T(8,128)(2,1)}, bf16[512,2048]{1,0:T(8,128)(2,1)}, u32[]{:S(2)}, u32[]{:S(2)}) collective-permute-start(bf16[512,2048]{1,0:T(8,128)(2,1)} %pad_maximum_fusion.12), channel_id=1, source_target_pairs={{0,4},{4,0},{8,12},{12,8},{16,20},{20,16},{24,28},{28,24},{1,5},{5... | collective-permute-start | bytes 6291464 | tf_op jit(solution)/shard_map/ppermute | solution.py:526
  507.2 111.3 %collective-permute-start.72 = (bf16[512,2048]{1,0:T(8,128)(2,1)}, bf16[512,2048]{1,0:T(8,128)(2,1)}, u32[]{:S(2)}, u32[]{:S(2)}) collective-permute-start(bf16[512,2048]{1,0:T(8,128)(2,1)} %pad_maximum_fusion.13), channel_id=1, source_target_pairs={{0,4},{4,0},{8,12},{12,8},{16,20},{20,16},{24,28},{28,24},{1,5},{5... | collective-permute-start | bytes 6291464 | tf_op jit(solution)/shard_map/ppermute | solution.py:526
  589.7 31.9 %collective-permute-start.96 = (bf16[512,2048]{1,0:T(8,128)(2,1)}, bf16[512,2048]{1,0:T(8,128)(2,1)}, u32[]{:S(2)}, u32[]{:S(2)}) collective-permute-start(bf16[512,2048]{1,0:T(8,128)(2,1)} %convolution_convert_fusion.4), channel_id=1, source_target_pairs={{0,4},{4,0},{8,12},{12,8},{16,20},{20,16},{24,28},{28,24},{1,5},{5... | collective-permute-start | bytes 6291464 | tf_op jit(solution)/shard_map/ppermute | solution.py:526
  610.1 123.4 %collective-permute-start.88 = (bf16[512,4096]{1,0:T(8,128)(2,1)}, bf16[512,4096]{1,0:T(8,128)(2,1)S(1)}, u32[]{:S(2)}, u32[]{:S(2)}) collective-permute-start(bf16[512,4096]{1,0:T(8,128)(2,1)} %pad_maximum_fusion.3), channel_id=1, source_target_pairs={{0,4},{4,0},{8,12},{12,8},{16,20},{20,16},{24,28},{28,24},{1,5},{5... | collective-permute-start | bytes 12582920 | tf_op jit(solution)/shard_map/ppermute | solution.py:526
  618.4 35.7 %collective-permute-start.59 = (bf16[256,1024]{1,0:T(8,128)(2,1)S(1)}, bf16[256,1024]{1,0:T(8,128)(2,1)S(1)}, u32[]{:S(2)}, u32[]{:S(2)}) collective-permute-start(bf16[256,1024]{1,0:T(8,128)(2,1)S(1)} %pad_maximum_fusion.34), channel_id=1, source_target_pairs={{0,8},{4,12},{8,0},{12,4},{16,24},{20,28},{24,16},{28,20},{1,9},{5... | collective-permute-start | bytes 1572872 | tf_op jit(solution)/shard_map/ppermute | solution.py:526
  621.6 21.6 %collective-permute-start.73 = (bf16[256,1024]{1,0:T(8,128)(2,1)S(1)}, bf16[256,1024]{1,0:T(8,128)(2,1)S(1)}, u32[]{:S(2)}, u32[]{:S(2)}) collective-permute-start(bf16[256,1024]{1,0:T(8,128)(2,1)S(1)} %concatenate.551), channel_id=1, source_target_pairs={{0,16},{4,20},{8,24},{12,28},{16,0},{20,4},{24,8},{28,12},{1,17},{... | collective-permute-start | bytes 1572872 | tf_op jit(solution)/shard_map/ppermute | solution.py:526
  625.8 28.3 %collective-permute-start.97 = (bf16[256,1024]{1,0:T(8,128)(2,1)S(1)}, bf16[256,1024]{1,0:T(8,128)(2,1)S(1)}, u32[]{:S(2)}, u32[]{:S(2)}) collective-permute-start(bf16[256,1024]{1,0:T(8,128)(2,1)S(1)} %concatenate.554), channel_id=1, source_target_pairs={{0,16},{4,20},{8,24},{12,28},{16,0},{20,4},{24,8},{28,12},{1,17},{... | collective-permute-start | bytes 1572872 | tf_op jit(solution)/shard_map/ppermute | solution.py:526
  632.0 25.5 %collective-permute-start.75 = (bf16[256,1024]{1,0:T(8,128)(2,1)S(1)}, bf16[256,1024]{1,0:T(8,128)(2,1)S(1)}, u32[]{:S(2)}, u32[]{:S(2)}) collective-permute-start(bf16[256,1024]{1,0:T(8,128)(2,1)S(1)} %pad_maximum_fusion.35), channel_id=1, source_target_pairs={{0,8},{4,12},{8,0},{12,4},{16,24},{20,28},{24,16},{28,20},{1,9},{5... | collective-permute-start | bytes 1572872 | tf_op jit(solution)/shard_map/ppermute | solution.py:526
  654.0 20.8 %collective-permute-start.100 = (bf16[256,1024]{1,0:T(8,128)(2,1)S(1)}, bf16[256,1024]{1,0:T(8,128)(2,1)S(1)}, u32[]{:S(2)}, u32[]{:S(2)}) collective-permute-start(bf16[256,1024]{1,0:T(8,128)(2,1)S(1)} %pad_maximum_fusion.37), channel_id=1, source_target_pairs={{0,8},{4,12},{8,0},{12,4},{16,24},{20,28},{24,16},{28,20},{1,9},{5... | collective-permute-start | bytes 1572872 | tf_op jit(solution)/shard_map/ppermute | solution.py:526
  654.1 37.2 %collective-permute-start.81 = (bf16[256,1024]{1,0:T(8,128)(2,1)S(1)}, bf16[256,1024]{1,0:T(8,128)(2,1)S(1)}, u32[]{:S(2)}, u32[]{:S(2)}) collective-permute-start(bf16[256,1024]{1,0:T(8,128)(2,1)S(1)} %concatenate.552), channel_id=1, source_target_pairs={{0,16},{4,20},{8,24},{12,28},{16,0},{20,4},{24,8},{28,12},{1,17},{... | collective-permute-start | bytes 1572872 | tf_op jit(solution)/shard_map/ppermute | solution.py:526
  655.2 19.3 %collective-permute-start.74 = (bf16[128,1024]{1,0:T(8,128)(2,1)S(1)}, bf16[128,1024]{1,0:T(8,128)(2,1)S(1)}, u32[]{:S(2)}, u32[]{:S(2)}) collective-permute-start(bf16[128,1024]{1,0:T(8,128)(2,1)S(1)} %add_convert_fusion.27), channel_id=1, source_target_pairs={{0,8},{4,12},{8,0},{12,4},{16,24},{20,28},{24,16},{28,20},{1,9},{5... | collective-permute-start | bytes 786440 | tf_op jit(solution)/shard_map/ppermute | solution.py:526
  657.5 78.4 %collective-permute-start.83 = (bf16[256,1024]{1,0:T(8,128)(2,1)S(1)}, bf16[256,1024]{1,0:T(8,128)(2,1)S(1)}, u32[]{:S(2)}, u32[]{:S(2)}) collective-permute-start(bf16[256,1024]{1,0:T(8,128)(2,1)S(1)} %pad_maximum_fusion.36), channel_id=1, source_target_pairs={{0,8},{4,12},{8,0},{12,4},{16,24},{20,28},{24,16},{28,20},{1,9},{5... | collective-permute-start | bytes 1572872 | tf_op jit(solution)/shard_map/ppermute | solution.py:526
  734.8 26.2 %collective-permute-start.89 = (bf16[256,2048]{1,0:T(8,128)(2,1)S(1)}, bf16[256,2048]{1,0:T(8,128)(2,1)S(1)}, u32[]{:S(2)}, u32[]{:S(2)}) collective-permute-start(bf16[256,2048]{1,0:T(8,128)(2,1)S(1)} %concatenate.553), channel_id=1, source_target_pairs={{0,16},{4,20},{8,24},{12,28},{16,0},{20,4},{24,8},{28,12},{1,17},{... | collective-permute-start | bytes 3145736 | tf_op jit(solution)/shard_map/ppermute | solution.py:526
  736.2 28.2 %collective-permute-start.84 = (bf16[128,1024]{1,0:T(8,128)(2,1)S(1)}, bf16[128,1024]{1,0:T(8,128)(2,1)S(1)}, u32[]{:S(2)}, u32[]{:S(2)}) collective-permute-start(bf16[128,1024]{1,0:T(8,128)(2,1)S(1)} %get-tuple-element.238), channel_id=1, source_target_pairs={{0,16},{4,20},{8,24},{12,28},{16,0},{20,4},{24,8},{28,12},{1,17},{... | collective-permute-start | bytes 786440 | tf_op jit(solution)/shard_map/ppermute | solution.py:526
  737.5 27.1 %collective-permute-start.91 = (bf16[256,2048]{1,0:T(8,128)(2,1)S(1)}, bf16[256,2048]{1,0:T(8,128)(2,1)S(1)}, u32[]{:S(2)}, u32[]{:S(2)}) collective-permute-start(bf16[256,2048]{1,0:T(8,128)(2,1)S(1)} %pad_maximum_fusion.21), channel_id=1, source_target_pairs={{0,8},{4,12},{8,0},{12,4},{16,24},{20,28},{24,16},{28,20},{1,9},{5... | collective-permute-start | bytes 3145736 | tf_op jit(solution)/shard_map/ppermute | solution.py:526
  783.0 20.7 %collective-permute-start.94 = (bf16[128,1024]{1,0:T(8,128)(2,1)S(1)}, bf16[128,1024]{1,0:T(8,128)(2,1)S(1)}, u32[]{:S(2)}, u32[]{:S(2)}) collective-permute-start(bf16[128,1024]{1,0:T(8,128)(2,1)S(1)} %pad_maximum_fusion.44), channel_id=1, source_target_pairs={{0,2},{1,3},{2,0},{3,1},{4,6},{5,7},{6,4},{7,5},{8,10},{9,11},{10,... | collective-permute-start | bytes 786440 | tf_op jit(solution)/shard_map/ppermute | solution.py:530
  783.2 20.6 %collective-permute-start.93 = (bf16[128,1024]{1,0:T(8,128)(2,1)S(1)}, bf16[128,1024]{1,0:T(8,128)(2,1)S(1)}, u32[]{:S(2)}, u32[]{:S(2)}) collective-permute-start(bf16[128,1024]{1,0:T(8,128)(2,1)S(1)} %pad_maximum_fusion.43), channel_id=1, source_target_pairs={{0,3},{1,0},{2,1},{3,2},{4,7},{5,4},{6,5},{7,6},{8,11},{9,8},{10,9... | collective-permute-start | bytes 786440 | tf_op jit(solution)/shard_map/ppermute | solution.py:530
  (290 other events, 5436.4 us)

commit v2 on v1

v2 whole, which is shorter than its diff:
```python
import functools

import jax
import jax.numpy as jnp
import numpy as np
from jax import lax
from jax.experimental import pallas as pl
from jax.experimental.pallas import tpu as pltpu
from jax.sharding import PartitionSpec as P

QH = 8
KVH = 2
HD = 64
MH = 24
MP = 64
NS = 128
KCONV = 4
GROUP = QH // KVH
INNER = MH * MP
SPAN = 128
HALO = 16
LANE = 128
QB = 128
KB = 256
NEG = -1e30
FFN_AFTER = 1
COST = pl.CostEstimate(flops=2_000_000_000, bytes_accessed=4_000_000, transcendentals=0)

epsilon = 1e-05
rope_base = 100000000000.0
f32 = jnp.float32
bf16 = jnp.bfloat16

NN = (((1,), (0,)), ((), ()))
NT = (((1,), (1,)), ((), ()))
TN = (((0,), (0,)), ((), ()))


def dot(a, b, dims=NN):
    return lax.dot_general(a, b, dims, preferred_element_type=f32)


def split2(v, axis=1):
    hi = v.astype(bf16)
    lo = (v - hi.astype(f32)).astype(bf16)
    return jnp.concatenate([hi, lo], axis=axis)


def params(mb):
    return pltpu.CompilerParams(vmem_limit_bytes=mb * 1024 * 1024)


def sds(shape, dtype):
    return jax.ShapeDtypeStruct(shape, dtype)


def whole(shape):
    return pl.BlockSpec(shape, lambda *_: (0,) * len(shape), pipeline_mode=pl.Buffered(1))


def wholes(arrays):
    return [whole(a.shape) for a in arrays]


def attn_keep(segk_ref, segq_ref, off, i, back):
    pos_k = lax.broadcasted_iota(jnp.int32, (KB, QB), 0) + off
    pos_q = lax.broadcasted_iota(jnp.int32, (KB, QB), 1) + (back + i * QB)
    same = segk_ref[pl.ds(off, KB), :] == segq_ref[:, i * QB : (i + 1) * QB]
    return same & (pos_k <= pos_q)


def head_columns(g):
    return [slice(c * HD, (c + 2) * HD) for c in range(g * GROUP, (g + 1) * GROUP, 2)]


def stack_heads(ref, i, columns):
    rows = slice(i * QB, (i + 1) * QB)
    heads = []
    for at in columns:
        pair = ref[rows, at]
        heads += [pair[:, :HD], pair[:, HD:]]
    return jnp.concatenate(heads, axis=0)


def turn(v, cosine, sine):
    lane = lax.broadcasted_iota(jnp.int32, v.shape, 1)
    swapped = jnp.where(lane % HD < HD // 2, pltpu.roll(v, LANE - HD // 2, 1), pltpu.roll(v, HD // 2, 1))
    return v * cosine + swapped * sine


def load_pairs(pair_ref, kv_refs, at):
    rows = kv_refs[0].shape[0]
    for n, ref in enumerate(kv_refs):
        both = ref[:, at : at + KVH * HD]
        for g in range(KVH):
            pair_ref[g, n * rows : (n + 1) * rows, :] = both[:, g * HD : (g + 1) * HD]


def attn_fwd_kernel(first_ref, q_ref, segq_ref, segk_ref, *refs):
    kv_refs, (o_ref, lse_ref, k_ref, vt_ref) = refs[:-4], refs[-4:]
    rows = q_ref.shape[0]
    back = k_ref.shape[1] - rows
    wide = GROUP * QB
    load_pairs(k_ref, kv_refs, 0)
    for n, ref in enumerate(kv_refs):
        vt_ref[:, n * rows : (n + 1) * rows] = ref[:, KVH * HD :].astype(f32).T.astype(bf16)
    for i in range(rows // QB):
        last = (back + (i + 1) * QB + KB - 1) // KB
        for g in range(KVH):
            columns = head_columns(g)
            queries = stack_heads(q_ref, i, columns)

            def body(j, carry):
                top, total, acc = carry
                off = pl.multiple_of(j * KB, KB)
                scores = dot(k_ref[g, pl.ds(off, KB), :], queries, NT)
                keep = attn_keep(segk_ref, segq_ref, off, i, back)
                keep = jnp.concatenate([keep] * GROUP, axis=1)
                scores = jnp.where(keep, scores, NEG)
                new_top = jnp.maximum(top, jnp.max(scores, axis=0, keepdims=True))
                scale = jnp.exp(top - new_top)
                probs = jnp.exp(scores - new_top)
                total = total * scale + jnp.sum(probs, axis=0, keepdims=True)
                vt = vt_ref[g * HD : (g + 1) * HD, pl.ds(off, KB)]
                acc = acc * scale + dot(vt, probs.astype(bf16))
                return new_top, total, acc

            start = (jnp.full((1, wide), NEG, f32), jnp.zeros((1, wide), f32), jnp.zeros((HD, wide), f32))
            top, total, acc = lax.fori_loop(first_ref[i], last, body, start)
            lse_ref[i * KVH + g : i * KVH + g + 1, :] = top + jnp.log(total)
            acc = acc / total
            for h in range(0, GROUP, 2):
                pair = jnp.concatenate(
                    [acc[:, h * QB : (h + 1) * QB], acc[:, (h + 1) * QB : (h + 2) * QB]], axis=0
                ).T
                o_ref[i * QB : (i + 1) * QB, columns[h // 2]] = pair.astype(bf16)


def attn_bwd_kernel(first_ref, q_ref, do_ref, o_ref, lse_ref, segq_ref, segk_ref, cos_ref, sin_ref, *refs):
    n_kv = (len(refs) - 5) // 2
    kv_refs, dq_ref, dkv_refs = refs[:n_kv], refs[n_kv], refs[n_kv + 1 : 2 * n_kv + 1]
    k_ref, v_ref, dk_ref, dv_ref = refs[2 * n_kv + 1 :]
    rows = q_ref.shape[0]
    back = k_ref.shape[1] - rows
    wide = GROUP * QB
    load_pairs(k_ref, kv_refs, 0)
    load_pairs(v_ref, kv_refs, KVH * HD)
    dk_ref[...] = jnp.zeros_like(dk_ref)
    dv_ref[...] = jnp.zeros_like(dv_ref)
    for i in range(rows // QB):
        last = (back + (i + 1) * QB + KB - 1) // KB
        here = slice(i * QB, (i + 1) * QB)
        for g in range(KVH):
            columns = head_columns(g)
            queries = stack_heads(q_ref, i, columns)
            grads = stack_heads(do_ref, i, columns)
            outs = stack_heads(o_ref, i, columns)
            prod = grads.astype(f32) * outs.astype(f32)
            ones = jnp.ones((8, 2 * HD), bf16)
            delta = dot(ones, split2(prod), NT)[0:1, :]
            lse = lse_ref[i * KVH + g : i * KVH + g + 1, :]

            def body(j, acc):
                off = pl.multiple_of(j * KB, KB)
                keys = k_ref[g, pl.ds(off, KB), :]
                vals = v_ref[g, pl.ds(off, KB), :]
                keep = attn_keep(segk_ref, segq_ref, off, i, back)
                keep = jnp.concatenate([keep] * GROUP, axis=1)
                scores = jnp.where(keep, dot(keys, queries, NT), NEG)
                probs = jnp.exp(scores - lse)
                dprobs = dot(vals, grads, NT)
                dscores = (probs * (dprobs - delta)).astype(bf16)
                dv_ref[g, pl.ds(off, KB), :] += dot(probs.astype(bf16), grads)
                dk_ref[g, pl.ds(off, KB), :] += dot(dscores, queries)
                return acc + dot(keys, dscores, TN)

            acc = lax.fori_loop(first_ref[i], last, body, jnp.zeros((HD, wide), f32))
            acc = acc * (HD ** -0.5)
            for h in range(0, GROUP, 2):
                pair = jnp.concatenate(
                    [acc[:, h * QB : (h + 1) * QB], acc[:, (h + 1) * QB : (h + 2) * QB]], axis=0
                ).T
                pair = turn(pair.astype(bf16).astype(f32), cos_ref[here, :], -sin_ref[here, :])
                dq_ref[here, columns[h // 2]] = pair.astype(bf16)
    for n, out in enumerate(dkv_refs):
        span = slice(n * rows, (n + 1) * rows)
        for at, ref in ((0, dk_ref), (KVH * HD, dv_ref)):
            both = jnp.concatenate([ref[g, span, :] for g in range(KVH)], axis=1)
            out[:, at : at + KVH * HD] = both.astype(out.dtype)


SMEM = pl.BlockSpec(memory_space=pltpu.SMEM)


def attn_fwd(first, q, segq, segk, kvs):
    rows = q.shape[0]
    total = rows * len(kvs)
    arrays = (q, segq, segk, *kvs)
    outs = (sds(q.shape, bf16), sds((rows // QB * KVH, GROUP * QB), f32))
    return pl.pallas_call(
        attn_fwd_kernel,
        grid=(1,),
        out_shape=outs,
        in_specs=[SMEM] + wholes(arrays),
        out_specs=tuple(wholes(outs)),
        scratch_shapes=[pltpu.VMEM((KVH, total, HD), bf16), pltpu.VMEM((KVH * HD, total), bf16)],
        compiler_params=params(40),
        cost_estimate=COST,
        name="attn_fwd",
    )(first, *arrays)


def attn_bwd(first, q, do, o, lse, segq, segk, cosine, sine, kvs):
    total = q.shape[0] * len(kvs)
    arrays = (q, do, o, lse, segq, segk, cosine, sine, *kvs)
    outs = (sds(q.shape, bf16), *[sds(a.shape, bf16) for a in kvs[:-1]], sds(kvs[-1].shape, f32))
    return pl.pallas_call(
        attn_bwd_kernel,
        grid=(1,),
        out_shape=outs,
        in_specs=[SMEM] + wholes(arrays),
        out_specs=tuple(wholes(outs)),
        scratch_shapes=[pltpu.VMEM((KVH, total, HD), bf16)] * 2 + [pltpu.VMEM((KVH, total, HD), f32)] * 2,
        compiler_params=params(40),
        cost_estimate=COST,
        name="attn_bwd",
    )(first, *arrays)


COLS = (INNER + 2 * NS) // LANE


def tri_masks():
    t = lax.broadcasted_iota(jnp.int32, (SPAN, SPAN), 0)
    s = lax.broadcasted_iota(jnp.int32, (SPAN, SPAN), 1)
    return t, s


def widen(v, spread2):
    return dot(split2(v), spread2)


def store_carry(step, carry_ref, state_ref, keep_ref):
    @pl.when(step == pl.num_programs(0) - 1)
    def _():
        carry_ref[:NS, :] = state_ref[...].astype(bf16)
        keep = keep_ref[...]
        high = keep.astype(bf16)
        carry_ref[NS:, :] = jnp.concatenate([high, (keep - high.astype(f32)).astype(bf16)], axis=0)


def load_carry(near_ref, far_refs):
    state = near_ref[:NS, :].astype(f32)
    for far_ref in far_refs:
        kept = near_ref[NS : NS + 1, :].astype(f32) + near_ref[NS + 8 : NS + 9, :].astype(f32)
        state = state + far_ref[:NS, :].astype(f32) * kept
    return state


def conv_block(u_ref, tap_ref, meta, base, col):
    lanes = slice(col * LANE, (col + 1) * LANE)
    window = u_ref[pl.ds(base + HALO - 8, SPAN + 8), lanes]
    taps = [window[8:, :]]
    for j in range(1, KCONV):
        taps.append(window[8 - j : 8 - j + SPAN, :] * meta[:, j : j + 1])
    total = tap_ref[KCONV : KCONV + 1, lanes] + tap_ref[KCONV - 1 : KCONV, lanes] * taps[0]
    for j in range(1, KCONV):
        total = total + tap_ref[KCONV - 1 - j : KCONV - j, lanes] * taps[j]
    return taps, total


def mamba_pre_kernel(u_ref, tap_ref, meta_ref, dtr_ref, head_ref, spread_ref,
                     mix_ref, dt_ref, cum_ref, cumt_ref, ec_ref, fw_ref, g_ref, carry_ref, fin_ref, keep_ref):
    c = pl.program_id(0)
    base = pl.multiple_of(c * SPAN, SPAN)

    @pl.when(c == 0)
    def _():
        fin_ref[...] = jnp.zeros_like(fin_ref)
        keep_ref[...] = jnp.ones_like(keep_ref)

    meta = meta_ref[...]
    for col in range(COLS):
        total = conv_block(u_ref, tap_ref, meta, base, col)[1]
        mix_ref[:, col * LANE : (col + 1) * LANE] = (total * jax.nn.sigmoid(total)).astype(bf16)
    raw = dtr_ref[...] + head_ref[0:1, :]
    dt = jnp.maximum(raw, 0.0) + jnp.log1p(jnp.exp(-jnp.abs(raw)))
    decay = dt * head_ref[1:2, :]
    t, s = tri_masks()
    lower = (t >= s).astype(f32)
    cum = lax.dot_general(lower, decay, NN, precision=lax.Precision.HIGHEST, preferred_element_type=f32)
    end = cum[SPAN - 1 : SPAN, :]
    ec = meta[:, 4:5] * jnp.exp(cum)
    fw = meta[:, 5:6] * jnp.exp(end - cum)
    gain = ec[SPAN - 1 : SPAN, :]
    dt_ref[...] = dt
    cum_ref[...] = cum
    cumt_ref[...] = cum.T[: cumt_ref.shape[0], :]
    ec_ref[...] = ec
    fw_ref[...] = fw
    gain8 = jnp.broadcast_to(gain, (8, LANE))
    g_ref[...] = gain8
    spread2 = spread_ref[...]
    weight = widen(fw * dt, spread2)
    x = mix_ref[:, :INNER].astype(f32)
    b = mix_ref[:, INNER : INNER + NS]
    gain_wide = widen(gain8, spread2)
    fin_ref[...] = fin_ref[...] * gain_wide[0:1, :] + dot(b, (x * weight).astype(bf16), TN)
    keep_ref[...] = keep_ref[...] * gain_wide
    store_carry(c, carry_ref, fin_ref, keep_ref)


def chunk_spec(width):
    return pl.BlockSpec((SPAN, width), lambda c: (c, 0))


def mamba_pre(u, taps, meta, dt_raw, heads, spread2):
    rows = meta.shape[0]
    n = rows // SPAN
    width = INNER + 2 * NS
    hl = 32
    return pl.pallas_call(
        mamba_pre_kernel,
        grid=(n,),
        in_specs=[whole(u.shape), whole(taps.shape), chunk_spec(8), chunk_spec(LANE), whole(heads.shape),
                  whole(spread2.shape)],
        out_specs=(chunk_spec(width), chunk_spec(LANE), chunk_spec(LANE), pl.BlockSpec((hl, SPAN), lambda c: (0, c)),
                   chunk_spec(LANE), chunk_spec(LANE), pl.BlockSpec((8, LANE), lambda c: (c, 0)), whole((NS + 16, INNER))),
        out_shape=(sds((rows, width), bf16), sds((rows, LANE), f32), sds((rows, LANE), f32), sds((hl, rows), f32),
                   sds((rows, LANE), f32), sds((rows, LANE), f32), sds((8 * n, LANE), f32),
                   sds((NS + 16, INNER), bf16)),
        scratch_shapes=[pltpu.VMEM((NS, INNER), f32), pltpu.VMEM((8, INNER), f32)],
        compiler_params=params(40),
        cost_estimate=COST,
        name="mamba_pre",
    )(u, taps, meta, dt_raw, heads, spread2)


def pair_halves(v):
    lane = lax.broadcasted_iota(jnp.int32, v.shape, 1)
    zero = jnp.zeros_like(v)
    return jnp.concatenate([jnp.where(lane < MP, v, zero), jnp.where(lane < MP, zero, v)], axis=0)


def mamba_fwd_kernel(mix_ref, dt_ref, cum_ref, cumt_ref, ec_ref, fw_ref, g_ref, segc_ref, segr_ref,
                     z_ref, skip_ref, spread_ref, *refs):
    carries, (gated_ref, full_ref, states_ref, state_ref) = refs[:-4], refs[-4:]
    c = pl.program_id(0)

    @pl.when(c == 0)
    def _():
        state_ref[...] = load_carry(carries[0], carries[1:])

    state = state_ref[...].astype(bf16)
    states_ref[0] = state
    spread2 = spread_ref[...]
    b = mix_ref[:, INNER : INNER + NS]
    cm = mix_ref[:, INNER + NS :]
    t, s = tri_masks()
    allowed = (segc_ref[...] == segr_ref[...]) & (t >= s)
    off = jnp.where(allowed, 0.0, NEG)
    affinity = dot(cm, b, NT)
    cum = cum_ref[...]
    dt = dt_ref[...]
    dt_wide = widen(dt, spread2)
    ec_wide = widen(ec_ref[...], spread2)
    carried = dot(cm, state) * ec_wide
    for p in range(MH // 2):
        lanes = slice(p * LANE, (p + 1) * LANE)
        x = mix_ref[:, lanes].astype(f32)
        pieces = []
        for h in (2 * p, 2 * p + 1):
            gap = cum[:, h : h + 1] - cumt_ref[h : h + 1, :] + off
            pieces.append((affinity * jnp.exp(gap)).astype(bf16))
        scaled = (x * dt_wide[:, lanes]).astype(bf16)
        y = dot(jnp.concatenate(pieces, axis=1), pair_halves(scaled)) + carried[:, lanes]
        y = y + skip_ref[0:1, lanes] * x
        z = z_ref[:, lanes]
        full_ref[:, lanes] = y.astype(bf16)
        gated_ref[:, lanes] = (y * (z * jax.nn.sigmoid(z))).astype(bf16)
    weight = widen(fw_ref[...] * dt, spread2)
    x = mix_ref[:, :INNER].astype(f32)
    gain = widen(g_ref[...], spread2)[0:1, :]
    state_ref[...] = state_ref[...] * gain + dot(b, (x * weight).astype(bf16), TN)


def mamba_fwd(mix, dt, cum, cumt, ec, fw, g, segc, segr, z, skip, spread2, carries):
    rows = mix.shape[0]
    n = rows // SPAN
    return pl.pallas_call(
        mamba_fwd_kernel,
        grid=(n,),
        in_specs=[chunk_spec(mix.shape[1]), chunk_spec(LANE), chunk_spec(LANE),
                  pl.BlockSpec((cumt.shape[0], SPAN), lambda c: (0, c)), chunk_spec(LANE), chunk_spec(LANE),
                  pl.BlockSpec((8, LANE), lambda c: (c, 0)), chunk_spec(1), pl.BlockSpec((1, SPAN), lambda c: (0, c)),
                  chunk_spec(INNER), whole(skip.shape), whole(spread2.shape), *wholes(carries)],
        out_specs=(chunk_spec(INNER), chunk_spec(INNER), pl.BlockSpec((1, NS, INNER), lambda c: (c, 0, 0))),
        out_shape=(sds((rows, INNER), bf16), sds((rows, INNER), bf16), sds((n, NS, INNER), bf16)),
        scratch_shapes=[pltpu.VMEM((NS, INNER), f32)],
        compiler_params=params(40),
        cost_estimate=COST,
        name="mamba_fwd",
    )(mix, dt, cum, cumt, ec, fw, g, segc, segr, z, skip, spread2, *carries)


def mamba_bpre_kernel(dg_ref, z_ref, full_ref, cm_ref, ec_ref, g_ref, spread_ref, dy_ref, dz_ref, carry_ref, back_ref, keep_ref):
    c = pl.program_id(0)

    @pl.when(c == 0)
    def _():
        back_ref[...] = jnp.zeros_like(back_ref)
        keep_ref[...] = jnp.ones_like(keep_ref)

    spread2 = spread_ref[...]
    z = z_ref[...]
    sig = jax.nn.sigmoid(z)
    dg = dg_ref[...].astype(f32)
    dy = dg * (z * sig)
    dy_ref[...] = dy.astype(bf16)
    dz_ref[...] = (dg * full_ref[...].astype(f32) * (sig * (1.0 + z * (1.0 - sig)))).astype(bf16)
    weighted = (dy * widen(ec_ref[...], spread2)).astype(bf16)
    gain_wide = widen(g_ref[...], spread2)
    back_ref[...] = back_ref[...] * gain_wide[0:1, :] + dot(cm_ref[...], weighted, TN)
    keep_ref[...] = keep_ref[...] * gain_wide
    store_carry(c, carry_ref, back_ref, keep_ref)


def mamba_bpre(dg, z, full, mix, ec, g, spread2):
    rows = dg.shape[0]
    n = rows // SPAN
    rev = lambda width, col=0: pl.BlockSpec((SPAN, width), lambda c: (n - 1 - c, col))
    return pl.pallas_call(
        mamba_bpre_kernel,
        grid=(n,),
        in_specs=[rev(INNER), rev(INNER), rev(INNER), rev(NS, (INNER + NS) // NS), rev(LANE),
                  pl.BlockSpec((8, LANE), lambda c: (n - 1 - c, 0)), whole(spread2.shape)],
        out_specs=(rev(INNER), rev(INNER), whole((NS + 16, INNER))),
        out_shape=(sds((rows, INNER), bf16), sds((rows, INNER), bf16), sds((NS + 16, INNER), bf16)),
        scratch_shapes=[pltpu.VMEM((NS, INNER), f32), pltpu.VMEM((8, INNER), f32)],
        compiler_params=params(40),
        cost_estimate=COST,
        name="mamba_bpre",
    )(dg, z, full, mix, ec, g, spread2)


def mamba_bwd_kernel(mix_ref, dt_ref, cum_ref, cumt_ref, ec_ref, fw_ref, g_ref, segc_ref, segr_ref,
                     dy_ref, states_ref, u_ref, tap_ref, meta_ref, skip_ref, head_ref, spread_ref, gather_ref, *refs):
    carries = refs[:-9]
    dpre_ref, ddt_ref, conv_ref, small_ref, dstate_ref, acc_ref, rows_ref, dx_ref, dbc_ref = refs[-9:]
    step = pl.program_id(0)
    c = pl.num_programs(0) - 1 - step
    base = pl.multiple_of(c * SPAN, SPAN)

    @pl.when(step == 0)
    def _():
        dstate_ref[...] = load_carry(carries[0], carries[1:])
        conv_ref[...] = jnp.zeros_like(conv_ref)
        small_ref[...] = jnp.zeros_like(small_ref)
        rows_ref[...] = jnp.zeros_like(rows_ref)

    spread2 = spread_ref[...]
    gather2 = gather_ref[...]
    b = mix_ref[:, INNER : INNER + NS]
    cm = mix_ref[:, INNER + NS :]
    cum = cum_ref[...]
    dt = dt_ref[...]
    dt_wide = widen(dt, spread2)
    s, t = tri_masks()
    allowed = (segc_ref[...] == segr_ref[...]) & (t >= s)
    off = jnp.where(allowed, 0.0, NEG)
    affinity = dot(b, cm, NT)
    acc_ref[...] = jnp.zeros_like(acc_ref)
    for p in range(MH // 2):
        lanes = slice(p * LANE, (p + 1) * LANE)
        x = mix_ref[:, lanes].astype(f32)
        scaled = (x * dt_wide[:, lanes]).astype(bf16)
        dy = dy_ref[:, lanes]
        dmix = dot(pair_halves(scaled), dy, NT)
        pieces = []
        total = None
        for q, h in enumerate((2 * p, 2 * p + 1)):
            gap = cumt_ref[h : h + 1, :] - cum[:, h : h + 1] + off
            decays = jnp.exp(gap)
            mixing = (affinity * decays).astype(bf16)
            pieces.append(mixing)
            dm = dmix[q * SPAN : (q + 1) * SPAN, :]
            rows_ref[h : h + 1, :] = jnp.sum(dm * mixing.astype(f32), axis=0, keepdims=True)
            part = dm * decays
            total = part if total is None else total + part
        acc_ref[...] += total
        dx_ref[:, lanes] = dot(jnp.concatenate(pieces, axis=1), pair_halves(dy))
    dscaled = dx_ref[...]
    x = mix_ref[:, :INNER].astype(f32)
    scaled = (x * dt_wide).astype(bf16).astype(f32)
    dy = dy_ref[...].astype(f32)
    dstate = dstate_ref[...]
    dstate_low = dstate.astype(bf16)
    state = states_ref[0]
    ec_wide = widen(ec_ref[...], spread2)
    fw_wide = widen(fw_ref[...], spread2)
    from_state = fw_wide * dot(b, dstate_low)
    carried = ec_wide * dot(cm, state)
    weighted_dy = (dy * ec_wide).astype(bf16)
    cols_sum = dot(split2(scaled * dscaled), gather2)
    carr_sum = dot(split2(dy * carried), gather2)
    fdf_sum = dot(split2(scaled * from_state), gather2)
    dxd = dscaled + from_state
    ddt_direct = dot(split2(x * dxd), gather2)
    skip_part = dot(split2(dy * x), gather2)
    gain = widen(g_ref[...], spread2)[0:1, :]
    state_dot = jnp.sum(dstate * state.astype(f32), axis=0, keepdims=True) * gain
    state_dot = dot(split2(jnp.broadcast_to(state_dot, (8, INNER))), gather2)[0:1, :]
    tt, ss = tri_masks()
    suffix = (ss >= tt).astype(bf16)
    prefix = (ss < tt).astype(bf16)
    suffix2 = jnp.concatenate([suffix, suffix], axis=1)
    dlog = dot(suffix2, split2(carr_sum - cols_sum, axis=0))
    dlog = dlog + dot(suffix2, split2(rows_ref[...]), NT)
    dlog = dlog + dot(jnp.concatenate([prefix, prefix], axis=1), split2(fdf_sum, axis=0)) + state_dot
    decay_rate = head_ref[1:2, :]
    ddt = (ddt_direct + dlog * decay_rate) * (1.0 - jnp.exp(-dt))
    ddt_ref[...] = ddt.astype(bf16)
    small_ref[0:1, :] += jnp.sum(dlog * dt, axis=0, keepdims=True) * decay_rate
    small_ref[1:2, :] += jnp.sum(skip_part, axis=0, keepdims=True)
    small_ref[2:3, :] += jnp.sum(ddt, axis=0, keepdims=True)
    dx_ref[...] = dxd * dt_wide + skip_ref[0:1, :] * dy
    daff = acc_ref[...]
    daff_low = daff.astype(bf16)
    fx = (scaled * fw_wide).astype(bf16)
    dbc_ref[:, :NS] = dot(daff_low, cm) + dot(fx, dstate_low, NT)
    dbc_ref[:, NS:] = dot(daff_low, b, TN) + dot(weighted_dy, state, NT)
    dstate_ref[...] = dstate * gain + dot(cm, weighted_dy, TN)
    meta = meta_ref[...]
    for col in range(COLS):
        lanes = slice(col * LANE, (col + 1) * LANE)
        taps, total = conv_block(u_ref, tap_ref, meta, base, col)
        sig = jax.nn.sigmoid(total)
        if col * LANE < INNER:
            dmixed = dx_ref[:, lanes]
        else:
            dmixed = dbc_ref[:, col * LANE - INNER : (col + 1) * LANE - INNER]
        dpre = dmixed * (sig * (1.0 + total * (1.0 - sig)))
        dpre_ref[:, lanes] = dpre
        for j in range(KCONV):
            conv_ref[KCONV - 1 - j : KCONV - j, lanes] += jnp.sum(dpre * taps[j], axis=0, keepdims=True)
        conv_ref[KCONV : KCONV + 1, lanes] += jnp.sum(dpre, axis=0, keepdims=True)


def mamba_bwd(mix, dt, cum, cumt, ec, fw, g, segc, segr, dy, states, u, taps, meta, skip, heads, spread2, gather2,
              carries):
    rows = mix.shape[0]
    n = rows // SPAN
    width = mix.shape[1]
    rev = lambda w: pl.BlockSpec((SPAN, w), lambda c: (n - 1 - c, 0))
    return pl.pallas_call(
        mamba_bwd_kernel,
        grid=(n,),
        in_specs=[rev(width), rev(LANE), rev(LANE),
                  pl.BlockSpec((cumt.shape[0], SPAN), lambda c: (0, n - 1 - c)), rev(LANE), rev(LANE),
                  pl.BlockSpec((8, LANE), lambda c: (n - 1 - c, 0)), rev(1),
                  pl.BlockSpec((1, SPAN), lambda c: (0, n - 1 - c)), rev(INNER),
                  pl.BlockSpec((1, NS, INNER), lambda c: (n - 1 - c, 0, 0)), whole(u.shape), whole(taps.shape),
                  rev(8), whole(skip.shape), whole(heads.shape), whole(spread2.shape), whole(gather2.shape),
                  *wholes(carries)],
        out_specs=(rev(width), rev(LANE), whole((8, width)), whole((8, LANE))),
        out_shape=(sds((rows, width), f32), sds((rows, LANE), bf16), sds((8, width), f32), sds((8, LANE), f32)),
        scratch_shapes=[pltpu.VMEM((NS, INNER), f32), pltpu.VMEM((SPAN, SPAN), f32), pltpu.VMEM((LANE, SPAN), f32),
                        pltpu.VMEM((SPAN, INNER), f32), pltpu.VMEM((SPAN, 2 * NS), f32)],
        compiler_params=params(56),
        cost_estimate=COST,
        name="mamba_bwd",
    )(mix, dt, cum, cumt, ec, fw, g, segc, segr, dy, states, u, taps, meta, skip, heads, spread2, gather2, *carries)


NB = 8
LOW = (0, 2, 4, 6)
ORDERS = ((2, 4), (4, 2))
SETS = ((0, 1), (2, 3))
SET_MASKS = ((0, 2, 4, 6), (0, 4, 2, 6))


class Ring:
    def __init__(self, mesh):
        self.nd = mesh.shape["dp"]
        self.nt = mesh.shape["tensor"]
        self.unit = self.nd // NB
        base = range(0, self.nd, self.unit)
        self.groups = [[b + i for i in range(self.unit)] for b in base]

    def dp(self, value, mask):
        step = mask * self.unit
        return lax.ppermute(value, "dp", [(i, i ^ step) for i in range(self.nd)])

    def shift(self, value, s):
        n = self.nt
        return lax.ppermute(value, "tensor", [(i, (i + s) % n) for i in range(n)])

    def line(self, value, s):
        n = self.nt
        return lax.ppermute(value, "tensor", [(i, i + s) for i in range(n) if 0 <= i + s < n])

    def block(self, value):
        if self.unit == 1:
            return value
        return lax.all_gather(value, "dp", axis=0, tiled=True, axis_index_groups=self.groups)

    def unblock(self, value):
        if self.unit == 1:
            return value
        return lax.psum_scatter(value, "dp", scatter_dimension=0, tiled=True, axis_index_groups=self.groups)

    def gather(self, pack, hold=lambda stage, values: values):
        own = self.block(pack)
        (own,) = hold(0, [own])
        parts = [own] + [self.shift(own, s) for s in range(1, self.nt)]
        pairs = hold(1, [join([parts[s] for s in members]) for members in SETS])
        nears = [self.dp(pair, one) for pair, (one, _) in zip(pairs, ORDERS)]
        firsts = [
            join([parts[s] for s in members] + [near]) for members, near in zip(SETS, nears)
        ]
        firsts = hold(2, firsts)
        sides = [[first, self.dp(first, two)] for first, (_, two) in zip(firsts, ORDERS)]
        sides = [hold(3, side) for side in sides]
        return [[lows, [self.dp(low, 1) for low in lows]] for lows in sides]

    def scatter(self, sent, kept):
        came = self.dp(sent, 1)
        parts = []
        for n, (second, first) in enumerate(ORDERS):
            here = slice(2 * n, 2 * n + 2)
            out = add(kept[here, 2:], came[here, 2:])
            mine = add(kept[here, :2], came[here, :2])
            got = self.dp(out, first)
            out = add(mine[:, 1:], got[:, 1:])
            mine = add(mine[:, :1], got[:, :1])
            got = self.dp(out, second)
            parts += [add(mine[i, 0], got[i, 0]) for i in range(2)]
        return parts

    def total(self, parts):
        total = parts[0].astype(f32)
        for s in range(1, self.nt):
            total = total + self.shift(parts[s], self.nt - s).astype(f32)
        return total

    def collect(self, parts):
        return self.unblock(self.total(parts))

    def all_sum(self, value):
        bit = 1
        while bit < self.nd:
            value = value + lax.ppermute(value, "dp", [(i, i ^ bit) for i in range(self.nd)])
            bit *= 2
        return value + sum(self.shift(value, s) for s in range(1, self.nt))


def after(values, *others):
    return lax.optimization_barrier((tuple(values), others))[0]


def add(a, b):
    return (a.astype(f32) + b.astype(f32)).astype(bf16)


def join_kernel(*refs):
    out = refs[-1]
    if len(out.shape) == 3:
        for i, ref in enumerate(refs[:-1]):
            out[i] = ref[...]
    else:
        for i, ref in enumerate(refs[:2]):
            out[0, i] = ref[...]
        out[1] = refs[2][...]


def join(pieces):
    rows, cols = pieces[0].shape
    shape = (2, rows, cols) if len(pieces) == 2 else (2, 2, rows, cols)
    return pl.pallas_call(
        join_kernel,
        grid=(1,),
        out_shape=sds(shape, bf16),
        in_specs=wholes(pieces),
        out_specs=whole(shape),
        compiler_params=params(40),
        cost_estimate=COST,
        name="join",
    )(*pieces)


def block_rows(index_ref, at, rows):
    return pl.ds(pl.multiple_of(index_ref[at] * rows, rows), rows)


def part_columns(index_ref, s, width):
    return pl.ds(pl.multiple_of(index_ref[8 + s] * width, width), width)


def assemble_kernel(widths, index_ref, *refs):
    buffers, outs = refs[:8], refs[8:]
    rows = buffers[0].shape[2]
    for n in range(2):
        for half in range(2):
            for k in range(4):
                buffer = buffers[4 * n + 2 * half + k // 2]
                m = LOW.index(SET_MASKS[n][k])
                here = block_rows(index_ref, 4 * half + m, rows)
                for i in range(2):
                    at = 0
                    for width, out in zip(widths, outs):
                        piece = buffer[k % 2, i, :, at : at + width]
                        at += width
                        if out.shape[1] == width:
                            out[here, :] = piece if n + i == 0 else out[here, :] + piece
                        else:
                            out[here, part_columns(index_ref, 2 * n + i, width)] = piece


def assemble(index, sides, widths, totals):
    buffers = [buffer for side in sides for lows in side for buffer in lows]
    model = NB * buffers[0].shape[2]
    outs = tuple(sds((model, total), bf16) for total in totals)
    return pl.pallas_call(
        functools.partial(assemble_kernel, widths),
        grid=(1,),
        out_shape=outs,
        in_specs=[SMEM] + wholes(buffers),
        out_specs=tuple(wholes(outs)),
        compiler_params=params(48),
        cost_estimate=COST,
        name="assemble",
    )(index, *buffers)


def project_kernel(widths, index_ref, *refs):
    buffers, (normed_ref, halo_ref, cos_ref, sin_ref) = refs[:8], refs[8:12]
    weights, (u_ref, q_ref, kv_ref, dt_ref) = refs[12:16], refs[16:]
    assemble_kernel(widths, index_ref, *buffers, *weights)
    w_q, w_step, w_x, w_shared = weights
    kv_width = KVH * HD
    half = normed_ref.shape[0] // 2
    for r in range(2):
        here = slice(r * half, (r + 1) * half)
        normed = normed_ref[here, :]
        cosine, sine = cos_ref[here, :], sin_ref[here, :]
        kv = dot(normed, w_shared[:, : 2 * kv_width])
        kv_ref[here, :kv_width] = turn(kv[:, :kv_width], cosine, sine).astype(bf16)
        kv_ref[here, kv_width:] = kv[:, kv_width:].astype(bf16)
        q = dot(normed, w_q[...])
        for c in range(0, q.shape[1], LANE):
            tile = turn(q[:, c : c + LANE], cosine, sine).astype(bf16)
            q_ref[here, c : c + LANE] = tile * jnp.asarray(HD ** -0.5, bf16)
        dt_ref[here, :] = dot(normed, w_step[...])
        below = slice(HALO + r * half, HALO + (r + 1) * half)
        u_ref[below, INNER:] = dot(normed, w_shared[:, 2 * kv_width :])
        for c in range(0, INNER, 512):
            u_ref[below, c : c + 512] = dot(normed, w_x[:, c : c + 512])
    u_ref[:HALO, INNER:] = dot(halo_ref[...], w_shared[:, 2 * kv_width :])
    for c in range(0, INNER, 512):
        u_ref[:HALO, c : c + 512] = dot(halo_ref[...], w_x[:, c : c + 512])


def project(index, sides, widths, totals, normed, halo, cosine, sine):
    buffers = [buffer for side in sides for lows in side for buffer in lows]
    rows, model = normed.shape
    arrays = (*buffers, normed, halo, cosine, sine)
    outs = tuple(sds((model, total), bf16) for total in totals)
    outs += (sds((HALO + rows, INNER + 2 * NS), f32), sds((rows, QH * HD), bf16), sds((rows, 2 * KVH * HD), bf16),
             sds((rows, LANE), f32))
    return pl.pallas_call(
        functools.partial(project_kernel, widths),
        grid=(1,),
        out_shape=outs,
        in_specs=[SMEM] + wholes(arrays),
        out_specs=tuple(wholes(outs)),
        compiler_params=params(56),
        cost_estimate=COST,
        name="project",
    )(index, *arrays)


def transpose_into(out_ref, values):
    for c in range(0, values.shape[1], LANE):
        out_ref[c : c + LANE, :] = values[:, c : c + LANE].astype(f32).T.astype(bf16)


def norm_kernel(h_ref, c_ref, gain_ref, n_ref, nt_ref, ct_ref, scale_ref):
    values = h_ref[...].astype(f32)
    scale = lax.rsqrt(jnp.mean(values * values, axis=-1, keepdims=True) + epsilon)
    scale_ref[...] = scale
    n_ref[...] = (values * scale * gain_ref[...]).astype(bf16)
    transpose_into(nt_ref, n_ref[...])
    transpose_into(ct_ref, c_ref[...])


def pack_kernel(flips, *refs):
    out, at = refs[-1], 0
    for flip, ref in zip(flips, refs[:-1]):
        if flip:
            count = ref.shape[0]
            for r in range(0, count, LANE):
                out[:, at + r : at + r + LANE] = ref[r : r + LANE, :].astype(f32).T.astype(bf16)
        else:
            count = ref.shape[1]
            out[:, at : at + count] = ref[...]
        at += count


def pack(arrays, flips):
    rows = arrays[0].shape[0]
    columns = sum(a.shape[0] if flip else a.shape[1] for a, flip in zip(arrays, flips))
    return simple_call(functools.partial(pack_kernel, flips), "pack", tuple(arrays), sds((rows, columns), bf16))


def middle_kernel(att_ref, gated_ref, wa_ref, wm_ref, h_ref, gain_ref, res_ref, n_ref, nt_ref, scale_ref):
    model = h_ref.shape[1]
    for c in range(0, model, 256):
        cols = slice(c, c + 256)
        mixer = dot(att_ref[...], wa_ref[cols, :], NT) + dot(gated_ref[...], wm_ref[cols, :], NT)
        res_ref[:, cols] = h_ref[:, cols].astype(f32) + mixer
    values = res_ref[...]
    scale = lax.rsqrt(jnp.mean(values * values, axis=-1, keepdims=True) + epsilon)
    scale_ref[...] = scale
    n_ref[...] = (values * scale * gain_ref[...]).astype(bf16)
    transpose_into(nt_ref, n_ref[...])


def after_ffn_kernel(dn_ref, res_ref, scale_ref, gain_ref, c_ref, wa_ref, wm_ref,
                     dres_ref, dmt_ref, dg_ref, da_ref, gain_grad_ref):
    dn, values, scale = dn_ref[...], res_ref[...], scale_ref[...]
    weighted = dn * gain_ref[...]
    inner = jnp.mean(weighted * values, axis=-1, keepdims=True)
    gain_grad_ref[...] = jnp.broadcast_to(jnp.sum(dn * values * scale, axis=0, keepdims=True), gain_grad_ref.shape)
    dres = c_ref[...].astype(f32) + scale * weighted - values * (scale * scale * scale * inner)
    dres_ref[...] = dres
    low = dres.astype(bf16)
    transpose_into(dmt_ref, low)
    da_ref[...] = dot(low, wa_ref[...]).astype(bf16)
    for c in range(0, wm_ref.shape[1], 512):
        dg_ref[:, c : c + 512] = dot(low, wm_ref[:, c : c + 512]).astype(bf16)


def conv_back_kernel(dpre_ref, after_ref, tap_ref, keep_ref, dkv_ref, dx_ref, dshared_ref):
    rows = dpre_ref.shape[0]
    kv = dkv_ref.shape[1]
    dshared_ref[:, :kv] = dkv_ref[...]
    for c in range(0, rows, SPAN):
        keep = keep_ref[c : c + SPAN, :]
        for col in range(COLS):
            lanes = slice(col * LANE, (col + 1) * LANE)
            if c + SPAN < rows:
                window = dpre_ref[c : c + SPAN + 8, lanes]
            else:
                window = jnp.concatenate([dpre_ref[c : c + SPAN, lanes], after_ref[:, lanes]], axis=0)
            total = tap_ref[KCONV - 1 : KCONV, lanes] * window[:SPAN, :]
            for j in range(1, KCONV):
                total = total + tap_ref[KCONV - 1 - j : KCONV - j, lanes] * window[j : j + SPAN, :] * keep[:, j : j + 1]
            if col * LANE < INNER:
                dx_ref[c : c + SPAN, lanes] = total.astype(bf16)
            else:
                at = kv + col * LANE - INNER
                dshared_ref[c : c + SPAN, at : at + LANE] = total.astype(bf16)


def kv_back_kernel(cos_ref, sin_ref, own_ref, *refs):
    out_ref = refs[-1]
    total = own_ref[...]
    for ref in refs[:-1]:
        total = total + ref[...].astype(f32)
    kv_width = KVH * HD
    out_ref[:, :kv_width] = turn(total[:, :kv_width], cos_ref[...], -sin_ref[...]).astype(bf16)
    out_ref[:, kv_width:] = total[:, kv_width:].astype(bf16)


def simple_call(kernel, name, arrays, outs, flops=0):
    single = not isinstance(outs, tuple)
    shapes = (outs,) if single else outs
    size = sum(a.size * a.dtype.itemsize for a in arrays) + sum(a.size * a.dtype.itemsize for a in shapes)
    return pl.pallas_call(
        kernel,
        grid=(1,),
        out_shape=outs,
        in_specs=wholes(arrays),
        out_specs=whole(outs.shape) if single else tuple(wholes(outs)),
        compiler_params=params(56),
        cost_estimate=COST,
        name=name,
    )(*arrays)


def left_rows(index_ref, left_ref, half, side):
    rows = left_ref.shape[0] // NB
    order = [LOW.index(m) for m in SET_MASKS[side]]
    return jnp.concatenate([left_ref[block_rows(index_ref, 4 * half + m, rows), :] for m in order], axis=0)


def grad_kernel(plan, n_left, n_right, index_ref, *refs):
    lefts = refs[:n_left]
    rights = refs[n_left : n_left + n_right]
    sent_ref, kept_ref = refs[n_left + n_right :]
    for s in range(4):
        for half, out in ((1, sent_ref), (0, kept_ref)):
            cache = {}
            at = 0
            for left, right, width, kind in plan:
                if kind == "fixed":
                    value = rights[right][:, s * width : (s + 1) * width]
                elif kind == "all":
                    value = rights[right][...]
                else:
                    value = rights[right][:, part_columns(index_ref, s, width)]
                if left not in cache:
                    cache[left] = left_rows(index_ref, lefts[left], half, s // 2)
                result = dot(cache[left], value)
                out[s, :, :, at : at + width] = result.reshape(4, -1, width).astype(bf16)
                at += width


def weight_grads(index, lefts, rights, plan):
    rows = lefts[0].shape[0] // NB
    columns = sum(width for _, _, width, _ in plan)
    outs = (sds((4, 4, rows, columns), bf16),) * 2
    return pl.pallas_call(
        functools.partial(grad_kernel, plan, len(lefts), len(rights)),
        grid=(1,),
        out_shape=outs,
        in_specs=[SMEM] + wholes(lefts) + wholes(rights),
        out_specs=tuple(wholes(outs)),
        compiler_params=params(56),
        cost_estimate=COST,
        name="weight_grads",
    )(index, *lefts, *rights)


def ffn_kernel(index_ref, w_ref, n_ref, nt_ref, c_ref, ct_ref, res_ref, grad_ref, out_ref, dn_ref, acc_ref):
    s = pl.program_id(0)
    model = n_ref.shape[1]
    units = w_ref.shape[3] // 3

    def weight(k):
        return w_ref[:, 0, :, k * units : (k + 1) * units].reshape(model, units)

    @pl.when(s == 0)
    def _():
        acc_ref[...] = res_ref[...]
        dn_ref[...] = jnp.zeros_like(dn_ref)

    gate = dot(n_ref[...], weight(0))
    up = dot(n_ref[...], weight(1))
    dact = dot(c_ref[...], weight(2)).astype(bf16).astype(f32)
    sig = jax.nn.sigmoid(gate)
    silu = gate * sig
    act = (silu * up).astype(bf16)
    dgate = (dact * up * (sig * (1.0 + gate * (1.0 - sig)))).astype(bf16)
    dup = (dact * silu).astype(bf16)
    acc_ref[...] += dot(act, weight(2), NT)
    dn_ref[...] += dot(dgate, weight(0), NT) + dot(dup, weight(1), NT)
    grad_ref[:, :units] = dot(nt_ref[...], dgate).astype(bf16)
    grad_ref[:, units : 2 * units] = dot(nt_ref[...], dup).astype(bf16)
    grad_ref[:, 2 * units :] = dot(ct_ref[...], act).astype(bf16)

    @pl.when(s == pl.num_programs(0) - 1)
    def _():
        out_ref[...] = acc_ref[...].astype(bf16)


def ffn(index, weights, normed, normed_t, cot, cot_t, residual):
    nd, nt, rows, columns = weights.shape
    tokens, model = normed.shape
    arrays = (normed, normed_t, cot, cot_t, residual)
    return pl.pallas_call(
        ffn_kernel,
        grid_spec=pltpu.PrefetchScalarGridSpec(
            num_scalar_prefetch=1,
            grid=(nt,),
            in_specs=[pl.BlockSpec((nd, 1, rows, columns), lambda s, index: (0, index[8 + s], 0, 0))] + wholes(arrays),
            out_specs=(
                pl.BlockSpec((model, columns), lambda s, index: (0, s)),
                whole((tokens, model)),
                whole((tokens, model)),
            ),
            scratch_shapes=[pltpu.VMEM((tokens, model), f32)],
        ),
        out_shape=(sds((model, nt * columns), bf16), sds((tokens, model), bf16), sds((tokens, model), f32)),
        compiler_params=params(60),
        cost_estimate=COST,
        name="ffn",
    )(index, weights, *arrays)


def rms_back(d_normed, values, scale, gain):
    weighted = d_normed * gain
    inner = jnp.mean(weighted * values, axis=-1, keepdims=True)
    gain_grad = jnp.sum(d_normed * values * scale, axis=0)
    return scale * weighted - values * (scale * scale * scale * inner), gain_grad


def rope_tables(rows, start):
    half = HD // 2
    frequency = rope_base ** (-2.0 * jnp.arange(half, dtype=f32) / HD)
    angles = (start + jnp.arange(rows)).astype(f32)[:, None] * frequency[None, :]
    cosine, sine = jnp.cos(angles), jnp.sin(angles)
    return jnp.concatenate([cosine] * 4, axis=1), jnp.concatenate([-sine, sine] * 2, axis=1)


def per_device(
    mesh,
    hidden,
    segments,
    cotangent,
    norm_gain,
    ffn_gain,
    query_proj,
    key_proj,
    value_proj,
    attn_out_proj,
    gate_inner,
    input_inner,
    state_proj,
    step_proj,
    mamba_out,
    conv_weight,
    conv_bias,
    decay_log,
    skip_gain,
    step_bias,
    ffn_gate,
    ffn_up,
    ffn_down,
):
    ring = Ring(mesh)
    nt = ring.nt
    di, ti = lax.axis_index("dp"), lax.axis_index("tensor")
    rows, width = hidden.shape
    seq = segments.shape[1]
    hops = -(-(seq // 2 - 1) // rows)
    back = hops * rows
    segment = segments[0]
    kv_width = KVH * HD
    step_cols = step_proj.shape[1]

    block = di // ring.unit
    index = jnp.stack(
        [block ^ m for m in LOW] + [block ^ m ^ 1 for m in LOW] + [lax.rem(ti + nt - s, nt) for s in range(nt)]
    ).astype(jnp.int32)

    start = ti * rows
    normed, normed_t, cot_t, scale1 = simple_call(
        norm_kernel,
        "norm_in",
        (hidden, cotangent, norm_gain[None, :]),
        (sds((rows, width), bf16), sds((width, rows), bf16), sds((width, rows), bf16), sds((rows, 1), f32)),
    )
    halo = ring.line(normed[rows - HALO :], 1)
    cosine, sine = rope_tables(rows, start)

    step_wide = jnp.zeros((step_proj.shape[0], LANE), bf16)
    step_wide = lax.dynamic_update_slice(step_wide, step_proj, (0, ti * step_cols))
    shared = jnp.concatenate([key_proj, value_proj, state_proj], axis=1)
    quarter = shared.shape[1] // nt
    shared_part = lax.dynamic_slice_in_dim(shared, ti * quarter, quarter, 1)
    widths1 = (query_proj.shape[1], LANE, input_inner.shape[1], quarter)
    widths2 = (gate_inner.shape[1], attn_out_proj.shape[0], mamba_out.shape[0])
    stages = {}

    def note(stage, values):
        stages[stage] = stages.get(stage, []) + list(values)
        return values

    def follow(stage, values):
        return after(values, *([stages[2]] if stage == 0 else [sides1] if stage == 1 else []))

    pack1 = pack((query_proj, step_wide, input_inner, shared_part), (False,) * 4)
    sides1 = ring.gather(pack1, note)
    pack2 = pack((gate_inner, attn_out_proj, mamba_out), (False, True, True))
    sides2 = ring.gather(pack2, follow)
    ffn_pack = pack((ffn_gate, ffn_up, ffn_down), (False, False, True))
    (ffn_pack,) = after([ffn_pack], *stages[FFN_AFTER]) if FFN_AFTER else [ffn_pack]
    w_ffn = lax.all_gather(ffn_pack, ("dp", "tensor"), axis=0, tiled=True)
    w_ffn = w_ffn.reshape(ring.nd, nt, *ffn_pack.shape)
    w_q, w_step, w_x, w_shared, u, query8, kv_own, dt_raw = project(
        index, sides1, widths1, (widths1[0] * nt, LANE, widths1[2] * nt, quarter * nt), normed, halo, cosine, sine
    )
    w_z, w_ao, w_mo = assemble(index, sides2, widths2, tuple(w * nt for w in widths2))

    padded = jnp.concatenate([jnp.full((back,), -1, jnp.int32), segment])
    seg_keys = lax.dynamic_slice_in_dim(padded, start, back + rows)
    seg_own = seg_keys[back:]
    seg_col, seg_row = seg_own[:, None], seg_own[None, :]
    chunks = rows // SPAN
    grouped = seg_own.reshape(chunks, SPAN)
    before = jnp.concatenate([seg_keys[back - 1 : back], grouped[:-1, -1]])
    carry_in = (grouped == before[:, None]).astype(f32).reshape(rows)
    in_last = (grouped == grouped[:, -1:]).astype(f32).reshape(rows)
    keeps = [(seg_keys[back - j : back - j + rows] == seg_own).astype(f32) for j in range(KCONV)]
    zero = jnp.zeros((rows,), f32)
    meta = jnp.stack(keeps + [carry_in, in_last, zero, zero], axis=1)
    first_tokens = seg_own.reshape(rows // QB, QB)[:, 0]
    doc_start = jnp.sum((segment[None, :] < first_tokens[:, None]).astype(jnp.int32), axis=1)
    first_block = (jnp.maximum(doc_start - (start - back), 0) // KB).astype(jnp.int32)

    seg_after = jnp.concatenate([segment, jnp.full((KCONV,), -2, jnp.int32)])
    keeps_after = [(lax.dynamic_slice_in_dim(seg_after, start + j, rows) == seg_own).astype(f32) for j in range(KCONV)]
    keeps_after = jnp.stack(keeps_after + [zero] * 4, axis=1)
    kvs = [ring.line(kv_own, s) for s in range(hops, 0, -1)] + [kv_own]

    taps = jnp.concatenate([conv_weight, conv_bias[None, :], jnp.zeros((3, INNER + 2 * NS), f32)], axis=0)
    rate = -jnp.exp(decay_log)
    heads = jnp.pad(jnp.stack([step_bias, rate]), ((0, 6), (0, LANE - MH)))
    skip = jnp.broadcast_to(jnp.repeat(skip_gain, MP)[None, :], (8, INNER))
    spread = np.arange(LANE)[:, None] == np.arange(INNER)[None, :] // MP
    spread2 = jnp.asarray(np.concatenate([spread, spread], axis=0), bf16)
    gather2 = jnp.asarray(np.concatenate([spread.T, spread.T], axis=0), bf16)

    mix, dt, cum, cumt, ec, fw, g, final = mamba_pre(u, taps, meta, dt_raw, heads, spread2)
    carries = [ring.line(final, s) for s in range(1, hops + 1)]
    attended, lse = attn_fwd(first_block, query8, seg_row, seg_keys[:, None], kvs)
    z_gate = dot(normed, w_z)
    gated, full, states = mamba_fwd(
        mix, dt, cum, cumt, ec, fw, g, seg_col, seg_row, z_gate, skip, spread2, carries
    )
    residual, normed2, normed2_t, scale2 = simple_call(
        middle_kernel,
        "middle",
        (attended, gated, w_ao, w_mo, hidden, ffn_gain[None, :]),
        (sds((rows, width), f32), sds((rows, width), bf16), sds((width, rows), bf16), sds((rows, 1), f32)),
        2 * rows * width * (INNER + QH * HD),
    )

    ffn_grads, output, d_normed2 = ffn(index, w_ffn, normed2, normed2_t, cotangent, cot_t, residual)
    ffn_grads = lax.psum_scatter(ffn_grads, "dp", scatter_dimension=0, tiled=True)
    units = ffn_gate.shape[1]
    g_ffn = ring.total([ffn_grads[:, s * 3 * units : (s + 1) * 3 * units] for s in range(nt)])
    d_residual, d_mixer_t, d_gated, d_attended, ffn_gain_grad = simple_call(
        after_ffn_kernel,
        "after_ffn",
        (d_normed2, residual, scale2, ffn_gain[None, :], cotangent, w_ao, w_mo),
        (sds((rows, width), f32), sds((width, rows), bf16), sds((rows, INNER), bf16), sds((rows, QH * HD), bf16),
         sds((8, width), f32)),
        2 * rows * width * (INNER + QH * HD),
    )
    ffn_gain_grad = ffn_gain_grad[0]

    dy, d_z, back_state = mamba_bpre(d_gated, z_gate, full, mix, ec, g, spread2)
    d_carries = [ring.line(back_state, -s) for s in range(1, hops + 1)]
    d_q, *d_kvs = attn_bwd(
        first_block, query8, d_attended, attended, lse, seg_row, seg_keys[:, None], cosine, sine, kvs
    )
    came = [ring.line(d_kvs[hops - s], -s) for s in range(1, hops + 1)]
    d_kv = simple_call(kv_back_kernel, "kv_back", (cosine, sine, d_kvs[-1], *came), sds(kv_own.shape, bf16))

    plan2 = (
        (0, 0, widths2[1], "part"),
        (0, 1, widths2[2], "part"),
        (1, 2, widths2[0], "part"),
        (1, 3, widths1[0], "part"),
    )
    grads2 = ring.collect(
        ring.scatter(*weight_grads(index, (d_mixer_t, normed_t), (attended, gated, d_z, d_q), plan2))
    )

    d_pre, d_step, conv_grads, small = mamba_bwd(
        mix, dt, cum, cumt, ec, fw, g, seg_col, seg_row, dy, states, u, taps, meta, skip, heads, spread2, gather2, d_carries
    )
    d_after = ring.line(d_pre[:8], -1)
    d_x, d_shared = simple_call(
        conv_back_kernel,
        "conv_back",
        (d_pre, d_after, taps, keeps_after, d_kv),
        (sds((rows, INNER), bf16), sds((rows, quarter * nt), bf16)),
    )

    d_x, d_shared = after([d_x, d_shared], ffn_grads)
    plan1 = ((0, 0, widths1[2], "part"), (0, 1, LANE, "all"), (0, 2, quarter, "fixed"))
    parts = ring.scatter(*weight_grads(index, (normed_t,), (d_x, d_step, d_shared), plan1))
    common = widths1[2] + LANE
    shared_sum = jnp.concatenate([part[:, common:] for part in parts], axis=1)
    shared_sum = ring.unblock(shared_sum)
    piece = shared_sum.shape[0] // nt
    parts = [part[:, :common] for part in parts]
    rows_of = []
    for s in range(nt):
        mine = lax.dynamic_slice_in_dim(shared_sum, lax.rem(ti + nt - s, nt) * piece, piece, 0)
        rows_of.append(jnp.concatenate([mine[:, i * quarter : (i + 1) * quarter] for i in range(nt)], axis=0))
    if ring.unit == 1:
        total = ring.total([jnp.concatenate(both, axis=1) for both in zip(parts, rows_of)])
        grads1, g_shared = total[:, :common], total[:, common:]
    else:
        grads1, g_shared = ring.collect(parts), ring.total(rows_of)
    g_shared = jnp.concatenate([g_shared[i * piece : (i + 1) * piece] for i in range(nt)], axis=1)

    d_normed = (
        dot(d_q, w_q, NT) + dot(d_z, w_z, NT) + dot(d_x, w_x, NT) + dot(d_shared, w_shared, NT) + dot(d_step, w_step, NT)
    )
    d_hid_norm, norm_gain_grad = rms_back(d_normed, hidden.astype(f32), scale1, norm_gain[None, :])
    hidden_grad = d_residual + d_hid_norm

    pieces = [norm_gain_grad, ffn_gain_grad, conv_grads[: KCONV + 1].reshape(-1), small[:3, :MH].reshape(-1)]
    vector = jnp.concatenate(pieces)
    size = vector.shape[0]
    vector = jnp.pad(vector, (0, -size % 1024)).reshape(-1, LANE)
    vector = ring.all_sum(vector).reshape(-1)
    at = 2 * width
    conv_sum = vector[at : at + (KCONV + 1) * (INNER + 2 * NS)].reshape(KCONV + 1, INNER + 2 * NS)
    small_sum = vector[size - 3 * MH : size].reshape(3, MH)

    def cut(value, *sizes):
        outs, at = [], 0
        for size in sizes:
            outs.append(value[:, at : at + size])
            at += size
        return outs

    g_fg, g_fu, g_fd = cut(g_ffn, units, units, units)
    g_ao, g_mo, g_z, g_q = cut(grads2, widths2[1], widths2[2], widths2[0], widths1[0])
    g_x, g_step_wide = cut(grads1, widths1[2], LANE)
    g_step = lax.dynamic_slice_in_dim(g_step_wide, ti * step_cols, step_cols, 1)
    return (
        output,
        hidden_grad,
        vector[:width],
        vector[width : 2 * width],
        g_q,
        g_shared[:, :kv_width],
        g_shared[:, kv_width : 2 * kv_width],
        g_ao.T,
        g_z,
        g_x,
        g_shared[:, 2 * kv_width :],
        g_step,
        g_mo.T,
        conv_sum[:KCONV],
        conv_sum[KCONV],
        small_sum[0],
        small_sum[1],
        small_sum[2],
        g_fg,
        g_fu,
        g_fd.T,
    )


def solution(mesh):
    in_specs = (
        P(("dp", "tensor"), None),
        P("dp", None),
        P(("dp", "tensor"), None),
        P(),
        P(),
        P("dp", "tensor"),
        P("dp", None),
        P("dp", None),
        P("tensor", "dp"),
        P("dp", "tensor"),
        P("dp", "tensor"),
        P("dp", None),
        P("dp", "tensor"),
        P("tensor", "dp"),
        P(),
        P(),
        P(),
        P(),
        P(),
        P("dp", "tensor"),
        P("dp", "tensor"),
        P("tensor", "dp"),
    )
    out_specs = (
        P(("dp", "tensor"), None),
        P(("dp", "tensor"), None),
        P(),
        P(),
        P("dp", "tensor"),
        P(("dp", "tensor"), None),
        P(("dp", "tensor"), None),
        P("tensor", "dp"),
        P("dp", "tensor"),
        P("dp", "tensor"),
        P(("dp", "tensor"), None),
        P("dp", "tensor"),
        P("tensor", "dp"),
        P(),
        P(),
        P(),
        P(),
        P(),
        P("dp", "tensor"),
        P("dp", "tensor"),
        P("tensor", "dp"),
    )
    return jax.shard_map(
        functools.partial(per_device, mesh), mesh=mesh, in_specs=in_specs, out_specs=out_specs, check_vma=False
    )
```

time: 818 us -> 524 us (0.64)
  other arithmetic: 170 us -> 28.4 us
  Pallas kernels: 54.4 us -> 159 us
  local copies, waits for them, and re-layouts: 128 us -> 35.6 us
  matrix products: 88 us -> 14.4 us
  waiting for transfers between devices: 243 us -> 175 us
  starting transfers between devices: 111 us -> 86.5 us
    concatenate x64 -> x8, other arithmetic: 137 us -> 4.05 us  [the longest x1 1.41 us: per_device(): shared = jnp.concatenate([key_proj, value_proj, state_proj], axis=1)]
    pallas_call x4 -> x25, Pallas kernels: 45.4 us -> 150 us  [the longest x8 34.1 us: simple_call(): pl.pallas_call(kernel, grid=(1,), out_shape=outs, in_specs=wholes(arrays)...]
    dot_general x41 -> x6, matrix products: 88 us -> 14.4 us  [dot(): return lax.dot_general(a, b, dims, preferred_element_type=f32)]
    ppermute x58 -> x29, waiting for transfers between devices: 164 us -> 108 us  [the longest x26 105 us: dp(): return lax.ppermute(value, 'dp', [(i, i ^ step) for i in range(self.nd)])]
    unnamed x564 -> x191, local copies, waits for them, and re-layouts: 67.8 us -> 21 us
    slice x66 -> x17, local copies, waits for them, and re-layouts: 26.1 us -> 4.25 us  [the longest x1 1.06 us: per_device(): ffn_grads[:, s * 3 * units:(s + 1) * 3 * units]]
    ppermute x13 -> x10, waiting for transfers between devices: 25.4 us -> 5.48 us  [line(): lax.ppermute(value, 'tensor', [(i, i + s) for i in range(n) if 0 <= i + s...]
    ppermute x33 -> x18, starting transfers between devices: 48.8 us -> 31.8 us  [shift(): return lax.ppermute(value, 'tensor', [(i, (i + s) % n) for i in range(n)])]
  transfers between devices with their start and end apart: 104 -> 59, of which waited for: 41 -> 20; matrix products, arithmetic and copies ran while one was open for 40% -> 11% of each run, Pallas kernels for 6% -> 23%
where the time goes in v2:
time: 524 us; the launch traced here: 515 us
  waiting for transfers between devices  175 us (33%)
  Pallas kernels  159 us (30%)
  starting transfers between devices  86.5 us (17%)
  local copies, waits for them, and re-layouts  35.6 us (7%)
  other arithmetic  28.4 us (5%)
  between operations  15.9 us (3%)
  matrix products  14.4 us (3%)
    ppermute x26, waiting for transfers between devices, dp(): return lax.ppermute(value, 'dp', [(i, i ^ step) for i in range(self.nd)])  105 us
    ppermute x18, waiting for transfers between devices, shift(): return lax.ppermute(value, 'tensor', [(i, (i + s) % n) for i in range(n)])  61.4 us
    pallas_call x8, Pallas kernels, simple_call(): pl.pallas_call(kernel, grid=(1,), out_shape=outs, in_specs=wholes(arrays)...  34.1 us
    ppermute x18, starting transfers between devices, shift(): return lax.ppermute(value, 'tensor', [(i, (i + s) % n) for i in range(n)])  31.8 us
    pallas_call x1, Pallas kernels, ffn(): pl.pallas_call(ffn_kernel, grid_spec=pltpu.PrefetchScalarGridSpec(num_sca...  28.6 us
    ppermute x10, starting transfers between devices, line(): lax.ppermute(value, 'tensor', [(i, i + s) for i in range(n) if 0 <= i + s...  27.8 us
    pallas_call x1, Pallas kernels, mamba_bwd(): pl.pallas_call(mamba_bwd_kernel, grid=(n,), in_specs=[rev(width), rev(LAN...  24.5 us
    ppermute x26, starting transfers between devices, dp(): return lax.ppermute(value, 'dp', [(i, i ^ step) for i in range(self.nd)])  24.2 us
  transfers between devices with their start and end apart: 59, of which 20 were waited for; matrix products, arithmetic and copies ran while one was open for 11% of the time, Pallas kernels for 23%

profile of v2, /device:TPU:0, one launch (start us, length us, event | category | flops | bytes accessed | tf_op | source)
XLA Modules:
  0.0 515.1 jit_solution(1928114517250892669)
XLA Ops:
  11.3 3.2 collective-permute-start
  14.6 2.6 collective-permute-start.1
  20.4 2.3 collective-permute-done.refs_1_
  22.8 7.6 %collective-permute-done.1.refs_0_ = bf16[128,768]{1,0:T(8,128)(2,1)S(1)} collective-permute-done((bf16[128,768]{1,0:T(8,128)(2,1)}, bf16[128,768]{1,0:T(8,128)(2,1)S(1)}, u32[]{:S(2)}, u32[]{:S(2)}) %collective-permute-start.1) | collective-permute-done | bytes 196640 | tf_op jit(solution)/shard_map/ppermute | solution.py:596
  33.5 7.9 %collective-permute-done.7.refs_2_ = bf16[2,128,768]{2,1,0:T(8,128)(2,1)S(1)} collective-permute-done((bf16[2,128,768]{2,1,0:T(8,128)(2,1)S(1)}, bf16[2,128,768]{2,1,0:T(8,128)(2,1)S(1)}, u32[]{:S(2)}, u32[]{:S(2)}) %collective-permute-start.7) | collective-permute-done | bytes 393248 | tf_op jit(solution)/shard_map/ppermute | solution.py:592
  47.5 3.9 collective-permute-start.15
  54.0 17.1 %collective-permute-done.15.refs_0_ = bf16[128,896]{1,0:T(8,128)(2,1)S(1)} collective-permute-done((bf16[128,896]{1,0:T(8,128)(2,1)}, bf16[128,896]{1,0:T(8,128)(2,1)S(1)}, u32[]{:S(2)}, u32[]{:S(2)}) %collective-permute-start.15) | collective-permute-done | bytes 229408 | tf_op jit(solution)/shard_map/ppermute | solution.py:596
  71.7 4.1 norm_in.1
  76.7 14.7 %collective-permute-done.16.refs_1_ = bf16[128,896]{1,0:T(8,128)(2,1)S(1)} collective-permute-done((bf16[128,896]{1,0:T(8,128)(2,1)}, bf16[128,896]{1,0:T(8,128)(2,1)S(1)}, u32[]{:S(2)}, u32[]{:S(2)}) %collective-permute-start.16) | collective-permute-done | bytes 229408 | tf_op jit(solution)/shard_map/ppermute | solution.py:596
  96.9 11.4 %collective-permute-done.18.refs_2_ = bf16[2,128,896]{2,1,0:T(8,128)(2,1)S(1)} collective-permute-done((bf16[2,128,896]{2,1,0:T(8,128)(2,1)S(1)}, bf16[2,128,896]{2,1,0:T(8,128)(2,1)S(1)}, u32[]{:S(2)}, u32[]{:S(2)}) %collective-permute-start.18) | collective-permute-done | bytes 458784 | tf_op jit(solution)/shard_map/ppermute | solution.py:592
  118.2 30.9 %collective-permute-done.22.refs_5_ = bf16[2,2,128,896]{3,2,1,0:T(8,128)(2,1)} collective-permute-done((bf16[2,2,128,896]{3,2,1,0:T(8,128)(2,1)}, bf16[2,2,128,896]{3,2,1,0:T(8,128)(2,1)}, u32[]{:S(2)}, u32[]{:S(2)}) %collective-permute-start.22) | collective-permute-done | bytes 917536 | tf_op jit(solution)/shard_map/ppermute | solution.py:592
  150.7 9.8 %project.1 = (bf16[1024,512]{1,0:T(8,128)(2,1)}, bf16[1024,128]{1,0:T(8,128)(2,1)}, bf16[1024,1536]{1,0:T(8,128)(2,1)}, bf16[1024,512]{1,0:T(8,128)(2,1)}, f32[5...) custom-call(s32[12]{0:T(128)} %stack.115.index_ref, ...), custom_call_target="tpu_custom_call" | custom-call | flops 2000000000 | bytes 4000000 | tf_op jit(solution)/shard_map/project/pallas_call | solution.py:770
  162.7 5.5 %collective-permute-done.12.refs_0_ = bf16[512,256]{1,0:T(8,128)(2,1)S(1)} collective-permute-done((bf16[512,256]{1,0:T(8,128)(2,1)}, bf16[512,256]{1,0:T(8,128)(2,1)S(1)}, u32[]{:S(2)}, u32[]{:S(2)}) %collective-permute-start.12) | collective-permute-done | bytes 262176 | tf_op jit(solution)/shard_map/ppermute | solution.py:600
  168.9 6.5 %collective-permute-start.13 = (bf16[512,256]{1,0:T(8,128)(2,1)}, bf16[512,256]{1,0:T(8,128)(2,1)S(1)}, u32[]{:S(2)}, u32[]{:S(2)}) collective-permute-start(bf16[512,256]{1,0:T(8,128)(2,1)} %get-tuple-element.93.refs_2_), channel_id=1, source_target_pairs={{0,1},{1,2},{2,3},{4,5},{5,6},{6,7},{8,9},{9,10},{10,11},{12,13},{... | collective-permute-start | bytes 786440 | tf_op jit(solution)/shard_map/ppermute | solution.py:600
  179.4 5.8 %mamba_pre.1 = (bf16[512,1792]{1,0:T(8,128)(2,1)S(1)}, f32[512,128]{1,0:T(8,128)S(1)}, f32[512,128]{1,0:T(8,128)S(1)}, f32[32,512]{1,0:T(8,128)S(1)}, f32[512,12...) custom-call(f32[528,1792]{1,0:T(8,128)S(1)} %copy-done.4, ...), custom_call_target="tpu_custom_call" | custom-call | flops 2000000000 | bytes 4000000 | tf_op jit(solution)/shard_map/mamba_pre/pallas_call | solution.py:322
  187.3 6.6 %attn_fwd.1 = (bf16[512,512]{1,0:T(8,128)(2,1)S(1)}, f32[8,512]{1,0:T(8,128)S(1)}) custom-call(s32[4]{0:T(128)S(1)} %and_select_fusion.first_ref, bf16[512,512]{1,0:T(8,128)(2,1)S(1)} %copy-done.34, s32[1,512]{1,0:T(1,128)S(1)} %bitcast.89, s32[1536,1]{1,0:T(8,128)S(1)} %broadcast_in_dim.53.segk_ref, bf16[512,256]{1,0:T(8,128)(2,1)S(1)} %copy-done.42, ...), custom_call_target="tpu_custom_call" | custom-call | flops 2000000000 | bytes 4000000 | tf_op jit(solution)/shard_map/attn_fwd/pallas_call | solution.py:200
  194.7 10.0 %collective-permute-start.26 = (bf16[144,1536]{1,0:T(8,128)(2,1)S(1)}, bf16[144,1536]{1,0:T(8,128)(2,1)S(1)}, u32[]{:S(2)}, u32[]{:S(2)}) collective-permute-start(bf16[144,1536]{1,0:T(8,128)(2,1)S(1)} %get-tuple-element.114), channel_id=1, source_target_pairs={{0,2},{1,3},{4,6},{5,7},{8,10},{9,11},{12,14},{13,15},{16,18},{17,... | collective-permute-start | bytes 1327112 | tf_op jit(solution)/shard_map/ppermute | solution.py:600
  204.8 6.7 %assemble.1 = (bf16[1024,1536]{1,0:T(8,128)(2,1)}, bf16[1024,512]{1,0:T(8,128)(2,1)}, bf16[1024,1536]{1,0:T(8,128)(2,1)}) custom-call(s32[12]{0:T(128)S(1)} %copy-done.30, bf16[2,2,128,896]{3,2,1,0:T(8,128)(2,1)} %join.14.refs_0_, bf16[2,2,128,896]{3,2,1,0:T(8,128)(2,1)} %collective-permute-done.19.refs_1_, ...), custom_call_target="tpu_custom_call" | custom-call | flops 2000000000 | bytes 4000000 | tf_op jit(solution)/shard_map/assemble/pallas_call | solution.py:723
  211.5 3.7 fusion.38.z_ref
  215.3 6.7 %mamba_fwd.1 = (bf16[512,1536]{1,0:T(8,128)(2,1)S(1)}, bf16[512,1536]{1,0:T(8,128)(2,1)S(1)}, bf16[4,128,1536]{2,1,0:T(8,128)(2,1)S(1)}) custom-call(bf16[512,1792]{1,0:T(8,128)(2,1)S(1)} %get-tuple-element.97.mix_ref.cm_ref, f32[512,128]{1,0:T(8,128)S(1)} %get-tuple-element.98.dt_ref, f32[512,128]{1,0:T(8,128)S(1)} %get-tuple-element.99.cum_ref, ...), custom_call_target="tpu_custom_call" | custom-call | flops 2000000000 | bytes 4000000 | tf_op jit(solution)/shard_map/mamba_fwd/pallas_call | solution.py:390
  225.5 7.6 %middle.1 = (f32[512,1024]{1,0:T(8,128)}, bf16[512,1024]{1,0:T(8,128)(2,1)}, bf16[1024,512]{1,0:T(8,128)(2,1)}, f32[512,1]{1,0:T(8,128)}) custom-call(bf16[512,512]{1,0:T(8,128)(2,1)} %copy-done.49, bf16[512,1536]{1,0:T(8,128)(2,1)} %copy-done.33, bf16[1024,512]{1,0:T(8,128)(2,1)} %get-tuple-element.116.wa_ref, ...), custom_call_target="tpu_custom_call" | custom-call | flops 2000000000 | bytes 4000000 | tf_op jit(solution)/shard_map/middle/pallas_call | solution.py:879
  233.1 28.6 %ffn.1 = (bf16[1024,6144]{1,0:T(8,128)(2,1)}, bf16[512,1024]{1,0:T(8,128)(2,1)}, f32[512,1024]{1,0:T(8,128)}) custom-call(s32[12]{0:T(128)} %stack.115.index_ref, bf16[8,4,128,1536]{3,2,1,0:T(8,128)(2,1)} %bitcast.93, bf16[512,1024]{1,0:T(8,128)(2,1)} %get-tuple-element.118.n_ref, bf16[1024,512]{1,0:T(8,128)(2,1)} %get-tuple-element.119.nt_ref, ...), custom_call_target="tpu_custom_call" | custom-call | flops 2000000000 | bytes 4000000 | tf_op jit(solution)/shard_map/ffn/pallas_call | solution.py:971
  261.8 8.6 %after_ffn.1 = (f32[512,1024]{1,0:T(8,128)}, bf16[1024,512]{1,0:T(8,128)(2,1)}, bf16[512,1536]{1,0:T(8,128)(2,1)}, bf16[512,512]{1,0:T(8,128)(2,1)}, f32[8,1024]{1,0:T(8,128)}) custom-call(f32[512,1024]{1,0:T(8,128)} %get-tuple-element.123.dn_ref, f32[512,1024]{1,0:T(8,128)} %get-tuple-element.121.res_ref, f32[512,1]{1,0:T(8,128)} %get-tuple-element.124.scale_ref, ...), custom_call_target="tpu_custom_call" | custom-call | flops 2000000000 | bytes 4000000 | tf_op jit(solution)/shard_map/after_ffn/pallas_call | solution.py:879
  271.9 3.2 mamba_bpre.1
  275.2 9.2 %attn_bwd.1 = (bf16[512,512]{1,0:T(8,128)(2,1)S(1)}, bf16[512,256]{1,0:T(8,128)(2,1)S(1)}, bf16[512,256]{1,0:T(8,128)(2,1)S(1)}, f32[512,256]{1,0:T(8,128)S(1)}) custom-call(s32[4]{0:T(128)S(1)} %and_select_fusion.first_ref, bf16[512,512]{1,0:T(8,128)(2,1)S(1)} %copy-done.35, bf16[512,512]{1,0:T(8,128)(2,1)S(1)} %copy-done.36, ...), custom_call_target="tpu_custom_call" | custom-call | flops 2000000000 | bytes 4000000 | tf_op jit(solution)/shard_map/attn_bwd/pallas_call | solution.py:217
  286.1 13.5 %weight_grads.2 = (bf16[4,4,128,1024]{3,2,1,0:T(8,128)(2,1)}, bf16[4,4,128,1024]{3,2,1,0:T(8,128)(2,1)}) custom-call(s32[12]{0:T(128)} %stack.115.index_ref, bf16[1024,512]{1,0:T(8,128)(2,1)} %get-tuple-element.153.refs_0_, bf16[1024,512]{1,0:T(8,128)(2,1)} %get-tuple-element.154.refs_1_.refs_0_, bf16[512,512]{1,0:T(8,128)(2,1)} %copy-done.49, ...), custom_call_target="tpu_custom_call" | custom-call | flops 2000000000 | bytes 4000000 | tf_op jit(solution)/shard_map/weight_grads/pallas_call | solution.py:923
  299.7 7.3 %collective-permute-done.38 = bf16[4,4,128,1024]{3,2,1,0:T(8,128)(2,1)S(1)} collective-permute-done((bf16[4,4,128,1024]{3,2,1,0:T(8,128)(2,1)}, bf16[4,4,128,1024]{3,2,1,0:T(8,128)(2,1)S(1)}, u32[]{:S(2)}, u32[]{:S(2)}) %collective-permute-start.38) | collective-permute-done | bytes 4194336 | tf_op jit(solution)/shard_map/ppermute | solution.py:592
  307.0 4.6 add_convert_fusion.3
  311.6 4.6 collective-permute-start.39
  322.9 5.0 fusion.40
  327.9 29.5 %collective-permute-done.39 = bf16[2,2,128,1024]{3,2,1,0:T(8,128)(2,1)} collective-permute-done((bf16[2,2,128,1024]{3,2,1,0:T(8,128)(2,1)}, bf16[2,2,128,1024]{3,2,1,0:T(8,128)(2,1)}, u32[]{:S(2)}, u32[]{:S(2)}) %collective-permute-start.39) | collective-permute-done | bytes 1048608 | tf_op jit(solution)/shard_map/ppermute | solution.py:592
  366.5 24.5 %mamba_bwd.1 = (f32[512,1792]{1,0:T(8,128)}, bf16[512,128]{1,0:T(8,128)(2,1)}, f32[8,1792]{1,0:T(8,128)}, f32[8,128]{1,0:T(8,128)}) custom-call(bf16[512,1792]{1,0:T(8,128)(2,1)} %copy-done, f32[512,128]{1,0:T(8,128)} %copy-done.14, f32[512,128]{1,0:T(8,128)} %copy-done.15, f32[32,512]{1,0:T(8,128)} %copy-done.25, f32[512,128]{1,0:T(8,128)} %copy-done.5, ...), custom_call_target="tpu_custom_call" | custom-call | flops 2000000000 | bytes 4000000 | tf_op jit(solution)/shard_map/mamba_bwd/pallas_call | solution.py:555
  394.1 5.7 %collective-permute-start.41 = (bf16[128,1024]{1,0:T(8,128)(2,1)}, bf16[128,1024]{1,0:T(8,128)(2,1)S(1)}, u32[]{:S(2)}, u32[]{:S(2)}) collective-permute-start(bf16[128,1024]{1,0:T(8,128)(2,1)} %fusion.10), channel_id=1, source_target_pairs={{0,3},{1,0},{2,1},{3,2},{4,7},{5,4},{6,5},{7,6},{8,11},{9,8},{10,9... | collective-permute-start | bytes 786440 | tf_op jit(solution)/shard_map/ppermute | solution.py:596
  402.1 2.3 kv_back.1.dkv_ref
  405.1 6.2 %conv_back.1 = (bf16[512,1536]{1,0:T(8,128)(2,1)}, bf16[512,512]{1,0:T(8,128)(2,1)}) custom-call(f32[512,1792]{1,0:T(8,128)} %get-tuple-element.137.dpre_ref, f32[8,1792]{1,0:T(8,128)} %copy-done.90, f32[8,1792]{1,0:T(8,128)} %maximum_maximum_fusion.3.tap_ref, f32[512,8]{1,0:T(8,128)} %copy.124.keep_ref, bf16[512,256]{1,0:T(8,128)(2,1)} %kv_back.1.dkv_ref), custom_call_target="tpu_custom_call" | custom-call | flops 2000000000 | bytes 4000000 | tf_op jit(solution)/shard_map/conv_back/pallas_call | solution.py:879
  411.4 10.1 %collective-permute-done.44 = bf16[128,1024]{1,0:T(8,128)(2,1)} collective-permute-done((bf16[128,1024]{1,0:T(8,128)(2,1)}, bf16[128,1024]{1,0:T(8,128)(2,1)}, u32[]{:S(2)}, u32[]{:S(2)}) %collective-permute-start.44) | collective-permute-done | bytes 262176 | tf_op jit(solution)/shard_map/ppermute | solution.py:596
  425.6 8.3 %weight_grads.3 = (bf16[4,4,128,640]{3,2,1,0:T(8,128)(2,1)}, bf16[4,4,128,640]{3,2,1,0:T(8,128)(2,1)}) custom-call(s32[12]{0:T(128)} %stack.115.index_ref, bf16[1024,512]{1,0:T(8,128)(2,1)} %get-tuple-element.154.refs_1_.refs_0_, bf16[512,1536]{1,0:T(8,128)(2,1)} %get-tuple-element.144.refs_1_, bf16[512,128]{1,0:T(8,128)(2,1)} %get-tuple-element.148.refs_2_, ...), custom_call_target="tpu_custom_call" | custom-call | flops 2000000000 | bytes 4000000 | tf_op jit(solution)/shard_map/weight_grads/pallas_call | solution.py:923
  437.7 2.4 fusion.4
  450.9 2.1 collective-permute-start.35
  453.0 3.2 collective-permute-start.36
  457.1 3.4 fusion.2
  462.6 3.2 add_convert_fusion.7
  469.8 9.8 %collective-permute-done.47 = bf16[2,2,128,640]{3,2,1,0:T(8,128)(2,1)S(1)} collective-permute-done((bf16[2,2,128,640]{3,2,1,0:T(8,128)(2,1)S(1)}, bf16[2,2,128,640]{3,2,1,0:T(8,128)(2,1)S(1)}, u32[]{:S(2)}, u32[]{:S(2)}) %collective-permute-start.47) | collective-permute-done | bytes 655392 | tf_op jit(solution)/shard_map/ppermute | solution.py:592
  480.5 3.3 collective-permute-done.49
  484.3 2.7 collective-permute-done.55
  488.4 2.7 collective-permute-done.50
  491.4 3.3 collective-permute-start.51
  499.7 5.3 %collective-permute-done.52 = bf16[128,640]{1,0:T(8,128)(2,1)S(1)} collective-permute-done((bf16[128,640]{1,0:T(8,128)(2,1)S(1)}, bf16[128,640]{1,0:T(8,128)(2,1)S(1)}, u32[]{:S(2)}, u32[]{:S(2)}) %collective-permute-start.52) | collective-permute-done | bytes 163872 | tf_op jit(solution)/shard_map/ppermute | solution.py:596
  (388 shorter events, 111.5 us)
Async XLA Ops:
  7.2 225.9 %all-gather.2.cloned.1.call-start = ((), (), s32[]{:S(2)}) async-start(), calls=%async_computation.1 | async-start | bytes 12976128 | tf_op jit(solution)/shard_map/all_gather | solution.py:1079
  11.3 11.4 %collective-permute-start = (bf16[128,768]{1,0:T(8,128)(2,1)}, bf16[128,768]{1,0:T(8,128)(2,1)S(1)}, u32[]{:S(2)}, u32[]{:S(2)}) collective-permute-start(bf16[128,768]{1,0:T(8,128)(2,1)} %pack.4.refs_0_), channel_id=1, source_target_pairs={{0,1},{1,2},{2,3},{3,0},{4,5},{5,6},{6,7},{7,4},{8,9},{9,10},{10,1... | collective-permute-start | bytes 589832 | tf_op jit(solution)/shard_map/ppermute | solution.py:596
  14.6 15.8 %collective-permute-start.1 = (bf16[128,768]{1,0:T(8,128)(2,1)}, bf16[128,768]{1,0:T(8,128)(2,1)S(1)}, u32[]{:S(2)}, u32[]{:S(2)}) collective-permute-start(bf16[128,768]{1,0:T(8,128)(2,1)} %pack.4.refs_0_), channel_id=1, source_target_pairs={{0,2},{1,3},{2,0},{3,1},{4,6},{5,7},{6,4},{7,5},{8,10},{9,11},{10,... | collective-permute-start | bytes 589832 | tf_op jit(solution)/shard_map/ppermute | solution.py:596
  17.2 13.2 %collective-permute-start.2 = (bf16[128,768]{1,0:T(8,128)(2,1)}, bf16[128,768]{1,0:T(8,128)(2,1)S(1)}, u32[]{:S(2)}, u32[]{:S(2)}) collective-permute-start(bf16[128,768]{1,0:T(8,128)(2,1)} %pack.4.refs_0_), channel_id=1, source_target_pairs={{0,3},{1,0},{2,1},{3,2},{4,7},{5,4},{6,5},{7,6},{8,11},{9,8},{10,9... | collective-permute-start | bytes 589832 | tf_op jit(solution)/shard_map/ppermute | solution.py:596
  30.4 395.2 %reduce-scatter.2.cloned.1.call-start = ((), (), s32[]{:S(2)}) async-start(), calls=%async_computation.2 | async-start | bytes 14155776 | tf_op jit(solution)/shard_map/reduce_scatter | solution.py:1131
  30.4 11.0 %collective-permute-start.7 = (bf16[2,128,768]{2,1,0:T(8,128)(2,1)S(1)}, bf16[2,128,768]{2,1,0:T(8,128)(2,1)S(1)}, u32[]{:S(2)}, u32[]{:S(2)}) collective-permute-start(bf16[2,128,768]{2,1,0:T(8,128)(2,1)S(1)} %join.9), channel_id=1, source_target_pairs={{0,16},{4,20},{8,24},{12,28},{16,0},{20,4},{24,8},{28,12},{1,17},{... | collective-permute-start | bytes 1179656 | tf_op jit(solution)/shard_map/ppermute | solution.py:592
  32.0 11.1 %collective-permute-start.3 = (bf16[2,128,768]{2,1,0:T(8,128)(2,1)S(1)}, bf16[2,128,768]{2,1,0:T(8,128)(2,1)S(1)}, u32[]{:S(2)}, u32[]{:S(2)}) collective-permute-start(bf16[2,128,768]{2,1,0:T(8,128)(2,1)S(1)} %join.8), channel_id=1, source_target_pairs={{0,8},{4,12},{8,0},{12,4},{16,24},{20,28},{24,16},{28,20},{1,9},{5... | collective-permute-start | bytes 1179656 | tf_op jit(solution)/shard_map/ppermute | solution.py:592
  41.5 29.5 %collective-permute-start.8 = (bf16[2,2,128,768]{3,2,1,0:T(8,128)(2,1)S(1)}, bf16[2,2,128,768]{3,2,1,0:T(8,128)(2,1)S(1)}, u32[]{:S(2)}, u32[]{:S(2)}) collective-permute-start(bf16[2,2,128,768]{3,2,1,0:T(8,128)(2,1)S(1)} %join.11.refs_4_), channel_id=1, source_target_pairs={{0,8},{4,12},{8,0},{12,4},{16,24},{20,28},{24,16},{28,20},{1,9},{5... | collective-permute-start | bytes 2359304 | tf_op jit(solution)/shard_map/ppermute | solution.py:592
  43.2 28.4 %collective-permute-start.4 = (bf16[2,2,128,768]{3,2,1,0:T(8,128)(2,1)S(1)}, bf16[2,2,128,768]{3,2,1,0:T(8,128)(2,1)S(1)}, u32[]{:S(2)}, u32[]{:S(2)}) collective-permute-start(bf16[2,2,128,768]{3,2,1,0:T(8,128)(2,1)S(1)} %join.10.refs_0_), channel_id=1, source_target_pairs={{0,16},{4,20},{8,24},{12,28},{16,0},{20,4},{24,8},{28,12},{1,17},{... | collective-permute-start | bytes 2359304 | tf_op jit(solution)/shard_map/ppermute | solution.py:592
  47.5 23.5 %collective-permute-start.15 = (bf16[128,896]{1,0:T(8,128)(2,1)}, bf16[128,896]{1,0:T(8,128)(2,1)S(1)}, u32[]{:S(2)}, u32[]{:S(2)}) collective-permute-start(bf16[128,896]{1,0:T(8,128)(2,1)} %pack.5.refs_0_), channel_id=1, source_target_pairs={{0,2},{1,3},{2,0},{3,1},{4,6},{5,7},{6,4},{7,5},{8,10},{9,11},{10,... | collective-permute-start | bytes 688136 | tf_op jit(solution)/shard_map/ppermute | solution.py:596
  52.1 19.5 %collective-permute-start.14 = (bf16[128,896]{1,0:T(8,128)(2,1)}, bf16[128,896]{1,0:T(8,128)(2,1)S(1)}, u32[]{:S(2)}, u32[]{:S(2)}) collective-permute-start(bf16[128,896]{1,0:T(8,128)(2,1)} %pack.5.refs_0_), channel_id=1, source_target_pairs={{0,1},{1,2},{2,3},{3,0},{4,5},{5,6},{6,7},{7,4},{8,9},{9,10},{10,1... | collective-permute-start | bytes 688136 | tf_op jit(solution)/shard_map/ppermute | solution.py:596
  54.0 38.8 %collective-permute-start.9 = (bf16[2,2,128,768]{3,2,1,0:T(8,128)(2,1)S(1)}, bf16[2,2,128,768]{3,2,1,0:T(8,128)(2,1)S(1)}, u32[]{:S(2)}, u32[]{:S(2)}) collective-permute-start(bf16[2,2,128,768]{3,2,1,0:T(8,128)(2,1)S(1)} %join.11.refs_4_), channel_id=1, source_target_pairs={{0,4},{4,0},{8,12},{12,8},{16,20},{20,16},{24,28},{28,24},{1,5},{5... | collective-permute-start | bytes 2359304 | tf_op jit(solution)/shard_map/ppermute | solution.py:592
  71.0 21.7 %collective-permute-start.5 = (bf16[2,2,128,768]{3,2,1,0:T(8,128)(2,1)S(1)}, bf16[2,2,128,768]{3,2,1,0:T(8,128)(2,1)S(1)}, u32[]{:S(2)}, u32[]{:S(2)}) collective-permute-start(bf16[2,2,128,768]{3,2,1,0:T(8,128)(2,1)S(1)} %join.10.refs_0_), channel_id=1, source_target_pairs={{0,4},{4,0},{8,12},{12,8},{16,20},{20,16},{24,28},{28,24},{1,5},{5... | collective-permute-start | bytes 2359304 | tf_op jit(solution)/shard_map/ppermute | solution.py:592
  71.1 21.7 %collective-permute-start.10 = (bf16[2,2,128,768]{3,2,1,0:T(8,128)(2,1)S(1)}, bf16[2,2,128,768]{3,2,1,0:T(8,128)(2,1)S(1)}, u32[]{:S(2)}, u32[]{:S(2)}) collective-permute-start(bf16[2,2,128,768]{3,2,1,0:T(8,128)(2,1)S(1)} %collective-permute-done.8.refs_5_), channel_id=1, source_target_pairs={{0,4},{4,0},{8,12},{12,8},{16,20},{20,16},{24,28},{28,24},{1,5},{5... | collective-permute-start | bytes 2359304 | tf_op jit(solution)/shard_map/ppermute | solution.py:592
  71.6 22.4 %collective-permute-start.6 = (bf16[2,2,128,768]{3,2,1,0:T(8,128)(2,1)S(1)}, bf16[2,2,128,768]{3,2,1,0:T(8,128)(2,1)}, u32[]{:S(2)}, u32[]{:S(2)}) collective-permute-start(bf16[2,2,128,768]{3,2,1,0:T(8,128)(2,1)S(1)} %collective-permute-done.4.refs_1_), channel_id=1, source_target_pairs={{0,4},{4,0},{8,12},{12,8},{16,20},{20,16},{24,28},{28,24},{1,5},{5... | collective-permute-start | bytes 2359304 | tf_op jit(solution)/shard_map/ppermute | solution.py:592
  71.7 19.7 %collective-permute-start.16 = (bf16[128,896]{1,0:T(8,128)(2,1)}, bf16[128,896]{1,0:T(8,128)(2,1)S(1)}, u32[]{:S(2)}, u32[]{:S(2)}) collective-permute-start(bf16[128,896]{1,0:T(8,128)(2,1)} %pack.5.refs_0_), channel_id=1, source_target_pairs={{0,3},{1,0},{2,1},{3,2},{4,7},{5,4},{6,5},{7,6},{8,11},{9,8},{10,9... | collective-permute-start | bytes 688136 | tf_op jit(solution)/shard_map/ppermute | solution.py:596
  91.4 58.7 %collective-permute-start.11 = (bf16[16,1024]{1,0:T(8,128)(2,1)S(1)}, bf16[16,1024]{1,0:T(8,128)(2,1)S(1)}, u32[]{:S(2)}, u32[]{:S(2)}) collective-permute-start(bf16[16,1024]{1,0:T(8,128)(2,1)S(1)} %slice.370), channel_id=1, source_target_pairs={{0,1},{1,2},{2,3},{4,5},{5,6},{6,7},{8,9},{9,10},{10,11},{12,13},{... | collective-permute-start | bytes 98312 | tf_op jit(solution)/shard_map/ppermute | solution.py:600
  94.0 14.4 %collective-permute-start.18 = (bf16[2,128,896]{2,1,0:T(8,128)(2,1)S(1)}, bf16[2,128,896]{2,1,0:T(8,128)(2,1)S(1)}, u32[]{:S(2)}, u32[]{:S(2)}) collective-permute-start(bf16[2,128,896]{2,1,0:T(8,128)(2,1)S(1)} %join.13), channel_id=1, source_target_pairs={{0,16},{4,20},{8,24},{12,28},{16,0},{20,4},{24,8},{28,12},{1,17},{... | collective-permute-start | bytes 1376264 | tf_op jit(solution)/shard_map/ppermute | solution.py:592
  94.9 16.3 %collective-permute-start.17 = (bf16[2,128,896]{2,1,0:T(8,128)(2,1)S(1)}, bf16[2,128,896]{2,1,0:T(8,128)(2,1)S(1)}, u32[]{:S(2)}, u32[]{:S(2)}) collective-permute-start(bf16[2,128,896]{2,1,0:T(8,128)(2,1)S(1)} %join.12), channel_id=1, source_target_pairs={{0,8},{4,12},{8,0},{12,4},{16,24},{20,28},{24,16},{28,20},{1,9},{5... | collective-permute-start | bytes 1376264 | tf_op jit(solution)/shard_map/ppermute | solution.py:592
  112.2 36.9 %collective-permute-start.22 = (bf16[2,2,128,896]{3,2,1,0:T(8,128)(2,1)}, bf16[2,2,128,896]{3,2,1,0:T(8,128)(2,1)}, u32[]{:S(2)}, u32[]{:S(2)}) collective-permute-start(bf16[2,2,128,896]{3,2,1,0:T(8,128)(2,1)} %join.15.refs_4_), channel_id=1, source_target_pairs={{0,8},{4,12},{8,0},{12,4},{16,24},{20,28},{24,16},{28,20},{1,9},{5... | collective-permute-start | bytes 2752520 | tf_op jit(solution)/shard_map/ppermute | solution.py:592
  113.7 35.9 %collective-permute-start.19 = (bf16[2,2,128,896]{3,2,1,0:T(8,128)(2,1)}, bf16[2,2,128,896]{3,2,1,0:T(8,128)(2,1)}, u32[]{:S(2)}, u32[]{:S(2)}) collective-permute-start(bf16[2,2,128,896]{3,2,1,0:T(8,128)(2,1)} %join.14.refs_0_), channel_id=1, source_target_pairs={{0,16},{4,20},{8,24},{12,28},{16,0},{20,4},{24,8},{28,12},{1,17},{... | collective-permute-start | bytes 2752520 | tf_op jit(solution)/shard_map/ppermute | solution.py:592
  149.1 45.6 %collective-permute-start.23 = (bf16[2,2,128,896]{3,2,1,0:T(8,128)(2,1)}, bf16[2,2,128,896]{3,2,1,0:T(8,128)(2,1)}, u32[]{:S(2)}, u32[]{:S(2)}) collective-permute-start(bf16[2,2,128,896]{3,2,1,0:T(8,128)(2,1)} %join.15.refs_4_), channel_id=1, source_target_pairs={{0,4},{4,0},{8,12},{12,8},{16,20},{20,16},{24,28},{28,24},{1,5},{5... | collective-permute-start | bytes 2752520 | tf_op jit(solution)/shard_map/ppermute | solution.py:592
  149.1 55.7 %collective-permute-start.24 = (bf16[2,2,128,896]{3,2,1,0:T(8,128)(2,1)}, bf16[2,2,128,896]{3,2,1,0:T(8,128)(2,1)}, u32[]{:S(2)}, u32[]{:S(2)}) collective-permute-start(bf16[2,2,128,896]{3,2,1,0:T(8,128)(2,1)} %collective-permute-done.22.refs_5_), channel_id=1, source_target_pairs={{0,4},{4,0},{8,12},{12,8},{16,20},{20,16},{24,28},{28,24},{1,5},{5... | collective-permute-start | bytes 2752520 | tf_op jit(solution)/shard_map/ppermute | solution.py:592
  149.6 55.2 %collective-permute-start.20 = (bf16[2,2,128,896]{3,2,1,0:T(8,128)(2,1)}, bf16[2,2,128,896]{3,2,1,0:T(8,128)(2,1)}, u32[]{:S(2)}, u32[]{:S(2)}) collective-permute-start(bf16[2,2,128,896]{3,2,1,0:T(8,128)(2,1)} %join.14.refs_0_), channel_id=1, source_target_pairs={{0,4},{4,0},{8,12},{12,8},{16,20},{20,16},{24,28},{28,24},{1,5},{5... | collective-permute-start | bytes 2752520 | tf_op jit(solution)/shard_map/ppermute | solution.py:592
  149.6 55.2 %collective-permute-start.21 = (bf16[2,2,128,896]{3,2,1,0:T(8,128)(2,1)}, bf16[2,2,128,896]{3,2,1,0:T(8,128)(2,1)}, u32[]{:S(2)}, u32[]{:S(2)}) collective-permute-start(bf16[2,2,128,896]{3,2,1,0:T(8,128)(2,1)} %collective-permute-done.19.refs_1_), channel_id=1, source_target_pairs={{0,4},{4,0},{8,12},{12,8},{16,20},{20,16},{24,28},{28,24},{1,5},{5... | collective-permute-start | bytes 2752520 | tf_op jit(solution)/shard_map/ppermute | solution.py:592
  168.9 16.4 %collective-permute-start.13 = (bf16[512,256]{1,0:T(8,128)(2,1)}, bf16[512,256]{1,0:T(8,128)(2,1)S(1)}, u32[]{:S(2)}, u32[]{:S(2)}) collective-permute-start(bf16[512,256]{1,0:T(8,128)(2,1)} %get-tuple-element.93.refs_2_), channel_id=1, source_target_pairs={{0,1},{1,2},{2,3},{4,5},{5,6},{6,7},{8,9},{9,10},{10,11},{12,13},{... | collective-permute-start | bytes 786440 | tf_op jit(solution)/shard_map/ppermute | solution.py:600
  185.3 29.9 %collective-permute-start.25 = (bf16[144,1536]{1,0:T(8,128)(2,1)S(1)}, bf16[144,1536]{1,0:T(8,128)(2,1)S(1)}, u32[]{:S(2)}, u32[]{:S(2)}) collective-permute-start(bf16[144,1536]{1,0:T(8,128)(2,1)S(1)} %get-tuple-element.114), channel_id=1, source_target_pairs={{0,1},{1,2},{2,3},{4,5},{5,6},{6,7},{8,9},{9,10},{10,11},{12,13},{... | collective-permute-start | bytes 1327112 | tf_op jit(solution)/shard_map/ppermute | solution.py:600
  194.7 20.5 %collective-permute-start.26 = (bf16[144,1536]{1,0:T(8,128)(2,1)S(1)}, bf16[144,1536]{1,0:T(8,128)(2,1)S(1)}, u32[]{:S(2)}, u32[]{:S(2)}) collective-permute-start(bf16[144,1536]{1,0:T(8,128)(2,1)S(1)} %get-tuple-element.114), channel_id=1, source_target_pairs={{0,2},{1,3},{4,6},{5,7},{8,10},{9,11},{12,14},{13,15},{16,18},{17,... | collective-permute-start | bytes 1327112 | tf_op jit(solution)/shard_map/ppermute | solution.py:600
  311.6 45.8 %collective-permute-start.39 = (bf16[2,2,128,1024]{3,2,1,0:T(8,128)(2,1)}, bf16[2,2,128,1024]{3,2,1,0:T(8,128)(2,1)}, u32[]{:S(2)}, u32[]{:S(2)}) collective-permute-start(bf16[2,2,128,1024]{3,2,1,0:T(8,128)(2,1)} %get-tuple-element.295), channel_id=1, source_target_pairs={{0,16},{4,20},{8,24},{12,28},{16,0},{20,4},{24,8},{28,12},{1,17},{... | collective-permute-start | bytes 3145736 | tf_op jit(solution)/shard_map/ppermute | solution.py:592
  316.2 44.4 %collective-permute-start.42 = (bf16[2,2,128,1024]{3,2,1,0:T(8,128)(2,1)}, bf16[2,2,128,1024]{3,2,1,0:T(8,128)(2,1)}, u32[]{:S(2)}, u32[]{:S(2)}) collective-permute-start(bf16[2,2,128,1024]{3,2,1,0:T(8,128)(2,1)} %get-tuple-element.293), channel_id=1, source_target_pairs={{0,8},{4,12},{8,0},{12,4},{16,24},{20,28},{24,16},{28,20},{1,9},{5... | collective-permute-start | bytes 3145736 | tf_op jit(solution)/shard_map/ppermute | solution.py:592
  318.8 45.4 %collective-permute-start.27 = (bf16[144,1536]{1,0:T(8,128)(2,1)S(1)}, bf16[144,1536]{1,0:T(8,128)(2,1)S(1)}, u32[]{:S(2)}, u32[]{:S(2)}) collective-permute-start(bf16[144,1536]{1,0:T(8,128)(2,1)S(1)} %copy-done.38), channel_id=1, source_target_pairs={{1,0},{2,1},{3,2},{5,4},{6,5},{7,6},{9,8},{10,9},{11,10},{13,12},{... | collective-permute-start | bytes 1327112 | tf_op jit(solution)/shard_map/ppermute | solution.py:600
  320.1 45.6 %collective-permute-start.28 = (bf16[144,1536]{1,0:T(8,128)(2,1)S(1)}, bf16[144,1536]{1,0:T(8,128)(2,1)S(1)}, u32[]{:S(2)}, u32[]{:S(2)}) collective-permute-start(bf16[144,1536]{1,0:T(8,128)(2,1)S(1)} %copy-done.38), channel_id=1, source_target_pairs={{2,0},{3,1},{6,4},{7,5},{10,8},{11,9},{14,12},{15,13},{18,16},{19,... | collective-permute-start | bytes 1327112 | tf_op jit(solution)/shard_map/ppermute | solution.py:600
  321.4 79.4 %collective-permute-start.30 = (bf16[512,256]{1,0:T(8,128)(2,1)S(1)}, bf16[512,256]{1,0:T(8,128)(2,1)}, u32[]{:S(2)}, u32[]{:S(2)}) collective-permute-start(bf16[512,256]{1,0:T(8,128)(2,1)S(1)} %get-tuple-element.139), channel_id=1, source_target_pairs={{1,0},{2,1},{3,2},{5,4},{6,5},{7,6},{9,8},{10,9},{11,10},{13,12},{... | collective-permute-start | bytes 786440 | tf_op jit(solution)/shard_map/ppermute | solution.py:600
  359.1 34.1 %collective-permute-start.40 = (bf16[2,1,128,1024]{3,2,1,0:T(8,128)(2,1)S(1)}, bf16[2,1,128,1024]{3,2,1,0:T(8,128)(2,1)S(1)}, u32[]{:S(2)}, u32[]{:S(2)}) collective-permute-start(bf16[2,1,128,1024]{3,2,1,0:T(8,128)(2,1)S(1)} %get-tuple-element.301), channel_id=1, source_target_pairs={{0,8},{4,12},{8,0},{12,4},{16,24},{20,28},{24,16},{28,20},{1,9},{5... | collective-permute-start | bytes 1572872 | tf_op jit(solution)/shard_map/ppermute | solution.py:592
  362.2 37.6 %collective-permute-start.43 = (bf16[2,1,128,1024]{3,2,1,0:T(8,128)(2,1)S(1)}, bf16[2,1,128,1024]{3,2,1,0:T(8,128)(2,1)S(1)}, u32[]{:S(2)}, u32[]{:S(2)}) collective-permute-start(bf16[2,1,128,1024]{3,2,1,0:T(8,128)(2,1)S(1)} %get-tuple-element.303), channel_id=1, source_target_pairs={{0,16},{4,20},{8,24},{12,28},{16,0},{20,4},{24,8},{28,12},{1,17},{... | collective-permute-start | bytes 1572872 | tf_op jit(solution)/shard_map/ppermute | solution.py:592
  364.2 37.2 %collective-permute-start.31 = (bf16[512,256]{1,0:T(8,128)(2,1)S(1)}, bf16[512,256]{1,0:T(8,128)(2,1)S(1)}, u32[]{:S(2)}, u32[]{:S(2)}) collective-permute-start(bf16[512,256]{1,0:T(8,128)(2,1)S(1)} %get-tuple-element.140), channel_id=1, source_target_pairs={{2,0},{3,1},{6,4},{7,5},{10,8},{11,9},{14,12},{15,13},{18,16},{19,... | collective-permute-start | bytes 786440 | tf_op jit(solution)/shard_map/ppermute | solution.py:600
  391.9 12.6 %collective-permute-start.29 = (f32[8,1792]{1,0:T(8,128)S(1)}, f32[8,1792]{1,0:T(8,128)S(1)}, u32[]{:S(2)}, u32[]{:S(2)}) collective-permute-start(f32[8,1792]{1,0:T(8,128)S(1)} %slice.377), channel_id=1, source_target_pairs={{1,0},{2,1},{3,2},{5,4},{6,5},{7,6},{9,8},{10,9},{11,10},{13,12},{... | collective-permute-start | bytes 172040 | tf_op jit(solution)/shard_map/ppermute | solution.py:600
  394.1 17.3 %collective-permute-start.41 = (bf16[128,1024]{1,0:T(8,128)(2,1)}, bf16[128,1024]{1,0:T(8,128)(2,1)S(1)}, u32[]{:S(2)}, u32[]{:S(2)}) collective-permute-start(bf16[128,1024]{1,0:T(8,128)(2,1)} %fusion.10), channel_id=1, source_target_pairs={{0,3},{1,0},{2,1},{3,2},{4,7},{5,4},{6,5},{7,6},{8,11},{9,8},{10,9... | collective-permute-start | bytes 786440 | tf_op jit(solution)/shard_map/ppermute | solution.py:596
  400.8 20.7 %collective-permute-start.44 = (bf16[128,1024]{1,0:T(8,128)(2,1)}, bf16[128,1024]{1,0:T(8,128)(2,1)}, u32[]{:S(2)}, u32[]{:S(2)}) collective-permute-start(bf16[128,1024]{1,0:T(8,128)(2,1)} %get-tuple-element.311), channel_id=1, source_target_pairs={{0,2},{1,3},{2,0},{3,1},{4,6},{5,7},{6,4},{7,5},{8,10},{9,11},{10,... | collective-permute-start | bytes 786440 | tf_op jit(solution)/shard_map/ppermute | solution.py:596
  400.8 20.7 %collective-permute-start.45 = (bf16[128,1024]{1,0:T(8,128)(2,1)}, bf16[128,1024]{1,0:T(8,128)(2,1)}, u32[]{:S(2)}, u32[]{:S(2)}) collective-permute-start(bf16[128,1024]{1,0:T(8,128)(2,1)} %get-tuple-element.312), channel_id=1, source_target_pairs={{0,1},{1,2},{2,3},{3,0},{4,5},{5,6},{6,7},{7,4},{8,9},{9,10},{10,1... | collective-permute-start | bytes 786440 | tf_op jit(solution)/shard_map/ppermute | solution.py:596
  433.9 28.7 %collective-permute-start.46 = (bf16[4,4,128,640]{3,2,1,0:T(8,128)(2,1)}, bf16[4,4,128,640]{3,2,1,0:T(8,128)(2,1)}, u32[]{:S(2)}, u32[]{:S(2)}) collective-permute-start(bf16[4,4,128,640]{3,2,1,0:T(8,128)(2,1)} %get-tuple-element.158), channel_id=1, source_target_pairs={{0,4},{4,0},{8,12},{12,8},{16,20},{20,16},{24,28},{28,24},{1,5},{5... | collective-permute-start | bytes 7864328 | tf_op jit(solution)/shard_map/ppermute | solution.py:592
  441.7 42.5 %collective-permute-start.54 = (bf16[128,1536]{1,0:T(8,128)(2,1)}, bf16[128,1536]{1,0:T(8,128)(2,1)}, u32[]{:S(2)}, u32[]{:S(2)}) collective-permute-start(bf16[128,1536]{1,0:T(8,128)(2,1)} %get-tuple-element.304), channel_id=1, source_target_pairs={{0,3},{1,0},{2,1},{3,2},{4,7},{5,4},{6,5},{7,6},{8,11},{9,8},{10,9... | collective-permute-start | bytes 1179656 | tf_op jit(solution)/shard_map/ppermute | solution.py:596
  460.5 26.4 %collective-permute-start.55 = (bf16[128,1536]{1,0:T(8,128)(2,1)}, bf16[128,1536]{1,0:T(8,128)(2,1)S(1)}, u32[]{:S(2)}, u32[]{:S(2)}) collective-permute-start(bf16[128,1536]{1,0:T(8,128)(2,1)} %get-tuple-element.306), channel_id=1, source_target_pairs={{0,2},{1,3},{2,0},{3,1},{4,6},{5,7},{6,4},{7,5},{8,10},{9,11},{10,... | collective-permute-start | bytes 1179656 | tf_op jit(solution)/shard_map/ppermute | solution.py:596
  461.2 25.8 %collective-permute-start.56 = (bf16[128,1536]{1,0:T(8,128)(2,1)S(1)}, bf16[128,1536]{1,0:T(8,128)(2,1)S(1)}, u32[]{:S(2)}, u32[]{:S(2)}) collective-permute-start(bf16[128,1536]{1,0:T(8,128)(2,1)S(1)} %copy-done.75), channel_id=1, source_target_pairs={{0,1},{1,2},{2,3},{3,0},{4,5},{5,6},{6,7},{7,4},{8,9},{9,10},{10,1... | collective-permute-start | bytes 1179656 | tf_op jit(solution)/shard_map/ppermute | solution.py:596
  465.9 13.7 %collective-permute-start.47 = (bf16[2,2,128,640]{3,2,1,0:T(8,128)(2,1)S(1)}, bf16[2,2,128,640]{3,2,1,0:T(8,128)(2,1)S(1)}, u32[]{:S(2)}, u32[]{:S(2)}) collective-permute-start(bf16[2,2,128,640]{3,2,1,0:T(8,128)(2,1)S(1)} %get-tuple-element.299), channel_id=1, source_target_pairs={{0,16},{4,20},{8,24},{12,28},{16,0},{20,4},{24,8},{28,12},{1,17},{... | collective-permute-start | bytes 1966088 | tf_op jit(solution)/shard_map/ppermute | solution.py:592
  467.8 16.0 %collective-permute-start.49 = (bf16[2,2,128,640]{3,2,1,0:T(8,128)(2,1)S(1)}, bf16[2,2,128,640]{3,2,1,0:T(8,128)(2,1)S(1)}, u32[]{:S(2)}, u32[]{:S(2)}) collective-permute-start(bf16[2,2,128,640]{3,2,1,0:T(8,128)(2,1)S(1)} %get-tuple-element.297), channel_id=1, source_target_pairs={{0,8},{4,12},{8,0},{12,4},{16,24},{20,28},{24,16},{28,20},{1,9},{5... | collective-permute-start | bytes 1966088 | tf_op jit(solution)/shard_map/ppermute | solution.py:592
  494.7 10.3 %collective-permute-start.52 = (bf16[128,640]{1,0:T(8,128)(2,1)S(1)}, bf16[128,640]{1,0:T(8,128)(2,1)S(1)}, u32[]{:S(2)}, u32[]{:S(2)}) collective-permute-start(bf16[128,640]{1,0:T(8,128)(2,1)S(1)} %maximum_maximum_fusion.1), channel_id=1, source_target_pairs={{0,2},{1,3},{2,0},{3,1},{4,6},{5,7},{6,4},{7,5},{8,10},{9,11},{10,... | collective-permute-start | bytes 491528 | tf_op jit(solution)/shard_map/ppermute | solution.py:596
  495.3 9.8 %collective-permute-start.53 = (bf16[128,640]{1,0:T(8,128)(2,1)S(1)}, bf16[128,640]{1,0:T(8,128)(2,1)S(1)}, u32[]{:S(2)}, u32[]{:S(2)}) collective-permute-start(bf16[128,640]{1,0:T(8,128)(2,1)S(1)} %maximum_maximum_fusion.2), channel_id=1, source_target_pairs={{0,1},{1,2},{2,3},{3,0},{4,5},{5,6},{6,7},{7,4},{8,9},{9,10},{10,1... | collective-permute-start | bytes 491528 | tf_op jit(solution)/shard_map/ppermute | solution.py:596
  (104 other events, 1405.0 us)
Sparse Core Ops, SparseCore 0:
  30.5 131.9 all-gather.1
  261.9 124.5 reduce-scatter.1

commit v3 on v2

--- a/solution.py
+++ b/solution.py
@@ -623,17 +623,25 @@
         sides = [hold(3, side) for side in sides]
         return [[lows, [self.dp(low, 1) for low in lows]] for lows in sides]
 
-    def scatter(self, sent, kept):
+    def scatter_sibling(self, sent, kept):
         came = self.dp(sent, 1)
+        halves = []
+        for n in range(2):
+            here = slice(2 * n, 2 * n + 2)
+            halves.append((add(kept[here, 2:], came[here, 2:]), add(kept[here, :2], came[here, :2])))
+        return halves
+
+    def scatter_first(self, halves):
+        quarters = []
+        for (out, mine), (_, axis) in zip(halves, ORDERS):
+            got = self.dp(out, axis)
+            quarters.append((add(mine[:, 1:], got[:, 1:]), add(mine[:, :1], got[:, :1])))
+        return quarters
+
+    def scatter_second(self, quarters):
         parts = []
-        for n, (second, first) in enumerate(ORDERS):
-            here = slice(2 * n, 2 * n + 2)
-            out = add(kept[here, 2:], came[here, 2:])
-            mine = add(kept[here, :2], came[here, :2])
-            got = self.dp(out, first)
-            out = add(mine[:, 1:], got[:, 1:])
-            mine = add(mine[:, :1], got[:, :1])
-            got = self.dp(out, second)
+        for (out, mine), (axis, _) in zip(quarters, ORDERS):
+            got = self.dp(out, axis)
             parts += [add(mine[i, 0], got[i, 0]) for i in range(2)]
         return parts
 
@@ -975,7 +983,7 @@
             grid=(nt,),
             in_specs=[pl.BlockSpec((nd, 1, rows, columns), lambda s, index: (0, index[8 + s], 0, 0))] + wholes(arrays),
             out_specs=(
-                pl.BlockSpec((model, columns), lambda s, index: (0, s)),
+                pl.BlockSpec((model, columns), lambda s, index: (0, index[8 + s])),
                 whole((tokens, model)),
                 whole((tokens, model)),
             ),
@@ -1064,16 +1072,16 @@
     stages = {}
 
     def note(stage, values):
+        if stage == 1:
+            values = after(values, normed)
+        if stage == 3:
+            values = after(values, halo)
         stages[stage] = stages.get(stage, []) + list(values)
         return values
-
-    def follow(stage, values):
-        return after(values, *([stages[2]] if stage == 0 else [sides1] if stage == 1 else []))
 
     pack1 = pack((query_proj, step_wide, input_inner, shared_part), (False,) * 4)
     sides1 = ring.gather(pack1, note)
     pack2 = pack((gate_inner, attn_out_proj, mamba_out), (False, True, True))
-    sides2 = ring.gather(pack2, follow)
     ffn_pack = pack((ffn_gate, ffn_up, ffn_down), (False, False, True))
     (ffn_pack,) = after([ffn_pack], *stages[FFN_AFTER]) if FFN_AFTER else [ffn_pack]
     w_ffn = lax.all_gather(ffn_pack, ("dp", "tensor"), axis=0, tiled=True)
@@ -1081,8 +1089,6 @@
     w_q, w_step, w_x, w_shared, u, query8, kv_own, dt_raw = project(
         index, sides1, widths1, (widths1[0] * nt, LANE, widths1[2] * nt, quarter * nt), normed, halo, cosine, sine
     )
-    w_z, w_ao, w_mo = assemble(index, sides2, widths2, tuple(w * nt for w in widths2))
-
     padded = jnp.concatenate([jnp.full((back,), -1, jnp.int32), segment])
     seg_keys = lax.dynamic_slice_in_dim(padded, start, back + rows)
     seg_own = seg_keys[back:]
@@ -1104,6 +1110,16 @@
     keeps_after = jnp.stack(keeps_after + [zero] * 4, axis=1)
     kvs = [ring.line(kv_own, s) for s in range(hops, 0, -1)] + [kv_own]
 
+    waits = {0: (stages[1],), 1: (kv_own,)}
+
+    def hold(stage, values):
+        return after(values, *waits[stage])
+
+    (own2,) = hold(0, [ring.block(pack2)])
+    parts2 = [own2] + [ring.shift(own2, s) for s in range(1, nt)]
+    pairs2 = hold(1, [join([parts2[s] for s in members]) for members in SETS])
+    nears2 = [ring.dp(pair, one) for pair, (one, _) in zip(pairs2, ORDERS)]
+    (u,) = after([u], pairs2)
     taps = jnp.concatenate([conv_weight, conv_bias[None, :], jnp.zeros((3, INNER + 2 * NS), f32)], axis=0)
     rate = -jnp.exp(decay_log)
     heads = jnp.pad(jnp.stack([step_bias, rate]), ((0, 6), (0, LANE - MH)))
@@ -1113,8 +1129,14 @@
     gather2 = jnp.asarray(np.concatenate([spread.T, spread.T], axis=0), bf16)
 
     mix, dt, cum, cumt, ec, fw, g, final = mamba_pre(u, taps, meta, dt_raw, heads, spread2)
+    firsts2 = after([join([parts2[s] for s in members] + [near]) for members, near in zip(SETS, nears2)], mix, kvs)
+    sides2 = [[first, ring.dp(first, two)] for first, (_, two) in zip(firsts2, ORDERS)]
+    (query8,) = after([query8], *firsts2)
     carries = [ring.line(final, s) for s in range(1, hops + 1)]
     attended, lse = attn_fwd(first_block, query8, seg_row, seg_keys[:, None], kvs)
+    waits[3] = (attended, carries)
+    sides2 = [[lows, [ring.dp(low, 1) for low in lows]] for lows in [hold(3, side) for side in sides2]]
+    w_z, w_ao, w_mo = assemble(index, sides2, widths2, tuple(w * nt for w in widths2))
     z_gate = dot(normed, w_z)
     gated, full, states = mamba_fwd(
         mix, dt, cum, cumt, ec, fw, g, seg_col, seg_row, z_gate, skip, spread2, carries
@@ -1130,7 +1152,7 @@
     ffn_grads, output, d_normed2 = ffn(index, w_ffn, normed2, normed2_t, cotangent, cot_t, residual)
     ffn_grads = lax.psum_scatter(ffn_grads, "dp", scatter_dimension=0, tiled=True)
     units = ffn_gate.shape[1]
-    g_ffn = ring.total([ffn_grads[:, s * 3 * units : (s + 1) * 3 * units] for s in range(nt)])
+    g_ffn = lax.psum_scatter(ffn_grads, "tensor", scatter_dimension=1, tiled=True).astype(f32)
     d_residual, d_mixer_t, d_gated, d_attended, ffn_gain_grad = simple_call(
         after_ffn_kernel,
         "after_ffn",
@@ -1147,7 +1169,9 @@
         first_block, query8, d_attended, attended, lse, seg_row, seg_keys[:, None], cosine, sine, kvs
     )
     came = [ring.line(d_kvs[hops - s], -s) for s in range(1, hops + 1)]
-    d_kv = simple_call(kv_back_kernel, "kv_back", (cosine, sine, d_kvs[-1], *came), sds(kv_own.shape, bf16))
+    def kv_back(own):
+        return simple_call(kv_back_kernel, "kv_back", (cosine, sine, own, *came), sds(kv_own.shape, bf16))
+
 
     plan2 = (
         (0, 0, widths2[1], "part"),
@@ -1155,24 +1179,32 @@
         (1, 2, widths2[0], "part"),
         (1, 3, widths1[0], "part"),
     )
-    grads2 = ring.collect(
-        ring.scatter(*weight_grads(index, (d_mixer_t, normed_t), (attended, gated, d_z, d_q), plan2))
-    )
+    (d_q2,) = after([d_q], *d_carries)
+    sent2, kept2 = weight_grads(index, (d_mixer_t, normed_t), (attended, gated, d_z, d_q2), plan2)
+    (dy,) = after([dy], sent2)
 
     d_pre, d_step, conv_grads, small = mamba_bwd(
         mix, dt, cum, cumt, ec, fw, g, seg_col, seg_row, dy, states, u, taps, meta, skip, heads, spread2, gather2, d_carries
     )
+    kept2, own_kv = after([kept2, d_kvs[-1]], d_pre)
+    d_kv = kv_back(own_kv)
+    halves2 = ring.scatter_sibling(sent2, kept2)
     d_after = ring.line(d_pre[:8], -1)
     d_x, d_shared = simple_call(
         conv_back_kernel,
         "conv_back",
-        (d_pre, d_after, taps, keeps_after, d_kv),
+        (d_pre, d_after, *after([taps], halves2, ffn_grads), keeps_after, d_kv),
         (sds((rows, INNER), bf16), sds((rows, quarter * nt), bf16)),
     )
 
-    d_x, d_shared = after([d_x, d_shared], ffn_grads)
     plan1 = ((0, 0, widths1[2], "part"), (0, 1, LANE, "all"), (0, 2, quarter, "fixed"))
-    parts = ring.scatter(*weight_grads(index, (normed_t,), (d_x, d_step, d_shared), plan1))
+    sent1, kept1 = weight_grads(index, (normed_t,), (d_x, d_step, d_shared), plan1)
+    quarters2 = ring.scatter_first([(out, after([mine], sent1)[0]) for out, mine in halves2])
+    halves1 = ring.scatter_sibling(sent1, after([kept1], quarters2)[0])
+    parts2 = ring.scatter_second([(out, after([mine], halves1)[0]) for out, mine in quarters2])
+    quarters1 = ring.scatter_first([(out, after([mine], parts2)[0]) for out, mine in halves1])
+    grads2 = ring.collect(after(parts2[:1], quarters1) + tuple(parts2[1:]))
+    parts = ring.scatter_second(quarters1)
     common = widths1[2] + LANE
     shared_sum = jnp.concatenate([part[:, common:] for part in parts], axis=1)
     shared_sum = ring.unblock(shared_sum)
@@ -1189,6 +1221,7 @@
         grads1, g_shared = ring.collect(parts), ring.total(rows_of)
     g_shared = jnp.concatenate([g_shared[i * piece : (i + 1) * piece] for i in range(nt)], axis=1)
 
+    d_q, d_x, d_z = after([d_q, d_x, d_z], halves1)
     d_normed = (
         dot(d_q, w_q, NT) + dot(d_z, w_z, NT) + dot(d_x, w_x, NT) + dot(d_shared, w_shared, NT) + dot(d_step, w_step, NT)
     )

time: 524 us -> 496 us (0.947)
  waiting for transfers between devices: 175 us -> 138 us
  other arithmetic: 28.4 us -> 35 us
    ppermute x26, waiting for transfers between devices: 105 us -> 54.6 us  [dp(): return lax.ppermute(value, 'dp', [(i, i ^ step) for i in range(self.nd)])]
    ppermute x10, waiting for transfers between devices: 5.48 us -> 35.2 us  [line(): lax.ppermute(value, 'tensor', [(i, i + s) for i in range(n) if 0 <= i + s...]
    ppermute x18 -> x15, waiting for transfers between devices: 61.4 us -> 46.4 us  [shift(): return lax.ppermute(value, 'tensor', [(i, (i + s) % n) for i in range(n)])]
    ppermute x10, starting transfers between devices: 27.8 us -> 40.5 us  [line(): lax.ppermute(value, 'tensor', [(i, i + s) for i in range(n) if 0 <= i + s...]
    ppermute x18 -> x15, starting transfers between devices: 31.8 us -> 23.2 us  [shift(): return lax.ppermute(value, 'tensor', [(i, (i + s) % n) for i in range(n)])]
    convert_element_type x10, other arithmetic: 13.4 us -> 20.2 us  [add(): return (a.astype(f32) + b.astype(f32)).astype(bf16)]
    unnamed x191 -> x203, local copies, waits for them, and re-layouts: 21 us -> 22.9 us
  transfers between devices with their start and end apart: 59 -> 57, of which waited for: 20 -> 23; matrix products, arithmetic and copies ran while one was open for 11% -> 12% of each run, Pallas kernels for 23% -> 24%
where the time goes in v3:
time: 496 us; the launch traced here: 486 us
  Pallas kernels  160 us (32%)
  waiting for transfers between devices  138 us (28%)
  starting transfers between devices  89 us (18%)
  local copies, waits for them, and re-layouts  36.3 us (7%)
  other arithmetic  35 us (7%)
  between operations  15.7 us (3%)
  matrix products  11.5 us (2%)
    ppermute x26, waiting for transfers between devices, dp(): return lax.ppermute(value, 'dp', [(i, i ^ step) for i in range(self.nd)])  54.6 us
    ppermute x15, waiting for transfers between devices, shift(): return lax.ppermute(value, 'tensor', [(i, (i + s) % n) for i in range(n)])  46.4 us
    ppermute x10, starting transfers between devices, line(): lax.ppermute(value, 'tensor', [(i, i + s) for i in range(n) if 0 <= i + s...  40.5 us
    ppermute x10, waiting for transfers between devices, line(): lax.ppermute(value, 'tensor', [(i, i + s) for i in range(n) if 0 <= i + s...  35.2 us
    pallas_call x8, Pallas kernels, simple_call(): pl.pallas_call(kernel, grid=(1,), out_shape=outs, in_specs=wholes(arrays)...  33.9 us
    pallas_call x1, Pallas kernels, ffn(): pl.pallas_call(ffn_kernel, grid_spec=pltpu.PrefetchScalarGridSpec(num_sca...  28.7 us
    pallas_call x1, Pallas kernels, mamba_bwd(): pl.pallas_call(mamba_bwd_kernel, grid=(n,), in_specs=[rev(width), rev(LAN...  24.5 us
    ppermute x15, starting transfers between devices, shift(): return lax.ppermute(value, 'tensor', [(i, (i + s) % n) for i in range(n)])  23.2 us
  transfers between devices with their start and end apart: 57, of which 23 were waited for; matrix products, arithmetic and copies ran while one was open for 12% of the time, Pallas kernels for 24%

profile of v3, /device:TPU:0, one launch (start us, length us, event | category | flops | bytes accessed | tf_op | source)
XLA Modules:
  0.0 486.1 jit_solution(2086551760011276562)
XLA Ops:
  11.3 4.3 collective-permute-start.1
  17.6 3.8 norm_in.1
  21.5 1.9 pack.3
  23.4 6.9 %collective-permute-done.refs_1_ = bf16[128,768]{1,0:T(8,128)(2,1)S(1)} collective-permute-done((bf16[128,768]{1,0:T(8,128)(2,1)}, bf16[128,768]{1,0:T(8,128)(2,1)S(1)}, u32[]{:S(2)}, u32[]{:S(2)}) %collective-permute-start) | collective-permute-done | bytes 196640 | tf_op jit(solution)/shard_map/ppermute | solution.py:596
  31.3 5.8 %collective-permute-start.5 = (bf16[16,1024]{1,0:T(8,128)(2,1)S(1)}, bf16[16,1024]{1,0:T(8,128)(2,1)S(1)}, u32[]{:S(2)}, u32[]{:S(2)}) collective-permute-start(bf16[16,1024]{1,0:T(8,128)(2,1)S(1)} %slice.358), channel_id=1, source_target_pairs={{0,1},{1,2},{2,3},{4,5},{5,6},{6,7},{8,9},{9,10},{10,11},{12,13},{... | collective-permute-start | bytes 98312 | tf_op jit(solution)/shard_map/ppermute | solution.py:600
  43.8 6.9 %collective-permute-done.8.refs_2_ = bf16[2,128,768]{2,1,0:T(8,128)(2,1)S(1)} collective-permute-done((bf16[2,128,768]{2,1,0:T(8,128)(2,1)S(1)}, bf16[2,128,768]{2,1,0:T(8,128)(2,1)S(1)}, u32[]{:S(2)}, u32[]{:S(2)}) %collective-permute-start.8) | collective-permute-done | bytes 393248 | tf_op jit(solution)/shard_map/ppermute | solution.py:592
  52.4 2.2 collective-permute-done.3.refs_2_
  59.8 10.2 %collective-permute-done.9.refs_5_ = bf16[2,2,128,768]{3,2,1,0:T(8,128)(2,1)} collective-permute-done((bf16[2,2,128,768]{3,2,1,0:T(8,128)(2,1)S(1)}, bf16[2,2,128,768]{3,2,1,0:T(8,128)(2,1)}, u32[]{:S(2)}, u32[]{:S(2)}) %collective-permute-start.9) | collective-permute-done | bytes 786464 | tf_op jit(solution)/shard_map/ppermute | solution.py:592
  76.2 15.4 %collective-permute-done.14.refs_1_ = bf16[128,896]{1,0:T(8,128)(2,1)S(1)} collective-permute-done((bf16[128,896]{1,0:T(8,128)(2,1)S(1)}, bf16[128,896]{1,0:T(8,128)(2,1)S(1)}, u32[]{:S(2)}, u32[]{:S(2)}) %collective-permute-start.14) | collective-permute-done | bytes 229408 | tf_op jit(solution)/shard_map/ppermute | solution.py:596
  92.3 9.6 %project.1 = (bf16[1024,512]{1,0:T(8,128)(2,1)}, bf16[1024,128]{1,0:T(8,128)(2,1)}, bf16[1024,1536]{1,0:T(8,128)(2,1)}, bf16[1024,512]{1,0:T(8,128)(2,1)}, f32[5...) custom-call(s32[12]{0:T(128)} %stack.115.index_ref, ...), custom_call_target="tpu_custom_call" | custom-call | flops 2000000000 | bytes 4000000 | tf_op jit(solution)/shard_map/project/pallas_call | solution.py:778
  105.0 2.3 collective-permute-start.18
  107.3 2.1 copy-done.4
  110.3 6.6 %mamba_pre.1 = (bf16[512,1792]{1,0:T(8,128)(2,1)S(1)}, f32[512,128]{1,0:T(8,128)S(1)}, f32[512,128]{1,0:T(8,128)S(1)}, f32[32,512]{1,0:T(8,128)S(1)}, f32[512,12...) custom-call(f32[528,1792]{1,0:T(8,128)S(1)} %copy-done.4, ...), custom_call_target="tpu_custom_call" | custom-call | flops 2000000000 | bytes 4000000 | tf_op jit(solution)/shard_map/mamba_pre/pallas_call | solution.py:322
  116.9 7.7 %collective-permute-done.16.refs_2_ = bf16[2,128,896]{2,1,0:T(8,128)(2,1)S(1)} collective-permute-done((bf16[2,128,896]{2,1,0:T(8,128)(2,1)S(1)}, bf16[2,128,896]{2,1,0:T(8,128)(2,1)S(1)}, u32[]{:S(2)}, u32[]{:S(2)}) %collective-permute-start.16) | collective-permute-done | bytes 458784 | tf_op jit(solution)/shard_map/ppermute | solution.py:592
  131.7 20.2 %collective-permute-start.20 = (bf16[144,1536]{1,0:T(8,128)(2,1)}, bf16[144,1536]{1,0:T(8,128)(2,1)}, u32[]{:S(2)}, u32[]{:S(2)}) collective-permute-start(bf16[144,1536]{1,0:T(8,128)(2,1)} %get-tuple-element.139), channel_id=1, source_target_pairs={{0,1},{1,2},{2,3},{4,5},{5,6},{6,7},{8,9},{9,10},{10,11},{12,13},{... | collective-permute-start | bytes 1327112 | tf_op jit(solution)/shard_map/ppermute | solution.py:600
  151.9 4.2 collective-permute-start.21
  159.7 6.6 %attn_fwd.1 = (bf16[512,512]{1,0:T(8,128)(2,1)S(1)}, f32[8,512]{1,0:T(8,128)S(1)}) custom-call(s32[4]{0:T(128)S(1)} %and_select_fusion.first_ref, bf16[512,512]{1,0:T(8,128)(2,1)S(1)} %copy-done.36, s32[1,512]{1,0:T(1,128)S(1)} %bitcast.85, s32[1536,1]{1,0:T(8,128)S(1)} %broadcast_in_dim.53.segk_ref, bf16[512,256]{1,0:T(8,128)(2,1)S(1)} %copy-done.42, ...), custom_call_target="tpu_custom_call" | custom-call | flops 2000000000 | bytes 4000000 | tf_op jit(solution)/shard_map/attn_fwd/pallas_call | solution.py:200
  167.2 4.9 %collective-permute-done.21.refs_1_ = bf16[144,1536]{1,0:T(8,128)(2,1)} collective-permute-done((bf16[144,1536]{1,0:T(8,128)(2,1)}, bf16[144,1536]{1,0:T(8,128)(2,1)}, u32[]{:S(2)}, u32[]{:S(2)}) %collective-permute-start.21) | collective-permute-done | bytes 442400 | tf_op jit(solution)/shard_map/ppermute | solution.py:600
  178.8 6.7 %assemble.1 = (bf16[1024,1536]{1,0:T(8,128)(2,1)}, bf16[1024,512]{1,0:T(8,128)(2,1)}, bf16[1024,1536]{1,0:T(8,128)(2,1)}) custom-call(s32[12]{0:T(128)S(1)} %copy-done.32, bf16[2,2,128,896]{3,2,1,0:T(8,128)(2,1)} %join.14.refs_0_, bf16[2,2,128,896]{3,2,1,0:T(8,128)(2,1)} %collective-permute-done.19.refs_1_, ...), custom_call_target="tpu_custom_call" | custom-call | flops 2000000000 | bytes 4000000 | tf_op jit(solution)/shard_map/assemble/pallas_call | solution.py:731
  185.6 3.7 fusion.36.z_ref
  189.4 8.0 %mamba_fwd.1 = (bf16[512,1536]{1,0:T(8,128)(2,1)S(1)}, bf16[512,1536]{1,0:T(8,128)(2,1)S(1)}, bf16[4,128,1536]{2,1,0:T(8,128)(2,1)S(1)}) custom-call(bf16[512,1792]{1,0:T(8,128)(2,1)S(1)} %get-tuple-element.128.mix_ref.cm_ref, f32[512,128]{1,0:T(8,128)S(1)} %get-tuple-element.133.dt_ref, f32[512,128]{1,0:T(8,128)S(1)} %copy-done.16, ...), custom_call_target="tpu_custom_call" | custom-call | flops 2000000000 | bytes 4000000 | tf_op jit(solution)/shard_map/mamba_fwd/pallas_call | solution.py:390
  200.9 7.6 %middle.1 = (f32[512,1024]{1,0:T(8,128)}, bf16[512,1024]{1,0:T(8,128)(2,1)}, bf16[1024,512]{1,0:T(8,128)(2,1)}, f32[512,1]{1,0:T(8,128)}) custom-call(bf16[512,512]{1,0:T(8,128)(2,1)} %copy-done.57, bf16[512,1536]{1,0:T(8,128)(2,1)} %copy-done.35, bf16[1024,512]{1,0:T(8,128)(2,1)} %get-tuple-element.146.wa_ref, ...), custom_call_target="tpu_custom_call" | custom-call | flops 2000000000 | bytes 4000000 | tf_op jit(solution)/shard_map/middle/pallas_call | solution.py:887
  208.5 28.7 %ffn.1 = (bf16[1024,6144]{1,0:T(8,128)(2,1)}, bf16[512,1024]{1,0:T(8,128)(2,1)}, f32[512,1024]{1,0:T(8,128)}) custom-call(s32[12]{0:T(128)} %stack.115.index_ref, bf16[8,4,128,1536]{3,2,1,0:T(8,128)(2,1)} %bitcast.90, bf16[512,1024]{1,0:T(8,128)(2,1)} %get-tuple-element.148.n_ref, bf16[1024,512]{1,0:T(8,128)(2,1)} %get-tuple-element.149.nt_ref, ...), custom_call_target="tpu_custom_call" | custom-call | flops 2000000000 | bytes 4000000 | tf_op jit(solution)/shard_map/ffn/pallas_call | solution.py:979
  237.8 8.6 %after_ffn.1 = (f32[512,1024]{1,0:T(8,128)}, bf16[1024,512]{1,0:T(8,128)(2,1)}, bf16[512,1536]{1,0:T(8,128)(2,1)}, bf16[512,512]{1,0:T(8,128)(2,1)}, f32[8,1024]{1,0:T(8,128)}) custom-call(f32[512,1024]{1,0:T(8,128)} %get-tuple-element.153.dn_ref, f32[512,1024]{1,0:T(8,128)} %get-tuple-element.151.res_ref, f32[512,1]{1,0:T(8,128)} %get-tuple-element.154.scale_ref, ...), custom_call_target="tpu_custom_call" | custom-call | flops 2000000000 | bytes 4000000 | tf_op jit(solution)/shard_map/after_ffn/pallas_call | solution.py:887
  247.9 3.2 mamba_bpre.1
  253.8 9.2 %attn_bwd.1 = (bf16[512,512]{1,0:T(8,128)(2,1)S(1)}, bf16[512,256]{1,0:T(8,128)(2,1)S(1)}, bf16[512,256]{1,0:T(8,128)(2,1)S(1)}, f32[512,256]{1,0:T(8,128)S(1)}) custom-call(s32[4]{0:T(128)S(1)} %and_select_fusion.first_ref, bf16[512,512]{1,0:T(8,128)(2,1)S(1)} %copy-done.37, bf16[512,512]{1,0:T(8,128)(2,1)S(1)} %copy-done.38, ...), custom_call_target="tpu_custom_call" | custom-call | flops 2000000000 | bytes 4000000 | tf_op jit(solution)/shard_map/attn_bwd/pallas_call | solution.py:217
  264.7 9.2 %collective-permute-done.27.refs_0_ = bf16[144,1536]{1,0:T(8,128)(2,1)S(1)} collective-permute-done((bf16[144,1536]{1,0:T(8,128)(2,1)S(1)}, bf16[144,1536]{1,0:T(8,128)(2,1)S(1)}, u32[]{:S(2)}, u32[]{:S(2)}) %collective-permute-start.27) | collective-permute-done | bytes 442400 | tf_op jit(solution)/shard_map/ppermute | solution.py:600
  273.8 20.1 %collective-permute-done.28.refs_1_ = bf16[144,1536]{1,0:T(8,128)(2,1)S(1)} collective-permute-done((bf16[144,1536]{1,0:T(8,128)(2,1)S(1)}, bf16[144,1536]{1,0:T(8,128)(2,1)S(1)}, u32[]{:S(2)}, u32[]{:S(2)}) %collective-permute-start.28) | collective-permute-done | bytes 442400 | tf_op jit(solution)/shard_map/ppermute | solution.py:600
  294.0 12.8 %weight_grads.2 = (bf16[4,4,128,1024]{3,2,1,0:T(8,128)(2,1)}, bf16[4,4,128,1024]{3,2,1,0:T(8,128)(2,1)}) custom-call(s32[12]{0:T(128)} %stack.115.index_ref, bf16[1024,512]{1,0:T(8,128)(2,1)} %get-tuple-element.163.refs_0_, bf16[1024,512]{1,0:T(8,128)(2,1)} %get-tuple-element.164.refs_1_.refs_0_, bf16[512,512]{1,0:T(8,128)(2,1)} %copy-done.57, ...), custom_call_target="tpu_custom_call" | custom-call | flops 2000000000 | bytes 4000000 | tf_op jit(solution)/shard_map/weight_grads/pallas_call | solution.py:931
  310.4 24.5 %mamba_bwd.1 = (f32[512,1792]{1,0:T(8,128)}, bf16[512,128]{1,0:T(8,128)(2,1)}, f32[8,1792]{1,0:T(8,128)}, f32[8,128]{1,0:T(8,128)}) custom-call(bf16[512,1792]{1,0:T(8,128)(2,1)} %copy-done, f32[512,128]{1,0:T(8,128)} %copy-done.14, f32[512,128]{1,0:T(8,128)} %copy-done.15, f32[32,512]{1,0:T(8,128)} %copy-done.27, f32[512,128]{1,0:T(8,128)} %copy-done.5, ...), custom_call_target="tpu_custom_call" | custom-call | flops 2000000000 | bytes 4000000 | tf_op jit(solution)/shard_map/mamba_bwd/pallas_call | solution.py:555
  338.7 2.3 kv_back.1.dkv_ref
  340.9 4.6 add_convert_fusion
  346.2 6.2 %conv_back.1 = (bf16[512,1536]{1,0:T(8,128)(2,1)}, bf16[512,512]{1,0:T(8,128)(2,1)}) custom-call(f32[512,1792]{1,0:T(8,128)} %get-tuple-element.171.dpre_ref, f32[8,1792]{1,0:T(8,128)} %copy-done.95, f32[8,1792]{1,0:T(8,128)} %maximum_maximum_fusion.3.tap_ref, f32[512,8]{1,0:T(8,128)} %copy.124.keep_ref, bf16[512,256]{1,0:T(8,128)(2,1)} %kv_back.1.dkv_ref), custom_call_target="tpu_custom_call" | custom-call | flops 2000000000 | bytes 4000000 | tf_op jit(solution)/shard_map/conv_back/pallas_call | solution.py:887
  352.4 8.3 %weight_grads.3 = (bf16[4,4,128,640]{3,2,1,0:T(8,128)(2,1)}, bf16[4,4,128,640]{3,2,1,0:T(8,128)(2,1)}) custom-call(s32[12]{0:T(128)} %stack.115.index_ref, bf16[1024,512]{1,0:T(8,128)(2,1)} %get-tuple-element.164.refs_1_.refs_0_, bf16[512,1536]{1,0:T(8,128)(2,1)} %get-tuple-element.191.refs_1_, bf16[512,128]{1,0:T(8,128)(2,1)} %get-tuple-element.181.refs_2_, ...), custom_call_target="tpu_custom_call" | custom-call | flops 2000000000 | bytes 4000000 | tf_op jit(solution)/shard_map/weight_grads/pallas_call | solution.py:931
  365.5 21.2 %collective-permute-done.33 = bf16[2,2,128,1024]{3,2,1,0:T(8,128)(2,1)} collective-permute-done((bf16[2,2,128,1024]{3,2,1,0:T(8,128)(2,1)}, bf16[2,2,128,1024]{3,2,1,0:T(8,128)(2,1)}, u32[]{:S(2)}, u32[]{:S(2)}) %collective-permute-start.33) | collective-permute-done | bytes 1048608 | tf_op jit(solution)/shard_map/ppermute | solution.py:592
  386.7 2.6 add_convert_fusion.10
  390.9 2.6 add_convert_fusion.8
  395.1 1.9 fusion.40
  397.1 3.8 add_convert_fusion.4
  412.7 3.5 fusion.2
  419.3 2.0 fusion.7
  421.7 3.6 collective-permute-start.39
  425.3 3.3 collective-permute-start.40
  429.9 2.0 fusion.9
  434.4 2.4 collective-permute-start.48
  447.7 9.7 %collective-permute-done.47 = bf16[128,1024]{1,0:T(8,128)(2,1)} collective-permute-done((bf16[128,1024]{1,0:T(8,128)(2,1)}, bf16[128,1024]{1,0:T(8,128)(2,1)}, u32[]{:S(2)}, u32[]{:S(2)}) %collective-permute-start.47) | collective-permute-done | bytes 262176 | tf_op jit(solution)/shard_map/ppermute | solution.py:596
  461.5 2.1 collective-permute-start.53
  466.5 9.8 %collective-permute-done.52 = bf16[128,640]{1,0:T(8,128)(2,1)S(1)} collective-permute-done((bf16[128,640]{1,0:T(8,128)(2,1)S(1)}, bf16[128,640]{1,0:T(8,128)(2,1)S(1)}, u32[]{:S(2)}, u32[]{:S(2)}) %collective-permute-start.52) | collective-permute-done | bytes 163872 | tf_op jit(solution)/shard_map/ppermute | solution.py:596
  (397 shorter events, 114.5 us)
Async XLA Ops:
  7.2 201.3 %all-gather.2.cloned.1.call-start = ((), (), s32[]{:S(2)}) async-start(), calls=%async_computation.2 | async-start | bytes 12976128 | tf_op jit(solution)/shard_map/all_gather | solution.py:1087
  11.3 19.1 %collective-permute-start.1 = (bf16[128,768]{1,0:T(8,128)(2,1)}, bf16[128,768]{1,0:T(8,128)(2,1)S(1)}, u32[]{:S(2)}, u32[]{:S(2)}) collective-permute-start(bf16[128,768]{1,0:T(8,128)(2,1)} %pack.4.refs_0_), channel_id=1, source_target_pairs={{0,2},{1,3},{2,0},{3,1},{4,6},{5,7},{6,4},{7,5},{8,10},{9,11},{10,... | collective-permute-start | bytes 589832 | tf_op jit(solution)/shard_map/ppermute | solution.py:596
  15.6 14.8 %collective-permute-start.2 = (bf16[128,768]{1,0:T(8,128)(2,1)}, bf16[128,768]{1,0:T(8,128)(2,1)S(1)}, u32[]{:S(2)}, u32[]{:S(2)}) collective-permute-start(bf16[128,768]{1,0:T(8,128)(2,1)} %pack.4.refs_0_), channel_id=1, source_target_pairs={{0,3},{1,0},{2,1},{3,2},{4,7},{5,4},{6,5},{7,6},{8,11},{9,8},{10,9... | collective-permute-start | bytes 589832 | tf_op jit(solution)/shard_map/ppermute | solution.py:596
  16.9 13.4 %collective-permute-start = (bf16[128,768]{1,0:T(8,128)(2,1)}, bf16[128,768]{1,0:T(8,128)(2,1)S(1)}, u32[]{:S(2)}, u32[]{:S(2)}) collective-permute-start(bf16[128,768]{1,0:T(8,128)(2,1)} %pack.4.refs_0_), channel_id=1, source_target_pairs={{0,1},{1,2},{2,3},{3,0},{4,5},{5,6},{6,7},{7,4},{8,9},{9,10},{10,1... | collective-permute-start | bytes 589832 | tf_op jit(solution)/shard_map/ppermute | solution.py:596
  30.5 315.1 %reduce-scatter.3.cloned.1.call-start = ((), (), s32[]{:S(2)}) async-start(), calls=%async_computation.3 | async-start | bytes 14155776 | tf_op jit(solution)/shard_map/reduce_scatter | solution.py:1153
  31.3 28.5 %collective-permute-start.5 = (bf16[16,1024]{1,0:T(8,128)(2,1)S(1)}, bf16[16,1024]{1,0:T(8,128)(2,1)S(1)}, u32[]{:S(2)}, u32[]{:S(2)}) collective-permute-start(bf16[16,1024]{1,0:T(8,128)(2,1)S(1)} %slice.358), channel_id=1, source_target_pairs={{0,1},{1,2},{2,3},{4,5},{5,6},{6,7},{8,9},{9,10},{10,11},{12,13},{... | collective-permute-start | bytes 98312 | tf_op jit(solution)/shard_map/ppermute | solution.py:600
  37.1 13.6 %collective-permute-start.8 = (bf16[2,128,768]{2,1,0:T(8,128)(2,1)S(1)}, bf16[2,128,768]{2,1,0:T(8,128)(2,1)S(1)}, u32[]{:S(2)}, u32[]{:S(2)}) collective-permute-start(bf16[2,128,768]{2,1,0:T(8,128)(2,1)S(1)} %join.9), channel_id=1, source_target_pairs={{0,16},{4,20},{8,24},{12,28},{16,0},{20,4},{24,8},{28,12},{1,17},{... | collective-permute-start | bytes 1179656 | tf_op jit(solution)/shard_map/ppermute | solution.py:592
  39.7 14.9 %collective-permute-start.3 = (bf16[2,128,768]{2,1,0:T(8,128)(2,1)S(1)}, bf16[2,128,768]{2,1,0:T(8,128)(2,1)S(1)}, u32[]{:S(2)}, u32[]{:S(2)}) collective-permute-start(bf16[2,128,768]{2,1,0:T(8,128)(2,1)S(1)} %join.8), channel_id=1, source_target_pairs={{0,8},{4,12},{8,0},{12,4},{16,24},{20,28},{24,16},{28,20},{1,9},{5... | collective-permute-start | bytes 1179656 | tf_op jit(solution)/shard_map/ppermute | solution.py:592
  50.8 19.2 %collective-permute-start.9 = (bf16[2,2,128,768]{3,2,1,0:T(8,128)(2,1)S(1)}, bf16[2,2,128,768]{3,2,1,0:T(8,128)(2,1)}, u32[]{:S(2)}, u32[]{:S(2)}) collective-permute-start(bf16[2,2,128,768]{3,2,1,0:T(8,128)(2,1)S(1)} %join.11.refs_4_), channel_id=1, source_target_pairs={{0,8},{4,12},{8,0},{12,4},{16,24},{20,28},{24,16},{28,20},{1,9},{5... | collective-permute-start | bytes 2359304 | tf_op jit(solution)/shard_map/ppermute | solution.py:592
  54.7 16.7 %collective-permute-start.4 = (bf16[2,2,128,768]{3,2,1,0:T(8,128)(2,1)S(1)}, bf16[2,2,128,768]{3,2,1,0:T(8,128)(2,1)}, u32[]{:S(2)}, u32[]{:S(2)}) collective-permute-start(bf16[2,2,128,768]{3,2,1,0:T(8,128)(2,1)S(1)} %join.10.refs_0_), channel_id=1, source_target_pairs={{0,16},{4,20},{8,24},{12,28},{16,0},{20,4},{24,8},{28,12},{1,17},{... | collective-permute-start | bytes 2359304 | tf_op jit(solution)/shard_map/ppermute | solution.py:592
  55.5 17.7 %collective-permute-start.13 = (bf16[128,896]{1,0:T(8,128)(2,1)S(1)}, bf16[128,896]{1,0:T(8,128)(2,1)S(1)}, u32[]{:S(2)}, u32[]{:S(2)}) collective-permute-start(bf16[128,896]{1,0:T(8,128)(2,1)S(1)} %copy-done.48), channel_id=1, source_target_pairs={{0,2},{1,3},{2,0},{3,1},{4,6},{5,7},{6,4},{7,5},{8,10},{9,11},{10,... | collective-permute-start | bytes 688136 | tf_op jit(solution)/shard_map/ppermute | solution.py:596
  59.5 14.5 %collective-permute-start.12 = (bf16[128,896]{1,0:T(8,128)(2,1)S(1)}, bf16[128,896]{1,0:T(8,128)(2,1)S(1)}, u32[]{:S(2)}, u32[]{:S(2)}) collective-permute-start(bf16[128,896]{1,0:T(8,128)(2,1)S(1)} %copy-done.48), channel_id=1, source_target_pairs={{0,1},{1,2},{2,3},{3,0},{4,5},{5,6},{6,7},{7,4},{8,9},{9,10},{10,1... | collective-permute-start | bytes 688136 | tf_op jit(solution)/shard_map/ppermute | solution.py:596
  70.0 22.3 %collective-permute-start.10 = (bf16[2,2,128,768]{3,2,1,0:T(8,128)(2,1)S(1)}, bf16[2,2,128,768]{3,2,1,0:T(8,128)(2,1)}, u32[]{:S(2)}, u32[]{:S(2)}) collective-permute-start(bf16[2,2,128,768]{3,2,1,0:T(8,128)(2,1)S(1)} %join.11.refs_4_), channel_id=1, source_target_pairs={{0,4},{4,0},{8,12},{12,8},{16,20},{20,16},{24,28},{28,24},{1,5},{5... | collective-permute-start | bytes 2359304 | tf_op jit(solution)/shard_map/ppermute | solution.py:592
  70.0 22.3 %collective-permute-start.11 = (bf16[2,2,128,768]{3,2,1,0:T(8,128)(2,1)}, bf16[2,2,128,768]{3,2,1,0:T(8,128)(2,1)}, u32[]{:S(2)}, u32[]{:S(2)}) collective-permute-start(bf16[2,2,128,768]{3,2,1,0:T(8,128)(2,1)} %collective-permute-done.9.refs_5_), channel_id=1, source_target_pairs={{0,4},{4,0},{8,12},{12,8},{16,20},{20,16},{24,28},{28,24},{1,5},{5... | collective-permute-start | bytes 2359304 | tf_op jit(solution)/shard_map/ppermute | solution.py:592
  71.4 20.9 %collective-permute-start.6 = (bf16[2,2,128,768]{3,2,1,0:T(8,128)(2,1)S(1)}, bf16[2,2,128,768]{3,2,1,0:T(8,128)(2,1)}, u32[]{:S(2)}, u32[]{:S(2)}) collective-permute-start(bf16[2,2,128,768]{3,2,1,0:T(8,128)(2,1)S(1)} %join.10.refs_0_), channel_id=1, source_target_pairs={{0,4},{4,0},{8,12},{12,8},{16,20},{20,16},{24,28},{28,24},{1,5},{5... | collective-permute-start | bytes 2359304 | tf_op jit(solution)/shard_map/ppermute | solution.py:592
  73.3 19.0 %collective-permute-start.7 = (bf16[2,2,128,768]{3,2,1,0:T(8,128)(2,1)}, bf16[2,2,128,768]{3,2,1,0:T(8,128)(2,1)}, u32[]{:S(2)}, u32[]{:S(2)}) collective-permute-start(bf16[2,2,128,768]{3,2,1,0:T(8,128)(2,1)} %collective-permute-done.4.refs_1_), channel_id=1, source_target_pairs={{0,4},{4,0},{8,12},{12,8},{16,20},{20,16},{24,28},{28,24},{1,5},{5... | collective-permute-start | bytes 2359304 | tf_op jit(solution)/shard_map/ppermute | solution.py:592
  74.0 17.5 %collective-permute-start.14 = (bf16[128,896]{1,0:T(8,128)(2,1)S(1)}, bf16[128,896]{1,0:T(8,128)(2,1)S(1)}, u32[]{:S(2)}, u32[]{:S(2)}) collective-permute-start(bf16[128,896]{1,0:T(8,128)(2,1)S(1)} %copy-done.48), channel_id=1, source_target_pairs={{0,3},{1,0},{2,1},{3,2},{4,7},{5,4},{6,5},{7,6},{8,11},{9,8},{10,9... | collective-permute-start | bytes 688136 | tf_op jit(solution)/shard_map/ppermute | solution.py:596
  101.9 22.7 %collective-permute-start.16 = (bf16[2,128,896]{2,1,0:T(8,128)(2,1)S(1)}, bf16[2,128,896]{2,1,0:T(8,128)(2,1)S(1)}, u32[]{:S(2)}, u32[]{:S(2)}) collective-permute-start(bf16[2,128,896]{2,1,0:T(8,128)(2,1)S(1)} %join.13), channel_id=1, source_target_pairs={{0,16},{4,20},{8,24},{12,28},{16,0},{20,4},{24,8},{28,12},{1,17},{... | collective-permute-start | bytes 1376264 | tf_op jit(solution)/shard_map/ppermute | solution.py:592
  102.0 23.6 %collective-permute-start.15 = (bf16[2,128,896]{2,1,0:T(8,128)(2,1)S(1)}, bf16[2,128,896]{2,1,0:T(8,128)(2,1)S(1)}, u32[]{:S(2)}, u32[]{:S(2)}) collective-permute-start(bf16[2,128,896]{2,1,0:T(8,128)(2,1)S(1)} %join.12), channel_id=1, source_target_pairs={{0,8},{4,12},{8,0},{12,4},{16,24},{20,28},{24,16},{28,20},{1,9},{5... | collective-permute-start | bytes 1376264 | tf_op jit(solution)/shard_map/ppermute | solution.py:592
  103.6 23.0 %collective-permute-start.17 = (bf16[512,256]{1,0:T(8,128)(2,1)}, bf16[512,256]{1,0:T(8,128)(2,1)S(1)}, u32[]{:S(2)}, u32[]{:S(2)}) collective-permute-start(bf16[512,256]{1,0:T(8,128)(2,1)} %get-tuple-element.122.refs_2_), channel_id=1, source_target_pairs={{0,2},{1,3},{4,6},{5,7},{8,10},{9,11},{12,14},{13,15},{16,18},{17,... | collective-permute-start | bytes 786440 | tf_op jit(solution)/shard_map/ppermute | solution.py:600
  105.0 23.4 %collective-permute-start.18 = (bf16[512,256]{1,0:T(8,128)(2,1)}, bf16[512,256]{1,0:T(8,128)(2,1)S(1)}, u32[]{:S(2)}, u32[]{:S(2)}) collective-permute-start(bf16[512,256]{1,0:T(8,128)(2,1)} %get-tuple-element.122.refs_2_), channel_id=1, source_target_pairs={{0,1},{1,2},{2,3},{4,5},{5,6},{6,7},{8,9},{9,10},{10,11},{12,13},{... | collective-permute-start | bytes 786440 | tf_op jit(solution)/shard_map/ppermute | solution.py:600
  129.0 43.1 %collective-permute-start.24 = (bf16[2,2,128,896]{3,2,1,0:T(8,128)(2,1)}, bf16[2,2,128,896]{3,2,1,0:T(8,128)(2,1)}, u32[]{:S(2)}, u32[]{:S(2)}) collective-permute-start(bf16[2,2,128,896]{3,2,1,0:T(8,128)(2,1)} %join.15.refs_4_), channel_id=1, source_target_pairs={{0,8},{4,12},{8,0},{12,4},{16,24},{20,28},{24,16},{28,20},{1,9},{5... | collective-permute-start | bytes 2752520 | tf_op jit(solution)/shard_map/ppermute | solution.py:592
  129.6 42.9 %collective-permute-start.19 = (bf16[2,2,128,896]{3,2,1,0:T(8,128)(2,1)}, bf16[2,2,128,896]{3,2,1,0:T(8,128)(2,1)}, u32[]{:S(2)}, u32[]{:S(2)}) collective-permute-start(bf16[2,2,128,896]{3,2,1,0:T(8,128)(2,1)} %join.14.refs_0_), channel_id=1, source_target_pairs={{0,16},{4,20},{8,24},{12,28},{16,0},{20,4},{24,8},{28,12},{1,17},{... | collective-permute-start | bytes 2752520 | tf_op jit(solution)/shard_map/ppermute | solution.py:592
  131.7 35.5 %collective-permute-start.20 = (bf16[144,1536]{1,0:T(8,128)(2,1)}, bf16[144,1536]{1,0:T(8,128)(2,1)}, u32[]{:S(2)}, u32[]{:S(2)}) collective-permute-start(bf16[144,1536]{1,0:T(8,128)(2,1)} %get-tuple-element.139), channel_id=1, source_target_pairs={{0,1},{1,2},{2,3},{4,5},{5,6},{6,7},{8,9},{9,10},{10,11},{12,13},{... | collective-permute-start | bytes 1327112 | tf_op jit(solution)/shard_map/ppermute | solution.py:600
  151.9 20.2 %collective-permute-start.21 = (bf16[144,1536]{1,0:T(8,128)(2,1)}, bf16[144,1536]{1,0:T(8,128)(2,1)}, u32[]{:S(2)}, u32[]{:S(2)}) collective-permute-start(bf16[144,1536]{1,0:T(8,128)(2,1)} %get-tuple-element.139), channel_id=1, source_target_pairs={{0,2},{1,3},{4,6},{5,7},{8,10},{9,11},{12,14},{13,15},{16,18},{17,... | collective-permute-start | bytes 1327112 | tf_op jit(solution)/shard_map/ppermute | solution.py:600
  237.3 202.0 %reduce-scatter.5.cloned.1.call-start = ((), (), s32[]{:S(2)}) async-start(), calls=%async_computation.4 | async-start | bytes 1966080 | tf_op jit(solution)/shard_map/reduce_scatter | solution.py:1155
  251.1 22.7 %collective-permute-start.27 = (bf16[144,1536]{1,0:T(8,128)(2,1)S(1)}, bf16[144,1536]{1,0:T(8,128)(2,1)S(1)}, u32[]{:S(2)}, u32[]{:S(2)}) collective-permute-start(bf16[144,1536]{1,0:T(8,128)(2,1)S(1)} %get-tuple-element.166), channel_id=1, source_target_pairs={{1,0},{2,1},{3,2},{5,4},{6,5},{7,6},{9,8},{10,9},{11,10},{13,12},{... | collective-permute-start | bytes 1327112 | tf_op jit(solution)/shard_map/ppermute | solution.py:600
  252.4 41.5 %collective-permute-start.28 = (bf16[144,1536]{1,0:T(8,128)(2,1)S(1)}, bf16[144,1536]{1,0:T(8,128)(2,1)S(1)}, u32[]{:S(2)}, u32[]{:S(2)}) collective-permute-start(bf16[144,1536]{1,0:T(8,128)(2,1)S(1)} %get-tuple-element.166), channel_id=1, source_target_pairs={{2,0},{3,1},{6,4},{7,5},{10,8},{11,9},{14,12},{15,13},{18,16},{19,... | collective-permute-start | bytes 1327112 | tf_op jit(solution)/shard_map/ppermute | solution.py:600
  306.8 34.2 %collective-permute-start.30 = (bf16[4,4,128,1024]{3,2,1,0:T(8,128)(2,1)}, bf16[4,4,128,1024]{3,2,1,0:T(8,128)(2,1)}, u32[]{:S(2)}, u32[]{:S(2)}) collective-permute-start(bf16[4,4,128,1024]{3,2,1,0:T(8,128)(2,1)} %get-tuple-element.168), channel_id=1, source_target_pairs={{0,4},{4,0},{8,12},{12,8},{16,20},{20,16},{24,28},{28,24},{1,5},{5... | collective-permute-start | bytes 12582920 | tf_op jit(solution)/shard_map/ppermute | solution.py:592
  306.8 30.4 %collective-permute-start.31 = (bf16[512,256]{1,0:T(8,128)(2,1)S(1)}, bf16[512,256]{1,0:T(8,128)(2,1)S(1)}, u32[]{:S(2)}, u32[]{:S(2)}) collective-permute-start(bf16[512,256]{1,0:T(8,128)(2,1)S(1)} %get-tuple-element.178), channel_id=1, source_target_pairs={{1,0},{2,1},{3,2},{5,4},{6,5},{7,6},{9,8},{10,9},{11,10},{13,12},{... | collective-permute-start | bytes 786440 | tf_op jit(solution)/shard_map/ppermute | solution.py:600
  308.1 29.1 %collective-permute-start.32 = (bf16[512,256]{1,0:T(8,128)(2,1)S(1)}, bf16[512,256]{1,0:T(8,128)(2,1)S(1)}, u32[]{:S(2)}, u32[]{:S(2)}) collective-permute-start(bf16[512,256]{1,0:T(8,128)(2,1)S(1)} %get-tuple-element.179), channel_id=1, source_target_pairs={{2,0},{3,1},{6,4},{7,5},{10,8},{11,9},{14,12},{15,13},{18,16},{19,... | collective-permute-start | bytes 786440 | tf_op jit(solution)/shard_map/ppermute | solution.py:600
  335.7 9.9 %collective-permute-start.29 = (f32[8,1792]{1,0:T(8,128)S(1)}, f32[8,1792]{1,0:T(8,128)S(1)}, u32[]{:S(2)}, u32[]{:S(2)}) collective-permute-start(f32[8,1792]{1,0:T(8,128)S(1)} %slice.365), channel_id=1, source_target_pairs={{1,0},{2,1},{3,2},{5,4},{6,5},{7,6},{9,8},{10,9},{11,10},{13,12},{... | collective-permute-start | bytes 172040 | tf_op jit(solution)/shard_map/ppermute | solution.py:600
  360.7 36.4 %collective-permute-start.35 = (bf16[4,4,128,640]{3,2,1,0:T(8,128)(2,1)}, bf16[4,4,128,640]{3,2,1,0:T(8,128)(2,1)}, u32[]{:S(2)}, u32[]{:S(2)}) collective-permute-start(bf16[4,4,128,640]{3,2,1,0:T(8,128)(2,1)} %get-tuple-element.184), channel_id=1, source_target_pairs={{0,4},{4,0},{8,12},{12,8},{16,20},{20,16},{24,28},{28,24},{1,5},{5... | collective-permute-start | bytes 7864328 | tf_op jit(solution)/shard_map/ppermute | solution.py:592
  361.2 25.5 %collective-permute-start.33 = (bf16[2,2,128,1024]{3,2,1,0:T(8,128)(2,1)}, bf16[2,2,128,1024]{3,2,1,0:T(8,128)(2,1)}, u32[]{:S(2)}, u32[]{:S(2)}) collective-permute-start(bf16[2,2,128,1024]{3,2,1,0:T(8,128)(2,1)} %get-tuple-element.339), channel_id=1, source_target_pairs={{0,16},{4,20},{8,24},{12,28},{16,0},{20,4},{24,8},{28,12},{1,17},{... | collective-permute-start | bytes 3145736 | tf_op jit(solution)/shard_map/ppermute | solution.py:592
  363.1 27.9 %collective-permute-start.34 = (bf16[2,2,128,1024]{3,2,1,0:T(8,128)(2,1)S(1)}, bf16[2,2,128,1024]{3,2,1,0:T(8,128)(2,1)}, u32[]{:S(2)}, u32[]{:S(2)}) collective-permute-start(bf16[2,2,128,1024]{3,2,1,0:T(8,128)(2,1)S(1)} %get-tuple-element.337), channel_id=1, source_target_pairs={{0,8},{4,12},{8,0},{12,4},{16,24},{20,28},{24,16},{28,20},{1,9},{5... | collective-permute-start | bytes 3145736 | tf_op jit(solution)/shard_map/ppermute | solution.py:592
  389.3 30.0 %collective-permute-start.42 = (bf16[2,1,128,1024]{3,2,1,0:T(8,128)(2,1)}, bf16[2,1,128,1024]{3,2,1,0:T(8,128)(2,1)}, u32[]{:S(2)}, u32[]{:S(2)}) collective-permute-start(bf16[2,1,128,1024]{3,2,1,0:T(8,128)(2,1)} %get-tuple-element.347), channel_id=1, source_target_pairs={{0,8},{4,12},{8,0},{12,4},{16,24},{20,28},{24,16},{28,20},{1,9},{5... | collective-permute-start | bytes 1572872 | tf_op jit(solution)/shard_map/ppermute | solution.py:592
  393.5 35.1 %collective-permute-start.43 = (bf16[2,1,128,1024]{3,2,1,0:T(8,128)(2,1)}, bf16[2,1,128,1024]{3,2,1,0:T(8,128)(2,1)}, u32[]{:S(2)}, u32[]{:S(2)}) collective-permute-start(bf16[2,1,128,1024]{3,2,1,0:T(8,128)(2,1)} %get-tuple-element.345), channel_id=1, source_target_pairs={{0,16},{4,20},{8,24},{12,28},{16,0},{20,4},{24,8},{28,12},{1,17},{... | collective-permute-start | bytes 1572872 | tf_op jit(solution)/shard_map/ppermute | solution.py:592
  400.9 41.2 %collective-permute-start.44 = (bf16[2,2,128,640]{3,2,1,0:T(8,128)(2,1)}, bf16[2,2,128,640]{3,2,1,0:T(8,128)(2,1)}, u32[]{:S(2)}, u32[]{:S(2)}) collective-permute-start(bf16[2,2,128,640]{3,2,1,0:T(8,128)(2,1)} %get-tuple-element.343), channel_id=1, source_target_pairs={{0,16},{4,20},{8,24},{12,28},{16,0},{20,4},{24,8},{28,12},{1,17},{... | collective-permute-start | bytes 1966088 | tf_op jit(solution)/shard_map/ppermute | solution.py:592
  401.3 43.6 %collective-permute-start.45 = (bf16[2,2,128,640]{3,2,1,0:T(8,128)(2,1)}, bf16[2,2,128,640]{3,2,1,0:T(8,128)(2,1)}, u32[]{:S(2)}, u32[]{:S(2)}) collective-permute-start(bf16[2,2,128,640]{3,2,1,0:T(8,128)(2,1)} %get-tuple-element.341), channel_id=1, source_target_pairs={{0,8},{4,12},{8,0},{12,4},{16,24},{20,28},{24,16},{28,20},{1,9},{5... | collective-permute-start | bytes 1966088 | tf_op jit(solution)/shard_map/ppermute | solution.py:592
  421.7 10.2 %collective-permute-start.39 = (f32[88,128]{1,0:T(8,128)S(1)}, f32[88,128]{1,0:T(8,128)S(1)}, u32[]{:S(2)}, u32[]{:S(2)}) collective-permute-start(f32[88,128]{1,0:T(8,128)S(1)} %add.256), channel_id=1, source_target_pairs={{0,1},{1,2},{2,3},{3,0},{4,5},{5,6},{6,7},{7,4},{8,9},{9,10},{10,1... | collective-permute-start | bytes 135176 | tf_op jit(solution)/shard_map/ppermute | solution.py:596
  425.3 8.6 %collective-permute-start.40 = (f32[88,128]{1,0:T(8,128)S(1)}, f32[88,128]{1,0:T(8,128)S(1)}, u32[]{:S(2)}, u32[]{:S(2)}) collective-permute-start(f32[88,128]{1,0:T(8,128)S(1)} %add.256), channel_id=1, source_target_pairs={{0,2},{1,3},{2,0},{3,1},{4,6},{5,7},{6,4},{7,5},{8,10},{9,11},{10,... | collective-permute-start | bytes 135176 | tf_op jit(solution)/shard_map/ppermute | solution.py:596
  432.0 15.7 %collective-permute-start.46 = (bf16[128,1024]{1,0:T(8,128)(2,1)}, bf16[128,1024]{1,0:T(8,128)(2,1)}, u32[]{:S(2)}, u32[]{:S(2)}) collective-permute-start(bf16[128,1024]{1,0:T(8,128)(2,1)} %get-tuple-element.353), channel_id=1, source_target_pairs={{0,3},{1,0},{2,1},{3,2},{4,7},{5,4},{6,5},{7,6},{8,11},{9,8},{10,9... | collective-permute-start | bytes 786440 | tf_op jit(solution)/shard_map/ppermute | solution.py:596
  433.9 23.5 %collective-permute-start.47 = (bf16[128,1024]{1,0:T(8,128)(2,1)}, bf16[128,1024]{1,0:T(8,128)(2,1)}, u32[]{:S(2)}, u32[]{:S(2)}) collective-permute-start(bf16[128,1024]{1,0:T(8,128)(2,1)} %get-tuple-element.354), channel_id=1, source_target_pairs={{0,2},{1,3},{2,0},{3,1},{4,6},{5,7},{6,4},{7,5},{8,10},{9,11},{10,... | collective-permute-start | bytes 786440 | tf_op jit(solution)/shard_map/ppermute | solution.py:596
  434.4 23.0 %collective-permute-start.48 = (bf16[128,1024]{1,0:T(8,128)(2,1)}, bf16[128,1024]{1,0:T(8,128)(2,1)}, u32[]{:S(2)}, u32[]{:S(2)}) collective-permute-start(bf16[128,1024]{1,0:T(8,128)(2,1)} %get-tuple-element.355), channel_id=1, source_target_pairs={{0,1},{1,2},{2,3},{3,0},{4,5},{5,6},{6,7},{7,4},{8,9},{9,10},{10,1... | collective-permute-start | bytes 786440 | tf_op jit(solution)/shard_map/ppermute | solution.py:596
  443.4 16.8 %collective-permute-start.49 = (bf16[2,1,128,640]{3,2,1,0:T(8,128)(2,1)S(1)}, bf16[2,1,128,640]{3,2,1,0:T(8,128)(2,1)S(1)}, u32[]{:S(2)}, u32[]{:S(2)}) collective-permute-start(bf16[2,1,128,640]{3,2,1,0:T(8,128)(2,1)S(1)} %get-tuple-element.351), channel_id=1, source_target_pairs={{0,8},{4,12},{8,0},{12,4},{16,24},{20,28},{24,16},{28,20},{1,9},{5... | collective-permute-start | bytes 983048 | tf_op jit(solution)/shard_map/ppermute | solution.py:592
  446.2 14.2 %collective-permute-start.50 = (bf16[2,1,128,640]{3,2,1,0:T(8,128)(2,1)S(1)}, bf16[2,1,128,640]{3,2,1,0:T(8,128)(2,1)S(1)}, u32[]{:S(2)}, u32[]{:S(2)}) collective-permute-start(bf16[2,1,128,640]{3,2,1,0:T(8,128)(2,1)S(1)} %get-tuple-element.349), channel_id=1, source_target_pairs={{0,16},{4,20},{8,24},{12,28},{16,0},{20,4},{24,8},{28,12},{1,17},{... | collective-permute-start | bytes 983048 | tf_op jit(solution)/shard_map/ppermute | solution.py:592
  460.7 15.6 %collective-permute-start.52 = (bf16[128,640]{1,0:T(8,128)(2,1)S(1)}, bf16[128,640]{1,0:T(8,128)(2,1)S(1)}, u32[]{:S(2)}, u32[]{:S(2)}) collective-permute-start(bf16[128,640]{1,0:T(8,128)(2,1)S(1)} %maximum_maximum_fusion.1), channel_id=1, source_target_pairs={{0,2},{1,3},{2,0},{3,1},{4,6},{5,7},{6,4},{7,5},{8,10},{9,11},{10,... | collective-permute-start | bytes 491528 | tf_op jit(solution)/shard_map/ppermute | solution.py:596
  461.5 14.8 %collective-permute-start.53 = (bf16[128,640]{1,0:T(8,128)(2,1)S(1)}, bf16[128,640]{1,0:T(8,128)(2,1)S(1)}, u32[]{:S(2)}, u32[]{:S(2)}) collective-permute-start(bf16[128,640]{1,0:T(8,128)(2,1)S(1)} %maximum_maximum_fusion.2), channel_id=1, source_target_pairs={{0,1},{1,2},{2,3},{3,0},{4,5},{5,6},{6,7},{7,4},{8,9},{9,10},{10,1... | collective-permute-start | bytes 491528 | tf_op jit(solution)/shard_map/ppermute | solution.py:596
  (108 other events, 1573.8 us)
Sparse Core Ops, SparseCore 0:
  30.6 127.3 all-gather.1
  237.4 103.2 reduce-scatter.2
  395.3 39.2 reduce-scatter.4

commit v4 on v3

--- a/solution.py
+++ b/solution.py
@@ -362,8 +362,9 @@
     affinity = dot(cm, b, NT)
     cum = cum_ref[...]
     dt = dt_ref[...]
-    dt_wide = widen(dt, spread2)
-    ec_wide = widen(ec_ref[...], spread2)
+    wide = widen(jnp.concatenate([dt, ec_ref[...], fw_ref[...] * dt, g_ref[...]], axis=0), spread2)
+    dt_wide, ec_wide, weight = wide[:SPAN], wide[SPAN : 2 * SPAN], wide[2 * SPAN : 3 * SPAN]
+    gain = wide[3 * SPAN : 3 * SPAN + 1]
     carried = dot(cm, state) * ec_wide
     for p in range(MH // 2):
         lanes = slice(p * LANE, (p + 1) * LANE)
@@ -378,9 +379,7 @@
         z = z_ref[:, lanes]
         full_ref[:, lanes] = y.astype(bf16)
         gated_ref[:, lanes] = (y * (z * jax.nn.sigmoid(z))).astype(bf16)
-    weight = widen(fw_ref[...] * dt, spread2)
     x = mix_ref[:, :INNER].astype(f32)
-    gain = widen(g_ref[...], spread2)[0:1, :]
     state_ref[...] = state_ref[...] * gain + dot(b, (x * weight).astype(bf16), TN)
 
 
@@ -464,7 +463,9 @@
     cm = mix_ref[:, INNER + NS :]
     cum = cum_ref[...]
     dt = dt_ref[...]
-    dt_wide = widen(dt, spread2)
+    wide = widen(jnp.concatenate([dt, ec_ref[...], fw_ref[...], g_ref[...]], axis=0), spread2)
+    dt_wide, ec_wide, fw_wide = wide[:SPAN], wide[SPAN : 2 * SPAN], wide[2 * SPAN : 3 * SPAN]
+    gain = wide[3 * SPAN : 3 * SPAN + 1]
     s, t = tri_masks()
     allowed = (segc_ref[...] == segr_ref[...]) & (t >= s)
     off = jnp.where(allowed, 0.0, NEG)
@@ -496,20 +497,18 @@
     dstate = dstate_ref[...]
     dstate_low = dstate.astype(bf16)
     state = states_ref[0]
-    ec_wide = widen(ec_ref[...], spread2)
-    fw_wide = widen(fw_ref[...], spread2)
     from_state = fw_wide * dot(b, dstate_low)
     carried = ec_wide * dot(cm, state)
     weighted_dy = (dy * ec_wide).astype(bf16)
-    cols_sum = dot(split2(scaled * dscaled), gather2)
-    carr_sum = dot(split2(dy * carried), gather2)
-    fdf_sum = dot(split2(scaled * from_state), gather2)
     dxd = dscaled + from_state
-    ddt_direct = dot(split2(x * dxd), gather2)
-    skip_part = dot(split2(dy * x), gather2)
-    gain = widen(g_ref[...], spread2)[0:1, :]
     state_dot = jnp.sum(dstate * state.astype(f32), axis=0, keepdims=True) * gain
-    state_dot = dot(split2(jnp.broadcast_to(state_dot, (8, INNER))), gather2)[0:1, :]
+    sums = [split2(scaled * dscaled, axis=0)]
+    sums += [v.astype(bf16) for v in (dy * carried, scaled * from_state, x * dxd, dy * x)]
+    sums.append(split2(jnp.broadcast_to(state_dot, (16, INNER)), axis=0))
+    sums = dot(jnp.concatenate(sums, axis=0), gather2[:INNER, :])
+    cols_sum = sums[:SPAN] + sums[SPAN : 2 * SPAN]
+    carr_sum, fdf_sum, ddt_direct, skip_part = [sums[n * SPAN : (n + 1) * SPAN] for n in range(2, 6)]
+    state_dot = sums[6 * SPAN : 6 * SPAN + 1] + sums[6 * SPAN + 16 : 6 * SPAN + 17]
     tt, ss = tri_masks()
     suffix = (ss >= tt).astype(bf16)
     prefix = (ss < tt).astype(bf16)
@@ -898,7 +897,7 @@
 
 def left_rows(index_ref, left_ref, half, side):
     rows = left_ref.shape[0] // NB
-    order = [LOW.index(m) for m in SET_MASKS[side]]
+    order = [0, 1 + side, 2 - side, 3]
     return jnp.concatenate([left_ref[block_rows(index_ref, 4 * half + m, rows), :] for m in order], axis=0)
 
 
@@ -906,22 +905,22 @@
     lefts = refs[:n_left]
     rights = refs[n_left : n_left + n_right]
     sent_ref, kept_ref = refs[n_left + n_right :]
-    for s in range(4):
-        for half, out in ((1, sent_ref), (0, kept_ref)):
-            cache = {}
-            at = 0
-            for left, right, width, kind in plan:
-                if kind == "fixed":
-                    value = rights[right][:, s * width : (s + 1) * width]
-                elif kind == "all":
-                    value = rights[right][...]
-                else:
-                    value = rights[right][:, part_columns(index_ref, s, width)]
-                if left not in cache:
-                    cache[left] = left_rows(index_ref, lefts[left], half, s // 2)
-                result = dot(cache[left], value)
-                out[s, :, :, at : at + width] = result.reshape(4, -1, width).astype(bf16)
-                at += width
+    s = pl.program_id(0)
+    for half, out in ((1, sent_ref), (0, kept_ref)):
+        cache = {}
+        at = 0
+        for left, right, width, kind in plan:
+            if kind == "fixed":
+                value = rights[right][:, pl.ds(pl.multiple_of(s * width, width), width)]
+            elif kind == "all":
+                value = rights[right][...]
+            else:
+                value = rights[right][:, part_columns(index_ref, s, width)]
+            if left not in cache:
+                cache[left] = left_rows(index_ref, lefts[left], half, s // 2)
+            result = dot(cache[left], value)
+            out[0, :, :, at : at + width] = result.reshape(4, -1, width).astype(bf16)
+            at += width
 
 
 def weight_grads(index, lefts, rights, plan):
@@ -930,10 +929,10 @@
     outs = (sds((4, 4, rows, columns), bf16),) * 2
     return pl.pallas_call(
         functools.partial(grad_kernel, plan, len(lefts), len(rights)),
-        grid=(1,),
+        grid=(4,),
         out_shape=outs,
         in_specs=[SMEM] + wholes(lefts) + wholes(rights),
-        out_specs=tuple(wholes(outs)),
+        out_specs=(pl.BlockSpec((1, 4, rows, columns), lambda s: (s, 0, 0, 0)),) * 2,
         compiler_params=params(56),
         cost_estimate=COST,
         name="weight_grads",
@@ -1198,9 +1197,10 @@
     )
 
     plan1 = ((0, 0, widths1[2], "part"), (0, 1, LANE, "all"), (0, 2, quarter, "fixed"))
+    quarters2 = ring.scatter_first([(out, after([mine], d_x)[0]) for out, mine in halves2])
+    (d_shared,) = after([d_shared], quarters2)
     sent1, kept1 = weight_grads(index, (normed_t,), (d_x, d_step, d_shared), plan1)
-    quarters2 = ring.scatter_first([(out, after([mine], sent1)[0]) for out, mine in halves2])
-    halves1 = ring.scatter_sibling(sent1, after([kept1], quarters2)[0])
+    halves1 = ring.scatter_sibling(sent1, kept1)
     parts2 = ring.scatter_second([(out, after([mine], halves1)[0]) for out, mine in quarters2])
     quarters1 = ring.scatter_first([(out, after([mine], parts2)[0]) for out, mine in halves1])
     grads2 = ring.collect(after(parts2[:1], quarters1) + tuple(parts2[1:]))

time: 496 us -> 483 us (0.974)
  starting transfers between devices: 89 us -> 79.1 us
    ppermute x26, waiting for transfers between devices: 54.6 us -> 34.5 us  [dp(): return lax.ppermute(value, 'dp', [(i, i ^ step) for i in range(self.nd)])]
    ppermute x10, waiting for transfers between devices: 35.2 us -> 49.4 us  [line(): lax.ppermute(value, 'tensor', [(i, i + s) for i in range(n) if 0 <= i + s...]
    ppermute x3, waiting for transfers between devices: 1.92 us -> 10 us  [all_sum(): lax.ppermute(value, 'dp', [(i, i ^ bit) for i in range(self.nd)])]
  transfers between devices with their start and end apart: 57 -> 57, of which waited for: 23 -> 24; matrix products, arithmetic and copies ran while one was open for 12% -> 11% of each run, Pallas kernels for 24% -> 25%
where the time goes in v4:
time: 483 us; the launch traced here: 473 us
  Pallas kernels  157 us (33%)
  waiting for transfers between devices  141 us (29%)
  starting transfers between devices  79.1 us (16%)
  local copies, waits for them, and re-layouts  35.7 us (7%)
  other arithmetic  33 us (7%)
  between operations  15.5 us (3%)
  matrix products  11.4 us (2%)
    ppermute x10, waiting for transfers between devices, line(): lax.ppermute(value, 'tensor', [(i, i + s) for i in range(n) if 0 <= i + s...  49.4 us
    ppermute x15, waiting for transfers between devices, shift(): return lax.ppermute(value, 'tensor', [(i, (i + s) % n) for i in range(n)])  46.8 us
    ppermute x10, starting transfers between devices, line(): lax.ppermute(value, 'tensor', [(i, i + s) for i in range(n) if 0 <= i + s...  40.3 us
    ppermute x26, waiting for transfers between devices, dp(): return lax.ppermute(value, 'dp', [(i, i ^ step) for i in range(self.nd)])  34.5 us
    pallas_call x8, Pallas kernels, simple_call(): pl.pallas_call(kernel, grid=(1,), out_shape=outs, in_specs=wholes(arrays)...  33.9 us
    pallas_call x1, Pallas kernels, ffn(): pl.pallas_call(ffn_kernel, grid_spec=pltpu.PrefetchScalarGridSpec(num_sca...  28.7 us
    pallas_call x1, Pallas kernels, mamba_bwd(): pl.pallas_call(mamba_bwd_kernel, grid=(n,), in_specs=[rev(width), rev(LAN...  24.2 us
    unnamed x203, local copies, waits for them, and re-layouts  22.2 us
  transfers between devices with their start and end apart: 57, of which 24 were waited for; matrix products, arithmetic and copies ran while one was open for 11% of the time, Pallas kernels for 25%

profile of v4, /device:TPU:0, one launch (start us, length us, event | category | flops | bytes accessed | tf_op | source)
XLA Modules:
  0.0 473.0 jit_solution(8314241848673013449)
XLA Ops:
  11.3 4.3 collective-permute-start.1
  17.6 3.8 norm_in.1
  23.4 6.9 %collective-permute-done.refs_1_ = bf16[128,768]{1,0:T(8,128)(2,1)S(1)} collective-permute-done((bf16[128,768]{1,0:T(8,128)(2,1)}, bf16[128,768]{1,0:T(8,128)(2,1)S(1)}, u32[]{:S(2)}, u32[]{:S(2)}) %collective-permute-start) | collective-permute-done | bytes 196640 | tf_op jit(solution)/shard_map/ppermute | solution.py:595
  31.3 5.8 %collective-permute-start.5 = (bf16[16,1024]{1,0:T(8,128)(2,1)S(1)}, bf16[16,1024]{1,0:T(8,128)(2,1)S(1)}, u32[]{:S(2)}, u32[]{:S(2)}) collective-permute-start(bf16[16,1024]{1,0:T(8,128)(2,1)S(1)} %slice.358), channel_id=1, source_target_pairs={{0,1},{1,2},{2,3},{4,5},{5,6},{6,7},{8,9},{9,10},{10,11},{12,13},{... | collective-permute-start | bytes 98312 | tf_op jit(solution)/shard_map/ppermute | solution.py:599
  43.8 6.9 %collective-permute-done.8.refs_2_ = bf16[2,128,768]{2,1,0:T(8,128)(2,1)S(1)} collective-permute-done((bf16[2,128,768]{2,1,0:T(8,128)(2,1)S(1)}, bf16[2,128,768]{2,1,0:T(8,128)(2,1)S(1)}, u32[]{:S(2)}, u32[]{:S(2)}) %collective-permute-start.8) | collective-permute-done | bytes 393248 | tf_op jit(solution)/shard_map/ppermute | solution.py:591
  52.4 2.2 collective-permute-done.3.refs_2_
  59.8 10.2 %collective-permute-done.9.refs_5_ = bf16[2,2,128,768]{3,2,1,0:T(8,128)(2,1)} collective-permute-done((bf16[2,2,128,768]{3,2,1,0:T(8,128)(2,1)S(1)}, bf16[2,2,128,768]{3,2,1,0:T(8,128)(2,1)}, u32[]{:S(2)}, u32[]{:S(2)}) %collective-permute-start.9) | collective-permute-done | bytes 786464 | tf_op jit(solution)/shard_map/ppermute | solution.py:591
  76.2 15.3 %collective-permute-done.14.refs_1_ = bf16[128,896]{1,0:T(8,128)(2,1)S(1)} collective-permute-done((bf16[128,896]{1,0:T(8,128)(2,1)S(1)}, bf16[128,896]{1,0:T(8,128)(2,1)S(1)}, u32[]{:S(2)}, u32[]{:S(2)}) %collective-permute-start.14) | collective-permute-done | bytes 229408 | tf_op jit(solution)/shard_map/ppermute | solution.py:595
  92.3 9.6 %project.1 = (bf16[1024,512]{1,0:T(8,128)(2,1)}, bf16[1024,128]{1,0:T(8,128)(2,1)}, bf16[1024,1536]{1,0:T(8,128)(2,1)}, bf16[1024,512]{1,0:T(8,128)(2,1)}, f32[5...) custom-call(s32[12]{0:T(128)} %stack.115.index_ref, ...), custom_call_target="tpu_custom_call" | custom-call | flops 2000000000 | bytes 4000000 | tf_op jit(solution)/shard_map/project/pallas_call | solution.py:777
  105.0 2.3 collective-permute-start.18
  107.3 2.1 copy-done.4
  110.3 6.6 %mamba_pre.1 = (bf16[512,1792]{1,0:T(8,128)(2,1)S(1)}, f32[512,128]{1,0:T(8,128)S(1)}, f32[512,128]{1,0:T(8,128)S(1)}, f32[32,512]{1,0:T(8,128)S(1)}, f32[512,12...) custom-call(f32[528,1792]{1,0:T(8,128)S(1)} %copy-done.4, ...), custom_call_target="tpu_custom_call" | custom-call | flops 2000000000 | bytes 4000000 | tf_op jit(solution)/shard_map/mamba_pre/pallas_call | solution.py:322
  116.9 7.7 %collective-permute-done.16.refs_2_ = bf16[2,128,896]{2,1,0:T(8,128)(2,1)S(1)} collective-permute-done((bf16[2,128,896]{2,1,0:T(8,128)(2,1)S(1)}, bf16[2,128,896]{2,1,0:T(8,128)(2,1)S(1)}, u32[]{:S(2)}, u32[]{:S(2)}) %collective-permute-start.16) | collective-permute-done | bytes 458784 | tf_op jit(solution)/shard_map/ppermute | solution.py:591
  131.7 20.2 %collective-permute-start.20 = (bf16[144,1536]{1,0:T(8,128)(2,1)}, bf16[144,1536]{1,0:T(8,128)(2,1)}, u32[]{:S(2)}, u32[]{:S(2)}) collective-permute-start(bf16[144,1536]{1,0:T(8,128)(2,1)} %get-tuple-element.139), channel_id=1, source_target_pairs={{0,1},{1,2},{2,3},{4,5},{5,6},{6,7},{8,9},{9,10},{10,11},{12,13},{... | collective-permute-start | bytes 1327112 | tf_op jit(solution)/shard_map/ppermute | solution.py:599
  151.9 4.2 collective-permute-start.21
  159.7 6.6 %attn_fwd.1 = (bf16[512,512]{1,0:T(8,128)(2,1)S(1)}, f32[8,512]{1,0:T(8,128)S(1)}) custom-call(s32[4]{0:T(128)S(1)} %and_select_fusion.first_ref, bf16[512,512]{1,0:T(8,128)(2,1)S(1)} %copy-done.36, s32[1,512]{1,0:T(1,128)S(1)} %bitcast.85, s32[1536,1]{1,0:T(8,128)S(1)} %broadcast_in_dim.53.segk_ref, bf16[512,256]{1,0:T(8,128)(2,1)S(1)} %copy-done.42, ...), custom_call_target="tpu_custom_call" | custom-call | flops 2000000000 | bytes 4000000 | tf_op jit(solution)/shard_map/attn_fwd/pallas_call | solution.py:200
  167.1 4.9 %collective-permute-done.21.refs_1_ = bf16[144,1536]{1,0:T(8,128)(2,1)} collective-permute-done((bf16[144,1536]{1,0:T(8,128)(2,1)}, bf16[144,1536]{1,0:T(8,128)(2,1)}, u32[]{:S(2)}, u32[]{:S(2)}) %collective-permute-start.21) | collective-permute-done | bytes 442400 | tf_op jit(solution)/shard_map/ppermute | solution.py:599
  178.8 6.7 %assemble.1 = (bf16[1024,1536]{1,0:T(8,128)(2,1)}, bf16[1024,512]{1,0:T(8,128)(2,1)}, bf16[1024,1536]{1,0:T(8,128)(2,1)}) custom-call(s32[12]{0:T(128)S(1)} %copy-done.32, bf16[2,2,128,896]{3,2,1,0:T(8,128)(2,1)} %join.14.refs_0_, bf16[2,2,128,896]{3,2,1,0:T(8,128)(2,1)} %collective-permute-done.19.refs_1_, ...), custom_call_target="tpu_custom_call" | custom-call | flops 2000000000 | bytes 4000000 | tf_op jit(solution)/shard_map/assemble/pallas_call | solution.py:730
  185.6 3.7 fusion.36.z_ref
  189.4 6.8 %mamba_fwd.1 = (bf16[512,1536]{1,0:T(8,128)(2,1)S(1)}, bf16[512,1536]{1,0:T(8,128)(2,1)S(1)}, bf16[4,128,1536]{2,1,0:T(8,128)(2,1)S(1)}) custom-call(bf16[512,1792]{1,0:T(8,128)(2,1)S(1)} %get-tuple-element.128.mix_ref.cm_ref, f32[512,128]{1,0:T(8,128)S(1)} %get-tuple-element.133.dt_ref, f32[512,128]{1,0:T(8,128)S(1)} %copy-done.16, ...), custom_call_target="tpu_custom_call" | custom-call | flops 2000000000 | bytes 4000000 | tf_op jit(solution)/shard_map/mamba_fwd/pallas_call | solution.py:389
  199.7 7.6 %middle.1 = (f32[512,1024]{1,0:T(8,128)}, bf16[512,1024]{1,0:T(8,128)(2,1)}, bf16[1024,512]{1,0:T(8,128)(2,1)}, f32[512,1]{1,0:T(8,128)}) custom-call(bf16[512,512]{1,0:T(8,128)(2,1)} %copy-done.57, bf16[512,1536]{1,0:T(8,128)(2,1)} %copy-done.35, bf16[1024,512]{1,0:T(8,128)(2,1)} %get-tuple-element.146.wa_ref, ...), custom_call_target="tpu_custom_call" | custom-call | flops 2000000000 | bytes 4000000 | tf_op jit(solution)/shard_map/middle/pallas_call | solution.py:886
  207.3 28.7 %ffn.1 = (bf16[1024,6144]{1,0:T(8,128)(2,1)}, bf16[512,1024]{1,0:T(8,128)(2,1)}, f32[512,1024]{1,0:T(8,128)}) custom-call(s32[12]{0:T(128)} %stack.115.index_ref, bf16[8,4,128,1536]{3,2,1,0:T(8,128)(2,1)} %bitcast.90, bf16[512,1024]{1,0:T(8,128)(2,1)} %get-tuple-element.148.n_ref, bf16[1024,512]{1,0:T(8,128)(2,1)} %get-tuple-element.149.nt_ref, ...), custom_call_target="tpu_custom_call" | custom-call | flops 2000000000 | bytes 4000000 | tf_op jit(solution)/shard_map/ffn/pallas_call | solution.py:978
  236.4 8.6 %after_ffn.1 = (f32[512,1024]{1,0:T(8,128)}, bf16[1024,512]{1,0:T(8,128)(2,1)}, bf16[512,1536]{1,0:T(8,128)(2,1)}, bf16[512,512]{1,0:T(8,128)(2,1)}, f32[8,1024]{1,0:T(8,128)}) custom-call(f32[512,1024]{1,0:T(8,128)} %get-tuple-element.153.dn_ref, f32[512,1024]{1,0:T(8,128)} %get-tuple-element.151.res_ref, f32[512,1]{1,0:T(8,128)} %get-tuple-element.154.scale_ref, ...), custom_call_target="tpu_custom_call" | custom-call | flops 2000000000 | bytes 4000000 | tf_op jit(solution)/shard_map/after_ffn/pallas_call | solution.py:886
  246.5 3.1 mamba_bpre.1
  252.4 9.4 %attn_bwd.1 = (bf16[512,512]{1,0:T(8,128)(2,1)S(1)}, bf16[512,256]{1,0:T(8,128)(2,1)S(1)}, bf16[512,256]{1,0:T(8,128)(2,1)S(1)}, f32[512,256]{1,0:T(8,128)S(1)}) custom-call(s32[4]{0:T(128)S(1)} %and_select_fusion.first_ref, bf16[512,512]{1,0:T(8,128)(2,1)S(1)} %copy-done.37, bf16[512,512]{1,0:T(8,128)(2,1)S(1)} %copy-done.38, ...), custom_call_target="tpu_custom_call" | custom-call | flops 2000000000 | bytes 4000000 | tf_op jit(solution)/shard_map/attn_bwd/pallas_call | solution.py:217
  263.5 8.9 %collective-permute-done.27.refs_0_ = bf16[144,1536]{1,0:T(8,128)(2,1)S(1)} collective-permute-done((bf16[144,1536]{1,0:T(8,128)(2,1)S(1)}, bf16[144,1536]{1,0:T(8,128)(2,1)S(1)}, u32[]{:S(2)}, u32[]{:S(2)}) %collective-permute-start.27) | collective-permute-done | bytes 442400 | tf_op jit(solution)/shard_map/ppermute | solution.py:599
  272.4 20.1 %collective-permute-done.28.refs_1_ = bf16[144,1536]{1,0:T(8,128)(2,1)S(1)} collective-permute-done((bf16[144,1536]{1,0:T(8,128)(2,1)S(1)}, bf16[144,1536]{1,0:T(8,128)(2,1)S(1)}, u32[]{:S(2)}, u32[]{:S(2)}) %collective-permute-start.28) | collective-permute-done | bytes 442400 | tf_op jit(solution)/shard_map/ppermute | solution.py:599
  292.6 11.4 %weight_grads.2 = (bf16[4,4,128,1024]{3,2,1,0:T(8,128)(2,1)}, bf16[4,4,128,1024]{3,2,1,0:T(8,128)(2,1)}) custom-call(s32[12]{0:T(128)} %stack.115.index_ref, bf16[1024,512]{1,0:T(8,128)(2,1)} %get-tuple-element.163.refs_0_, bf16[1024,512]{1,0:T(8,128)(2,1)} %get-tuple-element.164.refs_1_.refs_0_, bf16[512,512]{1,0:T(8,128)(2,1)} %copy-done.57, ...), custom_call_target="tpu_custom_call" | custom-call | flops 2000000000 | bytes 4000000 | tf_op jit(solution)/shard_map/weight_grads/pallas_call | solution.py:930
  304.1 24.2 %mamba_bwd.1 = (f32[512,1792]{1,0:T(8,128)}, bf16[512,128]{1,0:T(8,128)(2,1)}, f32[8,1792]{1,0:T(8,128)}, f32[8,128]{1,0:T(8,128)}) custom-call(bf16[512,1792]{1,0:T(8,128)(2,1)} %copy-done, f32[512,128]{1,0:T(8,128)} %copy-done.14, f32[512,128]{1,0:T(8,128)} %copy-done.15, f32[32,512]{1,0:T(8,128)} %copy-done.27, f32[512,128]{1,0:T(8,128)} %copy-done.5, ...), custom_call_target="tpu_custom_call" | custom-call | flops 2000000000 | bytes 4000000 | tf_op jit(solution)/shard_map/mamba_bwd/pallas_call | solution.py:554
  328.4 4.5 add_convert_fusion
  341.6 6.3 %collective-permute-done.31.refs_0_ = bf16[512,256]{1,0:T(8,128)(2,1)S(1)} collective-permute-done((bf16[512,256]{1,0:T(8,128)(2,1)S(1)}, bf16[512,256]{1,0:T(8,128)(2,1)S(1)}, u32[]{:S(2)}, u32[]{:S(2)}) %collective-permute-start.31) | collective-permute-done | bytes 262176 | tf_op jit(solution)/shard_map/ppermute | solution.py:599
  347.9 8.2 %collective-permute-done.32.refs_1_ = bf16[512,256]{1,0:T(8,128)(2,1)S(1)} collective-permute-done((bf16[512,256]{1,0:T(8,128)(2,1)S(1)}, bf16[512,256]{1,0:T(8,128)(2,1)S(1)}, u32[]{:S(2)}, u32[]{:S(2)}) %collective-permute-start.32) | collective-permute-done | bytes 262176 | tf_op jit(solution)/shard_map/ppermute | solution.py:599
  356.7 2.3 kv_back.1.dkv_ref
  359.6 6.2 %conv_back.1 = (bf16[512,1536]{1,0:T(8,128)(2,1)}, bf16[512,512]{1,0:T(8,128)(2,1)}) custom-call(f32[512,1792]{1,0:T(8,128)} %get-tuple-element.171.dpre_ref, f32[8,1792]{1,0:T(8,128)} %copy-done.95, f32[8,1792]{1,0:T(8,128)} %maximum_maximum_fusion.3.tap_ref, f32[512,8]{1,0:T(8,128)} %copy.124.keep_ref, bf16[512,256]{1,0:T(8,128)(2,1)} %kv_back.1.dkv_ref), custom_call_target="tpu_custom_call" | custom-call | flops 2000000000 | bytes 4000000 | tf_op jit(solution)/shard_map/conv_back/pallas_call | solution.py:886
  365.8 2.6 add_convert_fusion.8
  368.4 2.6 add_convert_fusion.10
  371.0 8.0 %weight_grads.3 = (bf16[4,4,128,640]{3,2,1,0:T(8,128)(2,1)}, bf16[4,4,128,640]{3,2,1,0:T(8,128)(2,1)}) custom-call(s32[12]{0:T(128)} %stack.115.index_ref, bf16[1024,512]{1,0:T(8,128)(2,1)} %get-tuple-element.164.refs_1_.refs_0_, bf16[512,1536]{1,0:T(8,128)(2,1)} %get-tuple-element.191.refs_1_, bf16[512,128]{1,0:T(8,128)(2,1)} %get-tuple-element.181.refs_2_, ...), custom_call_target="tpu_custom_call" | custom-call | flops 2000000000 | bytes 4000000 | tf_op jit(solution)/shard_map/weight_grads/pallas_call | solution.py:930
  380.8 2.1 fusion.40
  384.1 2.0 add_convert_fusion.4
  397.8 3.5 fusion.2
  401.2 8.3 %collective-permute-done.37 = f32[88,128]{1,0:T(8,128)S(1)} collective-permute-done((f32[88,128]{1,0:T(8,128)S(1)}, f32[88,128]{1,0:T(8,128)S(1)}, u32[]{:S(2)}, u32[]{:S(2)}) %collective-permute-start.37) | collective-permute-done | bytes 45088 | tf_op jit(solution)/shard_map/ppermute | solution.py:659
  410.0 2.0 fusion.7
  413.8 3.9 collective-permute-start.41
  417.7 2.0 fusion.9
  421.9 1.9 collective-permute-start.48
  432.5 11.3 %collective-permute-done.47 = bf16[128,1024]{1,0:T(8,128)(2,1)} collective-permute-done((bf16[128,1024]{1,0:T(8,128)(2,1)}, bf16[128,1024]{1,0:T(8,128)(2,1)}, u32[]{:S(2)}, u32[]{:S(2)}) %collective-permute-start.47) | collective-permute-done | bytes 262176 | tf_op jit(solution)/shard_map/ppermute | solution.py:595
  448.7 2.1 collective-permute-start.53
  452.3 11.1 %collective-permute-done.52 = bf16[128,640]{1,0:T(8,128)(2,1)S(1)} collective-permute-done((bf16[128,640]{1,0:T(8,128)(2,1)S(1)}, bf16[128,640]{1,0:T(8,128)(2,1)S(1)}, u32[]{:S(2)}, u32[]{:S(2)}) %collective-permute-start.52) | collective-permute-done | bytes 163872 | tf_op jit(solution)/shard_map/ppermute | solution.py:595
  (397 shorter events, 107.5 us)
Async XLA Ops:
  7.2 200.1 %all-gather.2.cloned.1.call-start = ((), (), s32[]{:S(2)}) async-start(), calls=%async_computation.2 | async-start | bytes 12976128 | tf_op jit(solution)/shard_map/all_gather | solution.py:1086
  11.3 19.1 %collective-permute-start.1 = (bf16[128,768]{1,0:T(8,128)(2,1)}, bf16[128,768]{1,0:T(8,128)(2,1)S(1)}, u32[]{:S(2)}, u32[]{:S(2)}) collective-permute-start(bf16[128,768]{1,0:T(8,128)(2,1)} %pack.4.refs_0_), channel_id=1, source_target_pairs={{0,2},{1,3},{2,0},{3,1},{4,6},{5,7},{6,4},{7,5},{8,10},{9,11},{10,... | collective-permute-start | bytes 589832 | tf_op jit(solution)/shard_map/ppermute | solution.py:595
  15.6 14.8 %collective-permute-start.2 = (bf16[128,768]{1,0:T(8,128)(2,1)}, bf16[128,768]{1,0:T(8,128)(2,1)S(1)}, u32[]{:S(2)}, u32[]{:S(2)}) collective-permute-start(bf16[128,768]{1,0:T(8,128)(2,1)} %pack.4.refs_0_), channel_id=1, source_target_pairs={{0,3},{1,0},{2,1},{3,2},{4,7},{5,4},{6,5},{7,6},{8,11},{9,8},{10,9... | collective-permute-start | bytes 589832 | tf_op jit(solution)/shard_map/ppermute | solution.py:595
  16.9 13.4 %collective-permute-start = (bf16[128,768]{1,0:T(8,128)(2,1)}, bf16[128,768]{1,0:T(8,128)(2,1)S(1)}, u32[]{:S(2)}, u32[]{:S(2)}) collective-permute-start(bf16[128,768]{1,0:T(8,128)(2,1)} %pack.4.refs_0_), channel_id=1, source_target_pairs={{0,1},{1,2},{2,3},{3,0},{4,5},{5,6},{6,7},{7,4},{8,9},{9,10},{10,1... | collective-permute-start | bytes 589832 | tf_op jit(solution)/shard_map/ppermute | solution.py:595
  30.5 328.5 %reduce-scatter.3.cloned.1.call-start = ((), (), s32[]{:S(2)}) async-start(), calls=%async_computation.3 | async-start | bytes 14155776 | tf_op jit(solution)/shard_map/reduce_scatter | solution.py:1152
  31.3 28.5 %collective-permute-start.5 = (bf16[16,1024]{1,0:T(8,128)(2,1)S(1)}, bf16[16,1024]{1,0:T(8,128)(2,1)S(1)}, u32[]{:S(2)}, u32[]{:S(2)}) collective-permute-start(bf16[16,1024]{1,0:T(8,128)(2,1)S(1)} %slice.358), channel_id=1, source_target_pairs={{0,1},{1,2},{2,3},{4,5},{5,6},{6,7},{8,9},{9,10},{10,11},{12,13},{... | collective-permute-start | bytes 98312 | tf_op jit(solution)/shard_map/ppermute | solution.py:599
  37.1 13.6 %collective-permute-start.8 = (bf16[2,128,768]{2,1,0:T(8,128)(2,1)S(1)}, bf16[2,128,768]{2,1,0:T(8,128)(2,1)S(1)}, u32[]{:S(2)}, u32[]{:S(2)}) collective-permute-start(bf16[2,128,768]{2,1,0:T(8,128)(2,1)S(1)} %join.9), channel_id=1, source_target_pairs={{0,16},{4,20},{8,24},{12,28},{16,0},{20,4},{24,8},{28,12},{1,17},{... | collective-permute-start | bytes 1179656 | tf_op jit(solution)/shard_map/ppermute | solution.py:591
  39.7 14.9 %collective-permute-start.3 = (bf16[2,128,768]{2,1,0:T(8,128)(2,1)S(1)}, bf16[2,128,768]{2,1,0:T(8,128)(2,1)S(1)}, u32[]{:S(2)}, u32[]{:S(2)}) collective-permute-start(bf16[2,128,768]{2,1,0:T(8,128)(2,1)S(1)} %join.8), channel_id=1, source_target_pairs={{0,8},{4,12},{8,0},{12,4},{16,24},{20,28},{24,16},{28,20},{1,9},{5... | collective-permute-start | bytes 1179656 | tf_op jit(solution)/shard_map/ppermute | solution.py:591
  50.8 19.2 %collective-permute-start.9 = (bf16[2,2,128,768]{3,2,1,0:T(8,128)(2,1)S(1)}, bf16[2,2,128,768]{3,2,1,0:T(8,128)(2,1)}, u32[]{:S(2)}, u32[]{:S(2)}) collective-permute-start(bf16[2,2,128,768]{3,2,1,0:T(8,128)(2,1)S(1)} %join.11.refs_4_), channel_id=1, source_target_pairs={{0,8},{4,12},{8,0},{12,4},{16,24},{20,28},{24,16},{28,20},{1,9},{5... | collective-permute-start | bytes 2359304 | tf_op jit(solution)/shard_map/ppermute | solution.py:591
  54.7 16.7 %collective-permute-start.4 = (bf16[2,2,128,768]{3,2,1,0:T(8,128)(2,1)S(1)}, bf16[2,2,128,768]{3,2,1,0:T(8,128)(2,1)}, u32[]{:S(2)}, u32[]{:S(2)}) collective-permute-start(bf16[2,2,128,768]{3,2,1,0:T(8,128)(2,1)S(1)} %join.10.refs_0_), channel_id=1, source_target_pairs={{0,16},{4,20},{8,24},{12,28},{16,0},{20,4},{24,8},{28,12},{1,17},{... | collective-permute-start | bytes 2359304 | tf_op jit(solution)/shard_map/ppermute | solution.py:591
  55.5 17.7 %collective-permute-start.13 = (bf16[128,896]{1,0:T(8,128)(2,1)S(1)}, bf16[128,896]{1,0:T(8,128)(2,1)S(1)}, u32[]{:S(2)}, u32[]{:S(2)}) collective-permute-start(bf16[128,896]{1,0:T(8,128)(2,1)S(1)} %copy-done.48), channel_id=1, source_target_pairs={{0,2},{1,3},{2,0},{3,1},{4,6},{5,7},{6,4},{7,5},{8,10},{9,11},{10,... | collective-permute-start | bytes 688136 | tf_op jit(solution)/shard_map/ppermute | solution.py:595
  59.5 14.5 %collective-permute-start.12 = (bf16[128,896]{1,0:T(8,128)(2,1)S(1)}, bf16[128,896]{1,0:T(8,128)(2,1)S(1)}, u32[]{:S(2)}, u32[]{:S(2)}) collective-permute-start(bf16[128,896]{1,0:T(8,128)(2,1)S(1)} %copy-done.48), channel_id=1, source_target_pairs={{0,1},{1,2},{2,3},{3,0},{4,5},{5,6},{6,7},{7,4},{8,9},{9,10},{10,1... | collective-permute-start | bytes 688136 | tf_op jit(solution)/shard_map/ppermute | solution.py:595
  70.0 22.3 %collective-permute-start.10 = (bf16[2,2,128,768]{3,2,1,0:T(8,128)(2,1)S(1)}, bf16[2,2,128,768]{3,2,1,0:T(8,128)(2,1)}, u32[]{:S(2)}, u32[]{:S(2)}) collective-permute-start(bf16[2,2,128,768]{3,2,1,0:T(8,128)(2,1)S(1)} %join.11.refs_4_), channel_id=1, source_target_pairs={{0,4},{4,0},{8,12},{12,8},{16,20},{20,16},{24,28},{28,24},{1,5},{5... | collective-permute-start | bytes 2359304 | tf_op jit(solution)/shard_map/ppermute | solution.py:591
  70.0 22.3 %collective-permute-start.11 = (bf16[2,2,128,768]{3,2,1,0:T(8,128)(2,1)}, bf16[2,2,128,768]{3,2,1,0:T(8,128)(2,1)}, u32[]{:S(2)}, u32[]{:S(2)}) collective-permute-start(bf16[2,2,128,768]{3,2,1,0:T(8,128)(2,1)} %collective-permute-done.9.refs_5_), channel_id=1, source_target_pairs={{0,4},{4,0},{8,12},{12,8},{16,20},{20,16},{24,28},{28,24},{1,5},{5... | collective-permute-start | bytes 2359304 | tf_op jit(solution)/shard_map/ppermute | solution.py:591
  71.4 20.9 %collective-permute-start.6 = (bf16[2,2,128,768]{3,2,1,0:T(8,128)(2,1)S(1)}, bf16[2,2,128,768]{3,2,1,0:T(8,128)(2,1)}, u32[]{:S(2)}, u32[]{:S(2)}) collective-permute-start(bf16[2,2,128,768]{3,2,1,0:T(8,128)(2,1)S(1)} %join.10.refs_0_), channel_id=1, source_target_pairs={{0,4},{4,0},{8,12},{12,8},{16,20},{20,16},{24,28},{28,24},{1,5},{5... | collective-permute-start | bytes 2359304 | tf_op jit(solution)/shard_map/ppermute | solution.py:591
  73.3 19.0 %collective-permute-start.7 = (bf16[2,2,128,768]{3,2,1,0:T(8,128)(2,1)}, bf16[2,2,128,768]{3,2,1,0:T(8,128)(2,1)}, u32[]{:S(2)}, u32[]{:S(2)}) collective-permute-start(bf16[2,2,128,768]{3,2,1,0:T(8,128)(2,1)} %collective-permute-done.4.refs_1_), channel_id=1, source_target_pairs={{0,4},{4,0},{8,12},{12,8},{16,20},{20,16},{24,28},{28,24},{1,5},{5... | collective-permute-start | bytes 2359304 | tf_op jit(solution)/shard_map/ppermute | solution.py:591
  74.0 17.5 %collective-permute-start.14 = (bf16[128,896]{1,0:T(8,128)(2,1)S(1)}, bf16[128,896]{1,0:T(8,128)(2,1)S(1)}, u32[]{:S(2)}, u32[]{:S(2)}) collective-permute-start(bf16[128,896]{1,0:T(8,128)(2,1)S(1)} %copy-done.48), channel_id=1, source_target_pairs={{0,3},{1,0},{2,1},{3,2},{4,7},{5,4},{6,5},{7,6},{8,11},{9,8},{10,9... | collective-permute-start | bytes 688136 | tf_op jit(solution)/shard_map/ppermute | solution.py:595
  101.9 22.7 %collective-permute-start.16 = (bf16[2,128,896]{2,1,0:T(8,128)(2,1)S(1)}, bf16[2,128,896]{2,1,0:T(8,128)(2,1)S(1)}, u32[]{:S(2)}, u32[]{:S(2)}) collective-permute-start(bf16[2,128,896]{2,1,0:T(8,128)(2,1)S(1)} %join.13), channel_id=1, source_target_pairs={{0,16},{4,20},{8,24},{12,28},{16,0},{20,4},{24,8},{28,12},{1,17},{... | collective-permute-start | bytes 1376264 | tf_op jit(solution)/shard_map/ppermute | solution.py:591
  102.0 23.6 %collective-permute-start.15 = (bf16[2,128,896]{2,1,0:T(8,128)(2,1)S(1)}, bf16[2,128,896]{2,1,0:T(8,128)(2,1)S(1)}, u32[]{:S(2)}, u32[]{:S(2)}) collective-permute-start(bf16[2,128,896]{2,1,0:T(8,128)(2,1)S(1)} %join.12), channel_id=1, source_target_pairs={{0,8},{4,12},{8,0},{12,4},{16,24},{20,28},{24,16},{28,20},{1,9},{5... | collective-permute-start | bytes 1376264 | tf_op jit(solution)/shard_map/ppermute | solution.py:591
  103.6 23.0 %collective-permute-start.17 = (bf16[512,256]{1,0:T(8,128)(2,1)}, bf16[512,256]{1,0:T(8,128)(2,1)S(1)}, u32[]{:S(2)}, u32[]{:S(2)}) collective-permute-start(bf16[512,256]{1,0:T(8,128)(2,1)} %get-tuple-element.122.refs_2_), channel_id=1, source_target_pairs={{0,2},{1,3},{4,6},{5,7},{8,10},{9,11},{12,14},{13,15},{16,18},{17,... | collective-permute-start | bytes 786440 | tf_op jit(solution)/shard_map/ppermute | solution.py:599
  105.0 23.4 %collective-permute-start.18 = (bf16[512,256]{1,0:T(8,128)(2,1)}, bf16[512,256]{1,0:T(8,128)(2,1)S(1)}, u32[]{:S(2)}, u32[]{:S(2)}) collective-permute-start(bf16[512,256]{1,0:T(8,128)(2,1)} %get-tuple-element.122.refs_2_), channel_id=1, source_target_pairs={{0,1},{1,2},{2,3},{4,5},{5,6},{6,7},{8,9},{9,10},{10,11},{12,13},{... | collective-permute-start | bytes 786440 | tf_op jit(solution)/shard_map/ppermute | solution.py:599
  129.0 43.0 %collective-permute-start.24 = (bf16[2,2,128,896]{3,2,1,0:T(8,128)(2,1)}, bf16[2,2,128,896]{3,2,1,0:T(8,128)(2,1)}, u32[]{:S(2)}, u32[]{:S(2)}) collective-permute-start(bf16[2,2,128,896]{3,2,1,0:T(8,128)(2,1)} %join.15.refs_4_), channel_id=1, source_target_pairs={{0,8},{4,12},{8,0},{12,4},{16,24},{20,28},{24,16},{28,20},{1,9},{5... | collective-permute-start | bytes 2752520 | tf_op jit(solution)/shard_map/ppermute | solution.py:591
  129.7 42.9 %collective-permute-start.19 = (bf16[2,2,128,896]{3,2,1,0:T(8,128)(2,1)}, bf16[2,2,128,896]{3,2,1,0:T(8,128)(2,1)}, u32[]{:S(2)}, u32[]{:S(2)}) collective-permute-start(bf16[2,2,128,896]{3,2,1,0:T(8,128)(2,1)} %join.14.refs_0_), channel_id=1, source_target_pairs={{0,16},{4,20},{8,24},{12,28},{16,0},{20,4},{24,8},{28,12},{1,17},{... | collective-permute-start | bytes 2752520 | tf_op jit(solution)/shard_map/ppermute | solution.py:591
  131.7 35.4 %collective-permute-start.20 = (bf16[144,1536]{1,0:T(8,128)(2,1)}, bf16[144,1536]{1,0:T(8,128)(2,1)}, u32[]{:S(2)}, u32[]{:S(2)}) collective-permute-start(bf16[144,1536]{1,0:T(8,128)(2,1)} %get-tuple-element.139), channel_id=1, source_target_pairs={{0,1},{1,2},{2,3},{4,5},{5,6},{6,7},{8,9},{9,10},{10,11},{12,13},{... | collective-permute-start | bytes 1327112 | tf_op jit(solution)/shard_map/ppermute | solution.py:599
  151.9 20.2 %collective-permute-start.21 = (bf16[144,1536]{1,0:T(8,128)(2,1)}, bf16[144,1536]{1,0:T(8,128)(2,1)}, u32[]{:S(2)}, u32[]{:S(2)}) collective-permute-start(bf16[144,1536]{1,0:T(8,128)(2,1)} %get-tuple-element.139), channel_id=1, source_target_pairs={{0,2},{1,3},{4,6},{5,7},{8,10},{9,11},{12,14},{13,15},{16,18},{17,... | collective-permute-start | bytes 1327112 | tf_op jit(solution)/shard_map/ppermute | solution.py:599
  236.1 190.2 %reduce-scatter.5.cloned.1.call-start = ((), (), s32[]{:S(2)}) async-start(), calls=%async_computation.4 | async-start | bytes 1966080 | tf_op jit(solution)/shard_map/reduce_scatter | solution.py:1154
  249.7 22.7 %collective-permute-start.27 = (bf16[144,1536]{1,0:T(8,128)(2,1)S(1)}, bf16[144,1536]{1,0:T(8,128)(2,1)S(1)}, u32[]{:S(2)}, u32[]{:S(2)}) collective-permute-start(bf16[144,1536]{1,0:T(8,128)(2,1)S(1)} %get-tuple-element.166), channel_id=1, source_target_pairs={{1,0},{2,1},{3,2},{5,4},{6,5},{7,6},{9,8},{10,9},{11,10},{13,12},{... | collective-permute-start | bytes 1327112 | tf_op jit(solution)/shard_map/ppermute | solution.py:599
  251.0 41.6 %collective-permute-start.28 = (bf16[144,1536]{1,0:T(8,128)(2,1)S(1)}, bf16[144,1536]{1,0:T(8,128)(2,1)S(1)}, u32[]{:S(2)}, u32[]{:S(2)}) collective-permute-start(bf16[144,1536]{1,0:T(8,128)(2,1)S(1)} %get-tuple-element.166), channel_id=1, source_target_pairs={{2,0},{3,1},{6,4},{7,5},{10,8},{11,9},{14,12},{15,13},{18,16},{19,... | collective-permute-start | bytes 1327112 | tf_op jit(solution)/shard_map/ppermute | solution.py:599
  304.0 24.3 %collective-permute-start.30 = (bf16[4,4,128,1024]{3,2,1,0:T(8,128)(2,1)}, bf16[4,4,128,1024]{3,2,1,0:T(8,128)(2,1)}, u32[]{:S(2)}, u32[]{:S(2)}) collective-permute-start(bf16[4,4,128,1024]{3,2,1,0:T(8,128)(2,1)} %get-tuple-element.168), channel_id=1, source_target_pairs={{0,4},{4,0},{8,12},{12,8},{16,20},{20,16},{24,28},{28,24},{1,5},{5... | collective-permute-start | bytes 12582920 | tf_op jit(solution)/shard_map/ppermute | solution.py:591
  332.9 33.0 %collective-permute-start.34 = (bf16[2,2,128,1024]{3,2,1,0:T(8,128)(2,1)}, bf16[2,2,128,1024]{3,2,1,0:T(8,128)(2,1)}, u32[]{:S(2)}, u32[]{:S(2)}) collective-permute-start(bf16[2,2,128,1024]{3,2,1,0:T(8,128)(2,1)} %get-tuple-element.337), channel_id=1, source_target_pairs={{0,8},{4,12},{8,0},{12,4},{16,24},{20,28},{24,16},{28,20},{1,9},{5... | collective-permute-start | bytes 3145736 | tf_op jit(solution)/shard_map/ppermute | solution.py:591
  334.4 34.0 %collective-permute-start.33 = (bf16[2,2,128,1024]{3,2,1,0:T(8,128)(2,1)}, bf16[2,2,128,1024]{3,2,1,0:T(8,128)(2,1)}, u32[]{:S(2)}, u32[]{:S(2)}) collective-permute-start(bf16[2,2,128,1024]{3,2,1,0:T(8,128)(2,1)} %get-tuple-element.339), channel_id=1, source_target_pairs={{0,16},{4,20},{8,24},{12,28},{16,0},{20,4},{24,8},{28,12},{1,17},{... | collective-permute-start | bytes 3145736 | tf_op jit(solution)/shard_map/ppermute | solution.py:591
  335.8 12.1 %collective-permute-start.31 = (bf16[512,256]{1,0:T(8,128)(2,1)S(1)}, bf16[512,256]{1,0:T(8,128)(2,1)S(1)}, u32[]{:S(2)}, u32[]{:S(2)}) collective-permute-start(bf16[512,256]{1,0:T(8,128)(2,1)S(1)} %get-tuple-element.178), channel_id=1, source_target_pairs={{1,0},{2,1},{3,2},{5,4},{6,5},{7,6},{9,8},{10,9},{11,10},{13,12},{... | collective-permute-start | bytes 786440 | tf_op jit(solution)/shard_map/ppermute | solution.py:599
  337.1 18.9 %collective-permute-start.32 = (bf16[512,256]{1,0:T(8,128)(2,1)S(1)}, bf16[512,256]{1,0:T(8,128)(2,1)S(1)}, u32[]{:S(2)}, u32[]{:S(2)}) collective-permute-start(bf16[512,256]{1,0:T(8,128)(2,1)S(1)} %get-tuple-element.179), channel_id=1, source_target_pairs={{2,0},{3,1},{6,4},{7,5},{10,8},{11,9},{14,12},{15,13},{18,16},{19,... | collective-permute-start | bytes 786440 | tf_op jit(solution)/shard_map/ppermute | solution.py:599
  340.1 18.9 %collective-permute-start.29 = (f32[8,1792]{1,0:T(8,128)S(1)}, f32[8,1792]{1,0:T(8,128)S(1)}, u32[]{:S(2)}, u32[]{:S(2)}) collective-permute-start(f32[8,1792]{1,0:T(8,128)S(1)} %slice.365), channel_id=1, source_target_pairs={{1,0},{2,1},{3,2},{5,4},{6,5},{7,6},{9,8},{10,9},{11,10},{13,12},{... | collective-permute-start | bytes 172040 | tf_op jit(solution)/shard_map/ppermute | solution.py:599
  380.0 30.0 %collective-permute-start.42 = (bf16[2,1,128,1024]{3,2,1,0:T(8,128)(2,1)}, bf16[2,1,128,1024]{3,2,1,0:T(8,128)(2,1)}, u32[]{:S(2)}, u32[]{:S(2)}) collective-permute-start(bf16[2,1,128,1024]{3,2,1,0:T(8,128)(2,1)} %get-tuple-element.347), channel_id=1, source_target_pairs={{0,8},{4,12},{8,0},{12,4},{16,24},{20,28},{24,16},{28,20},{1,9},{5... | collective-permute-start | bytes 1572872 | tf_op jit(solution)/shard_map/ppermute | solution.py:591
  380.6 33.2 %collective-permute-start.43 = (bf16[2,1,128,1024]{3,2,1,0:T(8,128)(2,1)}, bf16[2,1,128,1024]{3,2,1,0:T(8,128)(2,1)}, u32[]{:S(2)}, u32[]{:S(2)}) collective-permute-start(bf16[2,1,128,1024]{3,2,1,0:T(8,128)(2,1)} %get-tuple-element.345), channel_id=1, source_target_pairs={{0,16},{4,20},{8,24},{12,28},{16,0},{20,4},{24,8},{28,12},{1,17},{... | collective-permute-start | bytes 1572872 | tf_op jit(solution)/shard_map/ppermute | solution.py:591
  386.1 43.1 %collective-permute-start.44 = (bf16[2,2,128,640]{3,2,1,0:T(8,128)(2,1)}, bf16[2,2,128,640]{3,2,1,0:T(8,128)(2,1)}, u32[]{:S(2)}, u32[]{:S(2)}) collective-permute-start(bf16[2,2,128,640]{3,2,1,0:T(8,128)(2,1)} %get-tuple-element.343), channel_id=1, source_target_pairs={{0,16},{4,20},{8,24},{12,28},{16,0},{20,4},{24,8},{28,12},{1,17},{... | collective-permute-start | bytes 1966088 | tf_op jit(solution)/shard_map/ppermute | solution.py:591
  386.8 44.2 %collective-permute-start.45 = (bf16[2,2,128,640]{3,2,1,0:T(8,128)(2,1)}, bf16[2,2,128,640]{3,2,1,0:T(8,128)(2,1)}, u32[]{:S(2)}, u32[]{:S(2)}) collective-permute-start(bf16[2,2,128,640]{3,2,1,0:T(8,128)(2,1)} %get-tuple-element.341), channel_id=1, source_target_pairs={{0,8},{4,12},{8,0},{12,4},{16,24},{20,28},{24,16},{28,20},{1,9},{5... | collective-permute-start | bytes 1966088 | tf_op jit(solution)/shard_map/ppermute | solution.py:591
  397.1 12.4 %collective-permute-start.37 = (f32[88,128]{1,0:T(8,128)S(1)}, f32[88,128]{1,0:T(8,128)S(1)}, u32[]{:S(2)}, u32[]{:S(2)}) collective-permute-start(f32[88,128]{1,0:T(8,128)S(1)} %fusion.53), channel_id=1, source_target_pairs={{0,8},{4,12},{8,0},{12,4},{16,24},{20,28},{24,16},{28,20},{1,9},{5... | collective-permute-start | bytes 135176 | tf_op jit(solution)/shard_map/ppermute | solution.py:659
  413.7 6.7 %collective-permute-start.40 = (f32[88,128]{1,0:T(8,128)S(1)}, f32[88,128]{1,0:T(8,128)S(1)}, u32[]{:S(2)}, u32[]{:S(2)}) collective-permute-start(f32[88,128]{1,0:T(8,128)S(1)} %add.256), channel_id=1, source_target_pairs={{0,2},{1,3},{2,0},{3,1},{4,6},{5,7},{6,4},{7,5},{8,10},{9,11},{10,... | collective-permute-start | bytes 135176 | tf_op jit(solution)/shard_map/ppermute | solution.py:595
  413.8 8.1 %collective-permute-start.41 = (f32[88,128]{1,0:T(8,128)S(1)}, f32[88,128]{1,0:T(8,128)S(1)}, u32[]{:S(2)}, u32[]{:S(2)}) collective-permute-start(f32[88,128]{1,0:T(8,128)S(1)} %add.256), channel_id=1, source_target_pairs={{0,3},{1,0},{2,1},{3,2},{4,7},{5,4},{6,5},{7,6},{8,11},{9,8},{10,9... | collective-permute-start | bytes 135176 | tf_op jit(solution)/shard_map/ppermute | solution.py:595
  419.8 12.7 %collective-permute-start.46 = (bf16[128,1024]{1,0:T(8,128)(2,1)}, bf16[128,1024]{1,0:T(8,128)(2,1)}, u32[]{:S(2)}, u32[]{:S(2)}) collective-permute-start(bf16[128,1024]{1,0:T(8,128)(2,1)} %get-tuple-element.353), channel_id=1, source_target_pairs={{0,3},{1,0},{2,1},{3,2},{4,7},{5,4},{6,5},{7,6},{8,11},{9,8},{10,9... | collective-permute-start | bytes 786440 | tf_op jit(solution)/shard_map/ppermute | solution.py:595
  420.4 23.3 %collective-permute-start.47 = (bf16[128,1024]{1,0:T(8,128)(2,1)}, bf16[128,1024]{1,0:T(8,128)(2,1)}, u32[]{:S(2)}, u32[]{:S(2)}) collective-permute-start(bf16[128,1024]{1,0:T(8,128)(2,1)} %get-tuple-element.354), channel_id=1, source_target_pairs={{0,2},{1,3},{2,0},{3,1},{4,6},{5,7},{6,4},{7,5},{8,10},{9,11},{10,... | collective-permute-start | bytes 786440 | tf_op jit(solution)/shard_map/ppermute | solution.py:595
  421.9 21.8 %collective-permute-start.48 = (bf16[128,1024]{1,0:T(8,128)(2,1)}, bf16[128,1024]{1,0:T(8,128)(2,1)}, u32[]{:S(2)}, u32[]{:S(2)}) collective-permute-start(bf16[128,1024]{1,0:T(8,128)(2,1)} %get-tuple-element.355), channel_id=1, source_target_pairs={{0,1},{1,2},{2,3},{3,0},{4,5},{5,6},{6,7},{7,4},{8,9},{9,10},{10,1... | collective-permute-start | bytes 786440 | tf_op jit(solution)/shard_map/ppermute | solution.py:595
  430.4 16.1 %collective-permute-start.49 = (bf16[2,1,128,640]{3,2,1,0:T(8,128)(2,1)S(1)}, bf16[2,1,128,640]{3,2,1,0:T(8,128)(2,1)S(1)}, u32[]{:S(2)}, u32[]{:S(2)}) collective-permute-start(bf16[2,1,128,640]{3,2,1,0:T(8,128)(2,1)S(1)} %get-tuple-element.351), channel_id=1, source_target_pairs={{0,8},{4,12},{8,0},{12,4},{16,24},{20,28},{24,16},{28,20},{1,9},{5... | collective-permute-start | bytes 983048 | tf_op jit(solution)/shard_map/ppermute | solution.py:591
  432.3 14.4 %collective-permute-start.50 = (bf16[2,1,128,640]{3,2,1,0:T(8,128)(2,1)S(1)}, bf16[2,1,128,640]{3,2,1,0:T(8,128)(2,1)S(1)}, u32[]{:S(2)}, u32[]{:S(2)}) collective-permute-start(bf16[2,1,128,640]{3,2,1,0:T(8,128)(2,1)S(1)} %get-tuple-element.349), channel_id=1, source_target_pairs={{0,16},{4,20},{8,24},{12,28},{16,0},{20,4},{24,8},{28,12},{1,17},{... | collective-permute-start | bytes 983048 | tf_op jit(solution)/shard_map/ppermute | solution.py:591
  447.0 16.4 %collective-permute-start.52 = (bf16[128,640]{1,0:T(8,128)(2,1)S(1)}, bf16[128,640]{1,0:T(8,128)(2,1)S(1)}, u32[]{:S(2)}, u32[]{:S(2)}) collective-permute-start(bf16[128,640]{1,0:T(8,128)(2,1)S(1)} %maximum_maximum_fusion.1), channel_id=1, source_target_pairs={{0,2},{1,3},{2,0},{3,1},{4,6},{5,7},{6,4},{7,5},{8,10},{9,11},{10,... | collective-permute-start | bytes 491528 | tf_op jit(solution)/shard_map/ppermute | solution.py:595
  448.7 14.8 %collective-permute-start.53 = (bf16[128,640]{1,0:T(8,128)(2,1)S(1)}, bf16[128,640]{1,0:T(8,128)(2,1)S(1)}, u32[]{:S(2)}, u32[]{:S(2)}) collective-permute-start(bf16[128,640]{1,0:T(8,128)(2,1)S(1)} %maximum_maximum_fusion.2), channel_id=1, source_target_pairs={{0,1},{1,2},{2,3},{3,0},{4,5},{5,6},{6,7},{7,4},{8,9},{9,10},{10,1... | collective-permute-start | bytes 491528 | tf_op jit(solution)/shard_map/ppermute | solution.py:595
  (108 other events, 1529.3 us)
Sparse Core Ops, SparseCore 0:
  30.6 127.3 all-gather.1
  236.2 104.7 reduce-scatter.2
  380.9 33.8 reduce-scatter.4
